TPU v7x, 512 devices: a whole 4x8x8 slice. The times are simulated.
512 devices in a mesh: tx: 32 (over z_lo, y, core), ty: 16 (over z_hi, x).
Axes of the slice: x: 4, y: 8, z: 8 (z_hi: 4, z_lo: 2; z = z_hi * 2 + z_lo), core: 2. Of those that a mesh axis runs over, the one named last changes fastest.
Arguments:
- species: float32 [32, 1024, 4096], P(None, 'tx', 'ty'), may hold values from -6 to 6
- cell_factor: float32 [1024, 4096], P('tx', 'ty'), may hold values from 0.5 to 2
- species_rate: float32 [32], replicated, may hold values from 0.01 to 0.08
- factor_x: float32 [1024, 128], P('tx'), may hold values from -0.375 to 0.375
- factor_y: float32 [128, 128], P('ty'), may hold values from -0.75 to 0.75
- factor_species: float32 [32, 16], replicated, may hold values from -1 to 1
Outputs:
- advanced: float32 [32, 1024, 4096], P(None, 'tx', 'ty')
- core_tensor: float32 [128, 16, 4096], P('tx', None, 'ty')
All inputs are finite; a program needn't handle non-finite values.
Results may differ from a plain program's by a relative error of at most 0.000075.
Values sent between devices are 32-bit elements; how exact they have to be, the bound alone decides.
No kernel may reach another device: no remote copies, remote signals or barrier semaphores. Data moves between devices by JAX's collectives and lax.ppermute only.
A program may use at most 64 MiB of HBM per device.

v0:
```python
import jax
import jax.numpy as jnp
from jax import lax
from jax.sharding import PartitionSpec as P

exact_mode = lax.Precision.HIGHEST


def padded_2(x, sides, width):
    for axis, dim in sides:
        count, length = (lax.axis_size(axis), x.shape[dim])
        up = [(i, (i + 1) % count) for i in range(count - 1)]
        down = [(j, i) for i, j in up]
        last = lax.slice_in_dim(x, length - width, length, axis=dim)
        first = lax.slice_in_dim(x, 0, width, axis=dim)
        before = lax.ppermute(last, axis, up)
        after = lax.ppermute(first, axis, down)
        x = jnp.concatenate([before, x, after], axis=dim)
    return x


def laplace(padded):
    center = padded[:, 1:-1, 1:-1, :]
    z_padded = jnp.pad(center, ((0, 0), (0, 0), (0, 0), (1, 1)))
    total = padded[:, 2:, 1:-1, :] + padded[:, :-2, 1:-1, :]
    total = total + padded[:, 1:-1, 2:, :] + padded[:, 1:-1, :-2, :]
    total = total + z_padded[..., 2:] + z_padded[..., :-2]
    return total - 6.0 * center


def body(species, cell_factor, species_rate, factor_x, factor_y, factor_species):
    nspec, cells_x, merged = species.shape
    cells_y = factor_y.shape[0]
    depth = merged // cells_y
    field = species.reshape(nspec, cells_x, cells_y, depth)
    factor_grid = cell_factor.reshape(cells_x, cells_y, depth)
    rate_field = species_rate[:, None, None, None] * factor_grid[None]
    for iteration in range(2):
        padded = padded_2(field, (("tx", 1), ("ty", 2)), 1)
        field = field + rate_field * laplace(padded)
    advanced = field.reshape(nspec, cells_x, merged)
    reduced = jnp.einsum("sq,sxv->qxv", factor_species, advanced, precision=exact_mode)
    first = lax.psum_scatter(
        jnp.einsum("xa,qxv->aqv", factor_x, reduced, precision=exact_mode),
        "tx",
        scatter_dimension=0,
        tiled=True,
    )
    local_rank = first.shape[0]
    ranks_q = first.shape[1]
    first = first.reshape(local_rank, ranks_q, cells_y, depth)
    rank_y = factor_y.shape[1]
    partial_value = jnp.einsum("yb,aqyz->aqbz", factor_y, first, precision=exact_mode)
    partial_value = partial_value.reshape(local_rank, ranks_q, rank_y * depth)
    core = lax.psum_scatter(partial_value, "ty", scatter_dimension=2, tiled=True)
    return (advanced, core)


def solution(mesh):
    in_specs = (P(None, "tx", "ty"), P("tx", "ty"), P(), P("tx", None), P("ty", None), P())
    out_specs = (P(None, "tx", "ty"), P("tx", None, "ty"))
    return jax.shard_map(body, mesh=mesh, in_specs=in_specs, out_specs=out_specs, check_vma=False)
```

profile of v0, /device:TPU:1, one launch (start us, length us, event | category | flops | bytes accessed | tf_op | source)
XLA Modules:
  0.0 367.6 jit_solution(9832291149560014561)
XLA Ops:
  7.2 3.8 %reshape.18 = f32[32,32,8,32]{3,2,1,0:T(8,128)} reshape(f32[32,32,256]{2,1,0:T(8,128)} %param.6) | data formatting | bytes 2097152 | tf_op jit(solution)/shard_map/reshape | solution.py:35
  12.0 4.6 %collective-permute-start.1 = (f32[32,1,8,32]{3,2,1,0:T(8,128)S(1)}, f32[32,1,8,32]{3,2,1,0:T(8,128)S(1)}, u32[]{:S(2)}, u32[]{:S(2)}) collective-permute-start(f32[32,1,8,32]{3,2,1,0:T(8,128)S(1)} %get-tuple-element.11), channel_id=1, source_target_pairs={{0,16},{16,32},{32,48},{48,64},{64,80},{80,96},{96,112},{112,128},... | collective-permute-start | bytes 98312 | tf_op jit(solution)/shard_map/ppermute | solution.py:16
  16.6 5.5 %collective-permute-start = (f32[32,1,8,32]{3,2,1,0:T(8,128)S(1)}, f32[32,1,8,32]{3,2,1,0:T(8,128)S(1)}, u32[]{:S(2)}, u32[]{:S(2)}) collective-permute-start(f32[32,1,8,32]{3,2,1,0:T(8,128)S(1)} %get-tuple-element.10), channel_id=1, source_target_pairs={{16,0},{32,16},{48,32},{64,48},{80,64},{96,80},{112,96},{128,112},... | collective-permute-start | bytes 98312 | tf_op jit(solution)/shard_map/ppermute | solution.py:17
  22.1 2.5 constant_dynamic-update-slice_fusion.1
  24.7 2.0 copy-done.2
  31.1 9.4 %collective-permute-done.3 = f32[32,34,1,32]{1,3,2,0:T(8,128)S(1)} collective-permute-done((f32[32,34,1,32]{1,3,2,0:T(8,128)S(1)}, f32[32,34,1,32]{1,3,2,0:T(8,128)S(1)}, u32[]{:S(2)}, u32[]{:S(2)}) %collective-permute-start.3) | collective-permute-done | bytes 139296 | tf_op jit(solution)/shard_map/ppermute | solution.py:16
  40.9 4.2 %collective-permute-done.2 = f32[32,34,1,32]{1,3,2,0:T(8,128)S(1)} collective-permute-done((f32[32,34,1,32]{1,3,2,0:T(8,128)S(1)}, f32[32,34,1,32]{1,3,2,0:T(8,128)S(1)}, u32[]{:S(2)}, u32[]{:S(2)}) %collective-permute-start.2) | collective-permute-done | bytes 139296 | tf_op jit(solution)/shard_map/ppermute | solution.py:17
  45.6 12.4 %fusion = f32[32,32,8,32]{3,2,1,0:T(8,128)S(1)} fusion(f32[32,32,8,32]{3,2,1,0:T(8,128)} %reshape.18, f32[32,34,8,32]{3,2,1,0:T(8,128)} %copy-done.2, f32[32,34,1,32]{3,2,1,0:T(1,128)S(1)} %copy.21, f32[32,34,1,32]{3,2,1,0:T(1,128)S(1)} %copy.19, f32[32,1,8,32]{3,2,1,0:T(8,128)S(1)} %collective-permute-done.1, f32[32,1,8,32]{3,2,1,0:T(8,128)S(1)} %collective-permute-done, ...), kind=kLoop, calls=%fused_computation.2 | loop fusion | flops 3670016 | bytes 3588224 | tf_op jit(solution)/shard_map/add | solution.py:40
  58.1 3.9 %collective-permute-start.5 = (f32[32,1,8,32]{3,2,1,0:T(8,128)S(1)}, f32[32,1,8,32]{3,2,1,0:T(8,128)S(1)}, u32[]{:S(2)}, u32[]{:S(2)}) collective-permute-start(f32[32,1,8,32]{3,2,1,0:T(8,128)S(1)} %get-tuple-element.8), channel_id=1, source_target_pairs={{0,16},{16,32},{32,48},{48,64},{64,80},{80,96},{96,112},{112,128},... | collective-permute-start | bytes 98312 | tf_op jit(solution)/shard_map/ppermute | solution.py:16
  61.9 1.9 collective-permute-start.4
  63.9 4.3 %collective-permute-done.4 = f32[32,1,8,32]{3,2,1,0:T(8,128)S(1)} collective-permute-done((f32[32,1,8,32]{3,2,1,0:T(8,128)S(1)}, f32[32,1,8,32]{3,2,1,0:T(8,128)S(1)}, u32[]{:S(2)}, u32[]{:S(2)}) %collective-permute-start.4) | collective-permute-done | bytes 32800 | tf_op jit(solution)/shard_map/ppermute | solution.py:17
  69.5 3.1 collective-permute-start.7
  73.0 1.5 collective-permute-start.6
  74.5 7.2 %collective-permute-done.7 = f32[32,34,1,32]{1,3,2,0:T(8,128)S(1)} collective-permute-done((f32[32,34,1,32]{1,3,2,0:T(8,128)S(1)}, f32[32,34,1,32]{1,3,2,0:T(8,128)S(1)}, u32[]{:S(2)}, u32[]{:S(2)}) %collective-permute-start.7) | collective-permute-done | bytes 139296 | tf_op jit(solution)/shard_map/ppermute | solution.py:16
  82.2 5.4 %collective-permute-done.6 = f32[32,34,1,32]{1,3,2,0:T(8,128)S(1)} collective-permute-done((f32[32,34,1,32]{1,3,2,0:T(8,128)S(1)}, f32[32,34,1,32]{1,3,2,0:T(8,128)S(1)}, u32[]{:S(2)}, u32[]{:S(2)}) %collective-permute-start.6) | collective-permute-done | bytes 139296 | tf_op jit(solution)/shard_map/ppermute | solution.py:17
  88.1 16.3 %fusion.1 = f32[32,32,8,32]{3,2,1,0:T(8,128)} fusion(f32[32,32,8,32]{3,2,1,0:T(8,128)} %copy-done.1, f32[32,34,1,32]{3,2,1,0:T(1,128)S(1)} %copy.25, f32[32,1,8,32]{3,2,1,0:T(8,128)S(1)} %collective-permute-done.4, f32[32,1,8,32]{3,2,1,0:T(8,128)S(1)} %collective-permute-done.5, f32[32,34,1,32]{3,2,1,0:T(1,128)S(1)} %copy.23, f32[32,8,32]{2,1,0:T(8,128)S(1)} %mul.28, ...), kind=kLoop, calls=%fused_computation.3 | loop fusion | flops 4718592 | bytes 2474112 | tf_op jit(solution)/shard_map/add | solution.py:40
  104.5 3.4 reshape.19
  109.1 3.5 convolution_bitcast_fusion
  112.6 2.1 copy.28
  115.0 147.1 %reduce-scatter.3.cloned.1.call-done = f32[4,16,256]{2,1,0:T(8,128)} async-done(((f32[128,16,256]{2,1,0:T(8,128)}), f32[4,16,256]{2,1,0:T(8,128)}) %reduce-scatter.3.cloned.1.call-update) | async-done | bytes 65552 | tf_op jit(solution)/shard_map/reduce_scatter | solution.py:43
  263.0 1.8 convolution_bitcast_fusion.1
  264.9 2.7 copy.29
  267.5 4.3 %reshape.21 = f32[4,16,4096]{2,1,0:T(8,128)} reshape(f32[4,16,128,32]{3,2,1,0:T(8,128)} %copy.29) | data formatting | bytes 2097152 | tf_op jit(solution)/shard_map/reshape | solution.py:54
  271.9 88.9 %reduce-scatter.5.cloned.1.call-done = f32[4,16,256]{2,1,0:T(8,128)} async-done(((f32[4,16,4096]{2,1,0:T(8,128)}), f32[4,16,256]{2,1,0:T(8,128)}) %reduce-scatter.5.cloned.1.call-update) | async-done | bytes 65552 | tf_op jit(solution)/shard_map/reduce_scatter | solution.py:55
  (41 shorter events, 11.4 us)
Async XLA Ops:
  7.2 102.0 %copy-start = (f32[32,128]{1,0:T(8,128)S(1)}, f32[32,128]{1,0:T(8,128)}, u32[]{:S(2)}) copy-start(f32[32,128]{1,0:T(8,128)} %param.9) | copy-start | bytes 49156
  7.2 254.9 %reduce-scatter.3.cloned.1.call-start = ((), (), s32[]{:S(2)}) async-start(), calls=%async_computation.2 | async-start | bytes 2162688 | tf_op jit(solution)/shard_map/reduce_scatter | solution.py:43
  12.0 10.1 %collective-permute-start.1 = (f32[32,1,8,32]{3,2,1,0:T(8,128)S(1)}, f32[32,1,8,32]{3,2,1,0:T(8,128)S(1)}, u32[]{:S(2)}, u32[]{:S(2)}) collective-permute-start(f32[32,1,8,32]{3,2,1,0:T(8,128)S(1)} %get-tuple-element.11), channel_id=1, source_target_pairs={{0,16},{16,32},{32,48},{48,64},{64,80},{80,96},{96,112},{112,128},... | collective-permute-start | bytes 98312 | tf_op jit(solution)/shard_map/ppermute | solution.py:16
  16.6 8.1 %collective-permute-start = (f32[32,1,8,32]{3,2,1,0:T(8,128)S(1)}, f32[32,1,8,32]{3,2,1,0:T(8,128)S(1)}, u32[]{:S(2)}, u32[]{:S(2)}) collective-permute-start(f32[32,1,8,32]{3,2,1,0:T(8,128)S(1)} %get-tuple-element.10), channel_id=1, source_target_pairs={{16,0},{32,16},{48,32},{64,48},{80,64},{96,80},{112,96},{128,112},... | collective-permute-start | bytes 98312 | tf_op jit(solution)/shard_map/ppermute | solution.py:17
  24.6 6.3 %copy-start.4 = (f32[32,256]{1,0:T(8,128)S(1)}, f32[32,256]{1,0:T(8,128)}, u32[]{:S(2)}) copy-start(f32[32,256]{1,0:T(8,128)} %param.7) | copy-start | bytes 98308
  24.7 20.9 %copy-start.7 = (f32[32]{0:T(128)S(1)}, f32[32]{0:T(128)}, u32[]{:S(2)}) copy-start(f32[32]{0:T(128)} %param.8) | copy-start | bytes 388
  24.7 2.0 copy-start.2
  27.9 12.6 %collective-permute-start.3 = (f32[32,34,1,32]{1,3,2,0:T(8,128)S(1)}, f32[32,34,1,32]{1,3,2,0:T(8,128)S(1)}, u32[]{:S(2)}, u32[]{:S(2)}) collective-permute-start(f32[32,34,1,32]{1,3,2,0:T(8,128)S(1)} %copy.20), channel_id=1, source_target_pairs={{0,1},{1,2},{2,3},{3,4},{4,5},{5,6},{6,7},{7,8},{8,9},{9,10},{10,1... | collective-permute-start | bytes 417800 | tf_op jit(solution)/shard_map/ppermute | solution.py:16
  29.7 15.4 %collective-permute-start.2 = (f32[32,34,1,32]{1,3,2,0:T(8,128)S(1)}, f32[32,34,1,32]{1,3,2,0:T(8,128)S(1)}, u32[]{:S(2)}, u32[]{:S(2)}) collective-permute-start(f32[32,34,1,32]{1,3,2,0:T(8,128)S(1)} %copy.18), channel_id=1, source_target_pairs={{1,0},{2,1},{3,2},{4,3},{5,4},{6,5},{7,6},{8,7},{9,8},{10,9},{11,1... | collective-permute-start | bytes 417800 | tf_op jit(solution)/shard_map/ppermute | solution.py:17
  58.0 10.2 %copy-start.1 = (f32[32,32,8,32]{3,2,1,0:T(8,128)}, f32[32,32,8,32]{3,2,1,0:T(8,128)S(1)}, u32[]{:S(2)}) copy-start(f32[32,32,8,32]{3,2,1,0:T(8,128)S(1)} %fusion) | copy-start | bytes 3145732
  58.1 5.8 %collective-permute-start.5 = (f32[32,1,8,32]{3,2,1,0:T(8,128)S(1)}, f32[32,1,8,32]{3,2,1,0:T(8,128)S(1)}, u32[]{:S(2)}, u32[]{:S(2)}) collective-permute-start(f32[32,1,8,32]{3,2,1,0:T(8,128)S(1)} %get-tuple-element.8), channel_id=1, source_target_pairs={{0,16},{16,32},{32,48},{48,64},{64,80},{80,96},{96,112},{112,128},... | collective-permute-start | bytes 98312 | tf_op jit(solution)/shard_map/ppermute | solution.py:16
  61.9 6.3 %collective-permute-start.4 = (f32[32,1,8,32]{3,2,1,0:T(8,128)S(1)}, f32[32,1,8,32]{3,2,1,0:T(8,128)S(1)}, u32[]{:S(2)}, u32[]{:S(2)}) collective-permute-start(f32[32,1,8,32]{3,2,1,0:T(8,128)S(1)} %get-tuple-element.9), channel_id=1, source_target_pairs={{16,0},{32,16},{48,32},{64,48},{80,64},{96,80},{112,96},{128,112},... | collective-permute-start | bytes 98312 | tf_op jit(solution)/shard_map/ppermute | solution.py:17
  69.5 12.2 %collective-permute-start.7 = (f32[32,34,1,32]{1,3,2,0:T(8,128)S(1)}, f32[32,34,1,32]{1,3,2,0:T(8,128)S(1)}, u32[]{:S(2)}, u32[]{:S(2)}) collective-permute-start(f32[32,34,1,32]{1,3,2,0:T(8,128)S(1)} %copy.24), channel_id=1, source_target_pairs={{0,1},{1,2},{2,3},{3,4},{4,5},{5,6},{6,7},{7,8},{8,9},{9,10},{10,1... | collective-permute-start | bytes 417800 | tf_op jit(solution)/shard_map/ppermute | solution.py:16
  73.0 14.6 %collective-permute-start.6 = (f32[32,34,1,32]{1,3,2,0:T(8,128)S(1)}, f32[32,34,1,32]{1,3,2,0:T(8,128)S(1)}, u32[]{:S(2)}, u32[]{:S(2)}) collective-permute-start(f32[32,34,1,32]{1,3,2,0:T(8,128)S(1)} %copy.22), channel_id=1, source_target_pairs={{1,0},{2,1},{3,2},{4,3},{5,4},{6,5},{7,6},{8,7},{9,8},{10,9},{11,1... | collective-permute-start | bytes 417800 | tf_op jit(solution)/shard_map/ppermute | solution.py:17
  104.5 3.4 copy-start.5
  107.8 6.8 %copy-start.3 = (f32[32,32,256]{2,1,0:T(8,128)}, f32[32,32,256]{2,1,0:T(8,128)S(1)}, u32[]{:S(2)}) copy-start(f32[32,32,256]{2,1,0:T(8,128)S(1)} %reshape.19) | copy-start | bytes 3145732
  109.1 153.9 %copy-start.6 = (f32[8,128]{1,0:T(8,128)S(1)}, f32[8,128]{1,0:T(8,128)}, u32[]{:S(2)}) copy-start(f32[8,128]{1,0:T(8,128)} %param.10) | copy-start | bytes 12292
  114.7 246.0 %reduce-scatter.5.cloned.1.call-start = ((), (), s32[]{:S(2)}) async-start(), calls=%async_computation.3 | async-start | bytes 1114112 | tf_op jit(solution)/shard_map/reduce_scatter | solution.py:55
Sparse Core Ops, SparseCore 0:
  114.8 147.1 reduce-scatter.2
  272.0 88.6 reduce-scatter.4
where the time goes:
time: 369 us; the launch traced here: 368 us
  waiting for transfers between devices  267 us (72%)
  other arithmetic  29.6 us (8%)
  local copies, waits for them, and re-layouts  27.1 us (7%)
  starting transfers between devices  23.4 us (6%)
  between operations  14.4 us (4%)
  matrix products  6.56 us (2%)
    reduce_scatter x1, waiting for transfers between devices, body(): lax.psum_scatter(jnp.einsum('xa,qxv->aqv', factor_x, reduced, precision=e...  147 us
    reduce_scatter x1, waiting for transfers between devices, body(): lax.psum_scatter(partial_value, 'ty', scatter_dimension=2, tiled=True)  88.9 us
    add x2, other arithmetic, body(): field = field + rate_field * laplace(padded)  28.8 us
    ppermute x4, waiting for transfers between devices, padded_2(): before = lax.ppermute(last, axis, up)  16.6 us
    ppermute x4, waiting for transfers between devices, padded_2(): after = lax.ppermute(first, axis, down)  14 us
    ppermute x4, starting transfers between devices, padded_2(): before = lax.ppermute(last, axis, up)  13 us
    ppermute x4, starting transfers between devices, padded_2(): after = lax.ppermute(first, axis, down)  10.2 us
  transfers between devices with their start and end apart: 10, of which 7 were waited for; matrix products, arithmetic and copies ran while one was open for 1% of the time, Pallas kernels for 0%

commit v1 on v0

--- a/solution.py
+++ b/solution.py
@@ -28,10 +28,19 @@
     return total - 6.0 * center
 
 
+def whole_of(block, axis):
+    count = lax.axis_size(axis)
+    copies = jnp.broadcast_to(block[None], (count,) + block.shape)
+    return lax.all_to_all(copies, axis, 0, 0, tiled=True).reshape((-1,) + block.shape[1:])
+
+
 def body(species, cell_factor, species_rate, factor_x, factor_y, factor_species):
     nspec, cells_x, merged = species.shape
     cells_y = factor_y.shape[0]
     depth = merged // cells_y
+    n_tx, n_ty = lax.axis_size("tx"), lax.axis_size("ty")
+    whole_x = whole_of(factor_x, "tx")
+    whole_y = whole_of(factor_y, "ty")
     field = species.reshape(nspec, cells_x, cells_y, depth)
     factor_grid = cell_factor.reshape(cells_x, cells_y, depth)
     rate_field = species_rate[:, None, None, None] * factor_grid[None]
@@ -40,20 +49,20 @@
         field = field + rate_field * laplace(padded)
     advanced = field.reshape(nspec, cells_x, merged)
     reduced = jnp.einsum("sq,sxv->qxv", factor_species, advanced, precision=exact_mode)
-    first = lax.psum_scatter(
-        jnp.einsum("xa,qxv->aqv", factor_x, reduced, precision=exact_mode),
-        "tx",
-        scatter_dimension=0,
-        tiled=True,
-    )
-    local_rank = first.shape[0]
-    ranks_q = first.shape[1]
-    first = first.reshape(local_rank, ranks_q, cells_y, depth)
-    rank_y = factor_y.shape[1]
-    partial_value = jnp.einsum("yb,aqyz->aqbz", factor_y, first, precision=exact_mode)
-    partial_value = partial_value.reshape(local_rank, ranks_q, rank_y * depth)
-    core = lax.psum_scatter(partial_value, "ty", scatter_dimension=2, tiled=True)
-    return (advanced, core)
+    ranks_q = reduced.shape[0]
+    planes = reduced.reshape(ranks_q, cells_x, cells_y, depth).transpose(3, 1, 0, 2)
+    planes = planes.reshape(depth, cells_x, ranks_q * cells_y)
+    planes = lax.all_to_all(planes, "tx", 0, 0, tiled=True).reshape(-1, ranks_q * cells_y)
+    first = lax.dot_general(planes, whole_x, (((0,), (0,)), ((), ())), precision=exact_mode)
+    first = first.reshape(ranks_q, cells_y, -1)
+    first = lax.all_to_all(first, "ty", 0, 0, tiled=True).reshape(n_ty * cells_y, -1)
+    plane = lax.dot_general(first, whole_y, (((0,), (0,)), ((), ())), precision=exact_mode)
+    rank_a, rank_b = plane.shape
+    plane = plane.reshape(n_tx, rank_a // n_tx, n_ty, rank_b // n_ty).transpose(0, 2, 1, 3)
+    plane = plane.reshape(n_tx * n_ty, 1, -1)
+    core = lax.all_to_all(plane, ("tx", "ty"), 0, 0, tiled=True)
+    core = core.reshape(depth, ranks_q, rank_a // n_tx, rank_b // n_ty).transpose(2, 1, 3, 0)
+    return advanced, core.reshape(rank_a // n_tx, ranks_q, -1)
 
 
 def solution(mesh):

time: 369 us -> 247 us (0.67)
  waiting for transfers between devices: 267 us -> 55.8 us
  blocking collectives: 0 us -> 54.8 us
  starting transfers between devices: 23.4 us -> 76.9 us
  between operations: 14.4 us -> 1.02 us
    reduce_scatter x2 -> x0, waiting for transfers between devices: 236 us -> none  [the longest x1 147 us: body(): lax.psum_scatter(jnp.einsum('xa,qxv->aqv', factor_x, reduced, precision=e...]
    all_to_all x0 -> x2, blocking collectives: none -> 54.8 us  [the longest x1 30.3 us: body(): core = lax.all_to_all(plane, ('tx', 'ty'), 0, 0, tiled=True)]
    all_to_all x0 -> x3, starting transfers between devices: none -> 49.8 us  [the longest x2 46.2 us: whole_of(): lax.all_to_all(copies, axis, 0, 0, tiled=True)]
    all_to_all x0 -> x3, waiting for transfers between devices: none -> 33.1 us  [the longest x2 24.3 us: whole_of(): lax.all_to_all(copies, axis, 0, 0, tiled=True)]
    ppermute x4, waiting for transfers between devices: 16.6 us -> 4.26 us  [padded_2(): before = lax.ppermute(last, axis, up)]
    ppermute x4, waiting for transfers between devices: 14 us -> 18.5 us  [padded_2(): after = lax.ppermute(first, axis, down)]
    ppermute x4, starting transfers between devices: 13 us -> 16.7 us  [padded_2(): before = lax.ppermute(last, axis, up)]
  transfers between devices with their start and end apart: 10 -> 11, of which waited for: 7 -> 9; matrix products, arithmetic and copies ran while one was open for 1% -> 2% of each run, Pallas kernels for 0% -> 0%
where the time goes in v1:
time: 247 us; the launch traced here: 246 us
  starting transfers between devices  76.9 us (31%)
  waiting for transfers between devices  55.8 us (23%)
  blocking collectives  54.8 us (22%)
  other arithmetic  29.8 us (12%)
  local copies, waits for them, and re-layouts  23.8 us (10%)
  matrix products  3.82 us (2%)
    all_to_all x2, starting transfers between devices, whole_of(): lax.all_to_all(copies, axis, 0, 0, tiled=True)  46.2 us
    all_to_all x1, blocking collectives, body(): core = lax.all_to_all(plane, ('tx', 'ty'), 0, 0, tiled=True)  30.3 us
    add x2, other arithmetic, body(): field = field + rate_field * laplace(padded)  29 us
    all_to_all x1, blocking collectives, body(): lax.all_to_all(planes, 'tx', 0, 0, tiled=True)  24.5 us
    all_to_all x2, waiting for transfers between devices, whole_of(): lax.all_to_all(copies, axis, 0, 0, tiled=True)  24.3 us
    ppermute x4, waiting for transfers between devices, padded_2(): after = lax.ppermute(first, axis, down)  18.5 us
    ppermute x4, starting transfers between devices, padded_2(): before = lax.ppermute(last, axis, up)  16.7 us
    ppermute x4, starting transfers between devices, padded_2(): after = lax.ppermute(first, axis, down)  10.5 us
  transfers between devices with their start and end apart: 11, of which 9 were waited for; matrix products, arithmetic and copies ran while one was open for 2% of the time, Pallas kernels for 0%

profile of v1, /device:TPU:1, one launch (start us, length us, event | category | flops | bytes accessed | tf_op | source)
XLA Modules:
  0.0 245.9 jit_solution(15656150274058205356)
XLA Ops:
  0.6 3.8 %reshape.46 = f32[32,32,8,32]{3,2,1,0:T(8,128)} reshape(f32[32,32,256]{2,1,0:T(8,128)} %param.6) | data formatting | bytes 2097152 | tf_op jit(solution)/shard_map/reshape | solution.py:44
  5.5 4.6 %collective-permute-start.1 = (f32[32,1,8,32]{3,2,1,0:T(8,128)S(1)}, f32[32,1,8,32]{3,2,1,0:T(8,128)S(1)}, u32[]{:S(2)}, u32[]{:S(2)}) collective-permute-start(f32[32,1,8,32]{3,2,1,0:T(8,128)S(1)} %get-tuple-element.17), channel_id=1, source_target_pairs={{0,16},{16,32},{32,48},{48,64},{64,80},{80,96},{96,112},{112,128},... | collective-permute-start | bytes 98312 | tf_op jit(solution)/shard_map/ppermute | solution.py:16
  10.1 5.5 %collective-permute-start = (f32[32,1,8,32]{3,2,1,0:T(8,128)S(1)}, f32[32,1,8,32]{3,2,1,0:T(8,128)S(1)}, u32[]{:S(2)}, u32[]{:S(2)}) collective-permute-start(f32[32,1,8,32]{3,2,1,0:T(8,128)S(1)} %get-tuple-element.16), channel_id=1, source_target_pairs={{16,0},{32,16},{48,32},{64,48},{80,64},{96,80},{112,96},{128,112},... | collective-permute-start | bytes 98312 | tf_op jit(solution)/shard_map/ppermute | solution.py:17
  15.6 2.5 %constant_dynamic-update-slice_fusion.1 = f32[32,34,8,32]{3,2,1,0:T(8,128)S(1)} fusion(f32[32,34,8,32]{3,2,1,0:T(8,128)S(1)} %constant_dynamic-update-slice_fusion.2, f32[32,32,8,32]{3,2,1,0:T(8,128)} %reshape.46), kind=kLoop, calls=%fused_computation.40 | loop fusion | bytes 5242880
  18.2 2.0 copy-done.2
  23.1 4.0 %collective-permute-start.3 = (f32[32,34,1,32]{1,3,2,0:T(8,128)S(1)}, f32[32,34,1,32]{1,3,2,0:T(8,128)S(1)}, u32[]{:S(2)}, u32[]{:S(2)}) collective-permute-start(f32[32,34,1,32]{1,3,2,0:T(8,128)S(1)} %copy.46), channel_id=1, source_target_pairs={{0,1},{1,2},{2,3},{3,4},{4,5},{5,6},{6,7},{7,8},{8,9},{9,10},{10,1... | collective-permute-start | bytes 417800 | tf_op jit(solution)/shard_map/ppermute | solution.py:16
  27.2 9.7 %collective-permute-done.2 = f32[32,34,1,32]{1,3,2,0:T(8,128)S(1)} collective-permute-done((f32[32,34,1,32]{1,3,2,0:T(8,128)S(1)}, f32[32,34,1,32]{1,3,2,0:T(8,128)S(1)}, u32[]{:S(2)}, u32[]{:S(2)}) %collective-permute-start.2) | collective-permute-done | bytes 139296 | tf_op jit(solution)/shard_map/ppermute | solution.py:17
  39.1 12.5 %fusion = f32[32,32,8,32]{3,2,1,0:T(8,128)S(1)} fusion(f32[32,32,8,32]{3,2,1,0:T(8,128)} %reshape.46, f32[32,34,8,32]{3,2,1,0:T(8,128)} %copy-done.2, f32[32,34,1,32]{3,2,1,0:T(1,128)S(1)} %copy.47, f32[32,34,1,32]{3,2,1,0:T(1,128)S(1)} %copy.45, f32[32,1,8,32]{3,2,1,0:T(8,128)S(1)} %collective-permute-done.1, f32[32,1,8,32]{3,2,1,0:T(8,128)S(1)} %collective-permute-done, ...), kind=kLoop, calls=%fused_computation.2 | loop fusion | flops 3670016 | bytes 3588224 | tf_op jit(solution)/shard_map/add | solution.py:49
  51.7 2.4 collective-permute-start.4
  54.1 3.1 %collective-permute-start.5 = (f32[32,1,8,32]{3,2,1,0:T(8,128)S(1)}, f32[32,1,8,32]{3,2,1,0:T(8,128)S(1)}, u32[]{:S(2)}, u32[]{:S(2)}) collective-permute-start(f32[32,1,8,32]{3,2,1,0:T(8,128)S(1)} %get-tuple-element.14), channel_id=1, source_target_pairs={{0,16},{16,32},{32,48},{48,64},{64,80},{80,96},{96,112},{112,128},... | collective-permute-start | bytes 98312 | tf_op jit(solution)/shard_map/ppermute | solution.py:16
  62.1 4.9 %collective-permute-start.7 = (f32[32,34,1,32]{1,3,2,0:T(8,128)S(1)}, f32[32,34,1,32]{1,3,2,0:T(8,128)S(1)}, u32[]{:S(2)}, u32[]{:S(2)}) collective-permute-start(f32[32,34,1,32]{1,3,2,0:T(8,128)S(1)} %copy.50), channel_id=1, source_target_pairs={{0,1},{1,2},{2,3},{3,4},{4,5},{5,6},{6,7},{7,8},{8,9},{9,10},{10,1... | collective-permute-start | bytes 417800 | tf_op jit(solution)/shard_map/ppermute | solution.py:16
  67.1 8.1 %collective-permute-done.6 = f32[32,34,1,32]{1,3,2,0:T(8,128)S(1)} collective-permute-done((f32[32,34,1,32]{1,3,2,0:T(8,128)S(1)}, f32[32,34,1,32]{1,3,2,0:T(8,128)S(1)}, u32[]{:S(2)}, u32[]{:S(2)}) %collective-permute-start.6) | collective-permute-done | bytes 139296 | tf_op jit(solution)/shard_map/ppermute | solution.py:17
  75.7 1.7 collective-permute-done.7
  77.9 16.5 %fusion.1 = f32[32,32,8,32]{3,2,1,0:T(8,128)} fusion(f32[32,32,8,32]{3,2,1,0:T(8,128)} %copy-done.1, f32[32,34,1,32]{3,2,1,0:T(1,128)S(1)} %copy.51, f32[32,1,8,32]{3,2,1,0:T(8,128)S(1)} %collective-permute-done.4, f32[32,1,8,32]{3,2,1,0:T(8,128)S(1)} %collective-permute-done.5, f32[32,34,1,32]{3,2,1,0:T(1,128)S(1)} %copy.49, f32[32,8,32]{2,1,0:T(8,128)S(1)} %mul.28, ...), kind=kLoop, calls=%fused_computation.3 | loop fusion | flops 4718592 | bytes 2474112 | tf_op jit(solution)/shard_map/add | solution.py:49
  94.4 3.3 %reshape.47 = f32[32,32,256]{2,1,0:T(8,128)S(1)} reshape(f32[32,32,8,32]{3,2,1,0:T(8,128)} %fusion.1) | data formatting | bytes 2097152 | tf_op jit(solution)/shard_map/reshape | solution.py:50
  97.8 2.1 convolution_bitcast_fusion
  102.9 24.5 %all_to_all.25 = f32[32,32,128]{2,1,0:T(8,128)S(1)} all-to-all(f32[32,32,128]{2,1,0:T(8,128)} %copy.54), channel_id=1, replica_groups=mesh['tx'=32,'ty'=16] {'tx'}, dimensions={0} | all-to-all | bytes 1048576 | tf_op jit(solution)/shard_map/all_to_all | solution.py:55
  128.3 5.7 %all-to-all-start.1 = ((f32[32,32,128]{2,1,0:T(8,128)}), f32[32,32,128]{2,1,0:T(8,128)S(1)}, u32[]{:S(2)}, u32[]{:S(2)}) async-start(f32[32,32,128]{2,1,0:T(8,128)} %broadcast_in_dim.4), calls=%async_computation.1 | async-start | bytes 1048576 | tf_op jit(solution)/shard_map/all_to_all | solution.py:34
  134.1 16.5 %all-to-all-done.1 = f32[32,32,128]{2,1,0:T(8,128)S(1)} async-done(((f32[32,32,128]{2,1,0:T(8,128)}), f32[32,32,128]{2,1,0:T(8,128)S(1)}, u32[]{:S(2)}, u32[]{:S(2)}) %all-to-all-start.1) | async-done | bytes 524320 | tf_op jit(solution)/shard_map/all_to_all | solution.py:34
  151.3 40.6 %all-to-all-start.3 = ((f32[16,8,128]{2,1,0:T(8,128)}), f32[16,8,128]{2,1,0:T(8,128)S(1)}, u32[]{:S(2)}, u32[]{:S(2)}) async-start(f32[16,8,128]{2,1,0:T(8,128)} %broadcast_in_dim.5), calls=%async_computation.3 | async-start | bytes 131072 | tf_op jit(solution)/shard_map/all_to_all | solution.py:34
  193.2 7.7 %all-to-all-done.3 = f32[16,8,128]{2,1,0:T(8,128)S(1)} async-done(((f32[16,8,128]{2,1,0:T(8,128)}), f32[16,8,128]{2,1,0:T(8,128)S(1)}, u32[]{:S(2)}, u32[]{:S(2)}) %all-to-all-start.3) | async-done | bytes 65568 | tf_op jit(solution)/shard_map/all_to_all | solution.py:34
  200.9 3.5 %all-to-all-start.2 = ((f32[16,8,128]{2,1,0:T(8,128)}), f32[16,8,128]{2,1,0:T(8,128)S(1)}, u32[]{:S(2)}, u32[]{:S(2)}) async-start(f32[16,8,128]{2,1,0:T(8,128)} %fusion.15), calls=%async_computation.2 | async-start | bytes 131072 | tf_op jit(solution)/shard_map/all_to_all | solution.py:58
  204.5 8.8 %all-to-all-done.2 = f32[16,8,128]{2,1,0:T(8,128)S(1)} async-done(((f32[16,8,128]{2,1,0:T(8,128)}), f32[16,8,128]{2,1,0:T(8,128)S(1)}, u32[]{:S(2)}, u32[]{:S(2)}) %all-to-all-start.2) | async-done | bytes 65568 | tf_op jit(solution)/shard_map/all_to_all | solution.py:58
  214.5 30.3 %all_to_all.26 = f32[512,1,32]{2,1,0:T(1,128)S(1)} all-to-all(f32[512,1,32]{2,1,0:T(1,128)S(1)} %copy.61), channel_id=1, replica_groups=mesh['tx'=32,'ty'=16] {'tx','ty'}, dimensions={0} | all-to-all | bytes 131072 | tf_op jit(solution)/shard_map/all_to_all | solution.py:63
  (52 shorter events, 20.4 us)
Async XLA Ops:
  0.6 97.1 %copy-start = (f32[32,16]{0,1:T(8,128)S(1)}, f32[32,16]{0,1:T(8,128)}, u32[]{:S(2)}) copy-start(f32[32,16]{0,1:T(8,128)} %param.11) | copy-start | bytes 6148
  5.5 10.1 %collective-permute-start.1 = (f32[32,1,8,32]{3,2,1,0:T(8,128)S(1)}, f32[32,1,8,32]{3,2,1,0:T(8,128)S(1)}, u32[]{:S(2)}, u32[]{:S(2)}) collective-permute-start(f32[32,1,8,32]{3,2,1,0:T(8,128)S(1)} %get-tuple-element.17), channel_id=1, source_target_pairs={{0,16},{16,32},{32,48},{48,64},{64,80},{80,96},{96,112},{112,128},... | collective-permute-start | bytes 98312 | tf_op jit(solution)/shard_map/ppermute | solution.py:16
  10.1 8.1 %collective-permute-start = (f32[32,1,8,32]{3,2,1,0:T(8,128)S(1)}, f32[32,1,8,32]{3,2,1,0:T(8,128)S(1)}, u32[]{:S(2)}, u32[]{:S(2)}) collective-permute-start(f32[32,1,8,32]{3,2,1,0:T(8,128)S(1)} %get-tuple-element.16), channel_id=1, source_target_pairs={{16,0},{32,16},{48,32},{64,48},{80,64},{96,80},{112,96},{128,112},... | collective-permute-start | bytes 98312 | tf_op jit(solution)/shard_map/ppermute | solution.py:17
  18.1 9.0 %copy-start.4 = (f32[32,256]{1,0:T(8,128)S(1)}, f32[32,256]{1,0:T(8,128)}, u32[]{:S(2)}) copy-start(f32[32,256]{1,0:T(8,128)} %param.7) | copy-start | bytes 98308
  18.1 21.0 %copy-start.7 = (f32[32]{0:T(128)S(1)}, f32[32]{0:T(128)}, u32[]{:S(2)}) copy-start(f32[32]{0:T(128)} %param.8) | copy-start | bytes 388
  18.2 2.1 copy-start.2
  21.3 15.5 %collective-permute-start.2 = (f32[32,34,1,32]{1,3,2,0:T(8,128)S(1)}, f32[32,34,1,32]{1,3,2,0:T(8,128)S(1)}, u32[]{:S(2)}, u32[]{:S(2)}) collective-permute-start(f32[32,34,1,32]{1,3,2,0:T(8,128)S(1)} %copy.44), channel_id=1, source_target_pairs={{1,0},{2,1},{3,2},{4,3},{5,4},{6,5},{7,6},{8,7},{9,8},{10,9},{11,1... | collective-permute-start | bytes 417800 | tf_op jit(solution)/shard_map/ppermute | solution.py:17
  23.1 15.6 %collective-permute-start.3 = (f32[32,34,1,32]{1,3,2,0:T(8,128)S(1)}, f32[32,34,1,32]{1,3,2,0:T(8,128)S(1)}, u32[]{:S(2)}, u32[]{:S(2)}) collective-permute-start(f32[32,34,1,32]{1,3,2,0:T(8,128)S(1)} %copy.46), channel_id=1, source_target_pairs={{0,1},{1,2},{2,3},{3,4},{4,5},{5,6},{6,7},{7,8},{8,9},{9,10},{10,1... | collective-permute-start | bytes 417800 | tf_op jit(solution)/shard_map/ppermute | solution.py:16
  51.6 7.5 %copy-start.1 = (f32[32,32,8,32]{3,2,1,0:T(8,128)}, f32[32,32,8,32]{3,2,1,0:T(8,128)S(1)}, u32[]{:S(2)}) copy-start(f32[32,32,8,32]{3,2,1,0:T(8,128)S(1)} %fusion) | copy-start | bytes 3145732
  51.7 6.3 %collective-permute-start.4 = (f32[32,1,8,32]{3,2,1,0:T(8,128)S(1)}, f32[32,1,8,32]{3,2,1,0:T(8,128)S(1)}, u32[]{:S(2)}, u32[]{:S(2)}) collective-permute-start(f32[32,1,8,32]{3,2,1,0:T(8,128)S(1)} %get-tuple-element.15), channel_id=1, source_target_pairs={{16,0},{32,16},{48,32},{64,48},{80,64},{96,80},{112,96},{128,112},... | collective-permute-start | bytes 98312 | tf_op jit(solution)/shard_map/ppermute | solution.py:17
  54.1 5.1 %collective-permute-start.5 = (f32[32,1,8,32]{3,2,1,0:T(8,128)S(1)}, f32[32,1,8,32]{3,2,1,0:T(8,128)S(1)}, u32[]{:S(2)}, u32[]{:S(2)}) collective-permute-start(f32[32,1,8,32]{3,2,1,0:T(8,128)S(1)} %get-tuple-element.14), channel_id=1, source_target_pairs={{0,16},{16,32},{32,48},{48,64},{64,80},{80,96},{96,112},{112,128},... | collective-permute-start | bytes 98312 | tf_op jit(solution)/shard_map/ppermute | solution.py:16
  60.4 14.8 %collective-permute-start.6 = (f32[32,34,1,32]{1,3,2,0:T(8,128)S(1)}, f32[32,34,1,32]{1,3,2,0:T(8,128)S(1)}, u32[]{:S(2)}, u32[]{:S(2)}) collective-permute-start(f32[32,34,1,32]{1,3,2,0:T(8,128)S(1)} %copy.48), channel_id=1, source_target_pairs={{1,0},{2,1},{3,2},{4,3},{5,4},{6,5},{7,6},{8,7},{9,8},{10,9},{11,1... | collective-permute-start | bytes 417800 | tf_op jit(solution)/shard_map/ppermute | solution.py:17
  62.1 15.3 %collective-permute-start.7 = (f32[32,34,1,32]{1,3,2,0:T(8,128)S(1)}, f32[32,34,1,32]{1,3,2,0:T(8,128)S(1)}, u32[]{:S(2)}, u32[]{:S(2)}) collective-permute-start(f32[32,34,1,32]{1,3,2,0:T(8,128)S(1)} %copy.50), channel_id=1, source_target_pairs={{0,1},{1,2},{2,3},{3,4},{4,5},{5,6},{6,7},{7,8},{8,9},{9,10},{10,1... | collective-permute-start | bytes 417800 | tf_op jit(solution)/shard_map/ppermute | solution.py:16
  97.8 30.5 %copy-start.3 = (f32[32,32,256]{2,1,0:T(8,128)}, f32[32,32,256]{2,1,0:T(8,128)S(1)}, u32[]{:S(2)}) copy-start(f32[32,32,256]{2,1,0:T(8,128)S(1)} %reshape.47) | copy-start | bytes 3145732
  97.8 29.6 %copy-start.5 = (f32[32,128]{1,0:T(8,128)S(1)}, f32[32,128]{1,0:T(8,128)}, u32[]{:S(2)}) copy-start(f32[32,128]{1,0:T(8,128)} %param.9) | copy-start | bytes 49156
  99.9 50.8 %copy-start.6 = (f32[8,128]{1,0:T(8,128)S(1)}, f32[8,128]{1,0:T(8,128)}, u32[]{:S(2)}) copy-start(f32[8,128]{1,0:T(8,128)} %param.10) | copy-start | bytes 12292
  128.3 22.4 %all-to-all-start.1 = ((f32[32,32,128]{2,1,0:T(8,128)}), f32[32,32,128]{2,1,0:T(8,128)S(1)}, u32[]{:S(2)}, u32[]{:S(2)}) async-start(f32[32,32,128]{2,1,0:T(8,128)} %broadcast_in_dim.4), calls=%async_computation.1 | async-start | bytes 1048576 | tf_op jit(solution)/shard_map/all_to_all | solution.py:34
  151.3 49.6 %all-to-all-start.3 = ((f32[16,8,128]{2,1,0:T(8,128)}), f32[16,8,128]{2,1,0:T(8,128)S(1)}, u32[]{:S(2)}, u32[]{:S(2)}) async-start(f32[16,8,128]{2,1,0:T(8,128)} %broadcast_in_dim.5), calls=%async_computation.3 | async-start | bytes 131072 | tf_op jit(solution)/shard_map/all_to_all | solution.py:34
  200.9 12.4 %all-to-all-start.2 = ((f32[16,8,128]{2,1,0:T(8,128)}), f32[16,8,128]{2,1,0:T(8,128)S(1)}, u32[]{:S(2)}, u32[]{:S(2)}) async-start(f32[16,8,128]{2,1,0:T(8,128)} %fusion.15), calls=%async_computation.2 | async-start | bytes 131072 | tf_op jit(solution)/shard_map/all_to_all | solution.py:58

commit v2 on v1

v2 whole, which is shorter than its diff:
```python
import jax
import jax.numpy as jnp
from jax import lax
from jax.experimental import pallas as pl
from jax.experimental.pallas import tpu as pltpu
from jax.sharding import PartitionSpec as P

exact_mode = lax.Precision.HIGHEST
f32, bf16 = jnp.float32, jnp.bfloat16
NS, NX, NV, NH, NZ, NQ = 32, 32, 256, 128, 32, 16


def lanes(rows):
    return lax.broadcasted_iota(jnp.int32, (rows, 128), 1)


def pack_kernel(c0_ref, c1_ref, k_ref, xl_ref, xh_ref, yl_ref, yh_ref, mm_ref, mp_ref, pm_ref, pp_ref):
    low = lanes(NS // 2) < 64

    def row(x):
        return [r[pl.ds(x, NS, stride=NX), :] for r in (c0_ref, c1_ref)]

    for ref, at, x in ((xl_ref, 0, 0), (xl_ref, NS, 1), (xh_ref, 0, NX - 1), (xh_ref, NS, NX - 2)):
        ref[at : at + NS, :128], ref[at : at + NS, 128:] = row(x)
    xl_ref[2 * NS :, :] = jnp.broadcast_to(k_ref[0:1, :], (8, NV))
    xh_ref[2 * NS :, :] = jnp.broadcast_to(k_ref[NX - 1 : NX, :], (8, NV))
    mm_ref[...], mp_ref[...] = row(0)
    pm_ref[...], pp_ref[...] = row(NX - 1)
    half = NS // 2
    for x in range(NX):
        t0, t1 = row(x)
        yl_ref[x * half : (x + 1) * half, :] = jnp.where(low, t0[:half], pltpu.roll(t0[half:], 64, 1))
        yh_ref[x * half : (x + 1) * half, :] = jnp.where(low, pltpu.roll(t1[half:], 64, 1), t1[:half])
    yl_ref[NX * half :, :] = k_ref[:, :128]
    yh_ref[NX * half :, :] = k_ref[:, 128:]


def whole_block(shape):
    return pl.BlockSpec(shape, lambda i: (0, 0))


def halves(v):
    return [pl.BlockSpec((v.shape[0], 128), lambda i, side=side: (0, side)) for side in range(2)]


def pack(c2d, k):
    shapes = [(2 * NS + 8, NV)] * 2 + [(NX * NS // 2 + NX, 128)] * 2 + [(NS, 128)] * 4
    return pl.pallas_call(
        pack_kernel,
        grid=(1,),
        out_shape=[jax.ShapeDtypeStruct(s, f32) for s in shapes],
        in_specs=halves(c2d) + [whole_block(k.shape)],
        out_specs=[whole_block(s) for s in shapes],
        name="pack_faces",
    )(c2d, c2d, k)


def split_2(v):
    hi = v.astype(bf16)
    return hi, (v - hi.astype(f32)).astype(bf16)


def advance_kernel(c0_ref, c1_ref, k_ref, rate_ref, fs_ref, xl_ref, xh_ref, yl_ref, yh_ref, mm_ref, mp_ref, pm_ref, pp_ref, whole_ref,
                   adv_ref, planes_ref, e0, e1, ke, left, right):
    half = NS // 2
    lane_s, lane_h, lane_q = lanes(NS), lanes(half), lanes(NQ)
    z = lane_s % NZ
    not_first, not_last = z > 0, z < NZ - 1
    below, above = lane_s >= 32, lane_s < 96

    low_s, low_h = lane_s < 64, lane_h < 64
    e0[0, :, :NV] = xh_ref[NS : 2 * NS, :]
    e0[1, :, :NV] = xh_ref[0:NS, :]
    e0[1, :, NV:] = jnp.where(low_s, pm_ref[...], pp_ref[...])
    e0[NX + 2, :, :NV] = xl_ref[0:NS, :]
    e0[NX + 2, :, NV:] = jnp.where(low_s, mm_ref[...], mp_ref[...])
    e0[NX + 3, :, :NV] = xl_ref[NS : 2 * NS, :]
    e0[0, :, NV:] = jnp.zeros((NS, NH), f32)
    e0[NX + 3, :, NV:] = jnp.zeros((NS, NH), f32)
    for x in range(NX):
        after, before = yl_ref[x * half : (x + 1) * half, :], yh_ref[x * half : (x + 1) * half, :]
        e0[x + 2, :, :128] = c0_ref[pl.ds(x, NS, stride=NX), :]
        e0[x + 2, :, 128:NV] = c1_ref[pl.ds(x, NS, stride=NX), :]
        e0[x + 2, :half, NV:] = jnp.where(low_h, after, before)
        e0[x + 2, half:, NV:] = pltpu.roll(jnp.where(low_h, before, after), 64, 1)
    ke[8 : 8 + NX, :NV] = k_ref[...]
    ke[8 : 8 + NX, NV:] = jnp.where(lanes(NX) < 64, yl_ref[NX * half :, :], yh_ref[NX * half :, :])
    ke[0:8, :NV] = xh_ref[2 * NS :, :]
    ke[0:8, NV:] = jnp.zeros((8, NH), f32)
    ke[8 + NX :, :NV] = xl_ref[2 * NS :, :]
    ke[8 + NX :, NV:] = jnp.zeros((8, NH), f32)
    rate = jnp.broadcast_to(rate_ref[...], (NS, 128))

    def step(src, row, k_row, tiles):
        t = [src[row, :, i * 128 : (i + 1) * 128] for i in range(3)]
        up = [pltpu.roll(v, 96, 1) for v in t]
        down = [pltpu.roll(v, 32, 1) for v in t]
        out = []
        for i in range(tiles):
            cut = slice(i * 128, (i + 1) * 128)
            total = src[row - 1, :, cut] + src[row + 1, :, cut]
            total = total + jnp.where(above, up[i], up[(i + 1) % 3]) + jnp.where(below, down[i], down[(i + 2) % 3])
            total = total + jnp.where(not_first, pltpu.roll(t[i], 1, 1), 0.0)
            total = total + jnp.where(not_last, pltpu.roll(t[i], 127, 1), 0.0)
            lap = total - 6.0 * t[i]
            out.append(t[i] + (rate * k_row[:, cut]) * lap)
        return out

    def first_step(x, carry):
        for i, v in enumerate(step(e0, x + 1, ke[pl.ds(x + 7, 1), :], 3)):
            e1[x, :, i * 128 : (i + 1) * 128] = v
        return carry

    lax.fori_loop(0, NX + 2, first_step, 0)

    fs_hi, fs_lo = split_2(fs_ref[...])
    weights = jnp.concatenate([fs_hi, fs_hi, fs_lo, fs_lo], axis=1)

    low_q, even_q = lane_q < 64, (lane_q & 32) == 0

    def second_step(group, carry):
        rows = []
        for g in range(4):
            x = group * 4 + g
            done = step(e1, x + 1, ke[pl.ds(x + 8, 1), :], 2)
            left[pl.ds(x, NS, stride=NX), :], right[pl.ds(x, NS, stride=NX), :] = done
            v = jnp.concatenate(done, axis=1)
            hi, lo = split_2(v)
            stacked = jnp.concatenate([hi, lo, hi, lo], axis=0)
            rows.append(jnp.dot(weights, stacked, preferred_element_type=f32))
        swapped = []
        for t in range(2):
            v = [r[:, t * 128 : (t + 1) * 128] for r in rows]
            a = [jnp.where(low_q, v[g], pltpu.roll(v[g + 2], 64, 1)) for g in range(2)]
            b = [jnp.where(low_q, pltpu.roll(v[g], 64, 1), v[g + 2]) for g in range(2)]
            for p, r in (a, b):
                swapped.append(jnp.where(even_q, p, pltpu.roll(r, 32, 1)))
                swapped.append(jnp.where(even_q, pltpu.roll(p, 96, 1), r))
        turned = jnp.concatenate(swapped, axis=0).T
        for g in range(4):
            planes_ref[pl.ds(group * 4 + g, NZ, stride=NX), :] = turned[g * NZ : (g + 1) * NZ, :]
        return carry

    lax.fori_loop(0, NX // 4, second_step, 0)
    adv_ref[:, :128] = left[...]
    adv_ref[:, 128:] = right[...]


def advance(c2d, k, rate, fs, faces, whole):
    small = (k, rate, fs, *faces)
    shapes = [(NS * NX, NV), (NZ * NX, 128)]
    return pl.pallas_call(
        advance_kernel,
        grid=(1,),
        out_shape=[jax.ShapeDtypeStruct(s, f32) for s in shapes],
        in_specs=halves(c2d) + [whole_block(v.shape) for v in small] + [pl.BlockSpec(memory_space=pl.ANY)],
        out_specs=[whole_block(s) for s in shapes],
        scratch_shapes=[
            pltpu.VMEM((NX + 4, NS, NV + NH), f32),
            pltpu.VMEM((NX + 2, NS, NV + NH), f32),
            pltpu.VMEM((NX + 16, NV + NH), f32),
            pltpu.VMEM((NS * NX, 128), f32),
            pltpu.VMEM((NS * NX, 128), f32),
        ],
        compiler_params=pltpu.CompilerParams(vmem_limit_bytes=40 * 1024 * 1024),
        name="advance_twice",
    )(c2d, c2d, *small, whole)


def whole_of(block, axis):
    count = lax.axis_size(axis)
    copies = jnp.broadcast_to(block[None], (count,) + block.shape)
    return lax.all_to_all(copies, axis, 0, 0, tiled=True).reshape((-1,) + block.shape[1:])


def shift_to(v, dx, dy):
    n_tx, n_ty = lax.axis_size("tx"), lax.axis_size("ty")
    if dy == 0:
        return lax.ppermute(v, "tx", [(i, i + dx) for i in range(n_tx) if 0 <= i + dx < n_tx])
    if dx == 0:
        return lax.ppermute(v, "ty", [(j, j + dy) for j in range(n_ty) if 0 <= j + dy < n_ty])
    pairs = [
        (i * n_ty + j, (i + dx) * n_ty + j + dy)
        for i in range(n_tx)
        for j in range(n_ty)
        if 0 <= i + dx < n_tx and 0 <= j + dy < n_ty
    ]
    return lax.ppermute(v, ("tx", "ty"), pairs)


def body(species, cell_factor, species_rate, factor_x, factor_y, factor_species):
    nspec, cells_x, merged = species.shape
    cells_y = factor_y.shape[0]
    depth = merged // cells_y
    n_tx, n_ty = lax.axis_size("tx"), lax.axis_size("ty")
    ranks_q = factor_species.shape[1]
    whole_x = whole_of(factor_x, "tx")
    c2d = species.reshape(nspec * cells_x, merged)
    faces = pack(c2d, cell_factor)
    ways = [(-1, 0), (1, 0), (0, -1), (0, 1), (-1, -1), (-1, 1), (1, -1), (1, 1)]
    faces = [shift_to(v, dx, dy) for v, (dx, dy) in zip(faces, ways)]
    advanced, planes = advance(c2d, cell_factor, species_rate[:, None], factor_species.T, faces, whole_x)
    planes = planes.reshape(depth, cells_x, cells_y * ranks_q)
    planes = lax.all_to_all(planes, "tx", 0, 0, tiled=True).reshape(-1, cells_y * ranks_q)
    first = lax.dot_general(planes, whole_x, (((0,), (0,)), ((), ())), precision=exact_mode)
    first = first.reshape(cells_y, ranks_q, -1).transpose(1, 0, 2)
    sent = jnp.concatenate([first, jnp.broadcast_to(factor_y[None], (n_ty,) + factor_y.shape)], axis=1)
    came = lax.all_to_all(sent, "ty", 0, 0, tiled=True)
    first = came[:, :cells_y].reshape(n_ty * cells_y, -1)
    whole_y = came[:, cells_y:].reshape(n_ty * cells_y, -1)
    plane = lax.dot_general(first, whole_y, (((0,), (0,)), ((), ())), precision=exact_mode)
    rank_a, rank_b = plane.shape
    plane = plane.reshape(n_tx, rank_a // n_tx, n_ty, rank_b // n_ty).transpose(0, 2, 1, 3)
    plane = plane.reshape(n_tx * n_ty, 1, -1)
    core = lax.all_to_all(plane, ("tx", "ty"), 0, 0, tiled=True)
    core = core.reshape(depth, ranks_q, rank_a // n_tx, rank_b // n_ty).transpose(2, 1, 3, 0)
    return advanced.reshape(species.shape), core.reshape(rank_a // n_tx, ranks_q, -1)


def solution(mesh):
    in_specs = (P(None, "tx", "ty"), P("tx", "ty"), P(), P("tx", None), P("ty", None), P())
    out_specs = (P(None, "tx", "ty"), P("tx", None, "ty"))
    return jax.shard_map(body, mesh=mesh, in_specs=in_specs, out_specs=out_specs, check_vma=False)
```

time: 247 us -> 154 us (0.62)
  waiting for transfers between devices: 55.8 us -> 10.9 us
  starting transfers between devices: 76.9 us -> 38.7 us
  other arithmetic: 29.8 us -> 0.01 us
  blocking collectives: 54.8 us -> 83.5 us
  local copies, waits for them, and re-layouts: 23.8 us -> 3.88 us
  Pallas kernels: 0 us -> 14.3 us
  matrix products: 3.82 us -> 1.1 us
    all_to_all x2 -> x1, starting transfers between devices: 46.2 us -> 10.6 us  [whole_of(): lax.all_to_all(copies, axis, 0, 0, tiled=True)]
    add x2 -> x0, other arithmetic: 29 us -> none  [body(): field = field + rate_field * laplace(padded)]
    all_to_all x0 -> x1, blocking collectives: none -> 28.5 us  [body(): came = lax.all_to_all(sent, 'ty', 0, 0, tiled=True)]
    all_to_all x2 -> x1, waiting for transfers between devices: 24.3 us -> 0.01 us  [whole_of(): lax.all_to_all(copies, axis, 0, 0, tiled=True)]
    pallas_call x0 -> x2, Pallas kernels: none -> 14.3 us  [the longest x1 11.6 us: advance(): pl.pallas_call(advance_kernel, grid=(1,), out_shape=[jax.ShapeDtypeStruct...]
    ppermute x8, waiting for transfers between devices: 22.7 us -> 10.9 us  [the longest x4 10.9 us: shift_to(): return lax.ppermute(v, ('tx', 'ty'), pairs)]
    reshape x5 -> x1, local copies, waits for them, and re-layouts: 10.3 us -> 0.2 us  [body(): lax.all_to_all(planes, 'tx', 0, 0, tiled=True)]
    all_to_all x1 -> x0, waiting for transfers between devices: 8.78 us -> none  [body(): lax.all_to_all(first, 'ty', 0, 0, tiled=True).reshape(n_ty * cells_y, -1)]
  transfers between devices with their start and end apart: 11 -> 9, of which waited for: 9 -> 4; matrix products, arithmetic and copies ran while one was open for 2% -> 0% of each run, Pallas kernels for 0% -> 2%
where the time goes in v2:
time: 154 us; the launch traced here: 153 us
  blocking collectives  83.5 us (54%)
  starting transfers between devices  38.7 us (25%)
  Pallas kernels  14.3 us (9%)
  waiting for transfers between devices  10.9 us (7%)
  local copies, waits for them, and re-layouts  3.88 us (3%)
    all_to_all x1, blocking collectives, body(): core = lax.all_to_all(plane, ('tx', 'ty'), 0, 0, tiled=True)  29.4 us
    all_to_all x1, blocking collectives, body(): came = lax.all_to_all(sent, 'ty', 0, 0, tiled=True)  28.5 us
    all_to_all x1, blocking collectives, body(): lax.all_to_all(planes, 'tx', 0, 0, tiled=True)  25.5 us
    ppermute x4, starting transfers between devices, shift_to(): return lax.ppermute(v, ('tx', 'ty'), pairs)  16.8 us
    pallas_call x1, Pallas kernels, advance(): pl.pallas_call(advance_kernel, grid=(1,), out_shape=[jax.ShapeDtypeStruct...  11.6 us
    ppermute x4, waiting for transfers between devices, shift_to(): return lax.ppermute(v, ('tx', 'ty'), pairs)  10.9 us
    all_to_all x1, starting transfers between devices, whole_of(): lax.all_to_all(copies, axis, 0, 0, tiled=True)  10.6 us
    ppermute x2, starting transfers between devices, shift_to(): lax.ppermute(v, 'tx', [(i, i + dx) for i in range(n_tx) if 0 <= i + dx <...  6.02 us
  transfers between devices with their start and end apart: 9, of which 4 were waited for; matrix products, arithmetic and copies ran while one was open for 0% of the time, Pallas kernels for 2%

profile of v2, /device:TPU:1, one launch (start us, length us, event | category | flops | bytes accessed | tf_op | source)
XLA Modules:
  0.0 153.2 jit_solution(16243958550032575306)
XLA Ops:
  0.6 1.6 %broadcast_in_dim.7 = f32[32,32,128]{2,1,0:T(8,128)} broadcast(f32[32,128]{1,0:T(8,128)} %param.9), dimensions={1,2} | broadcast | bytes 540672 | tf_op jit(solution)/shard_map/broadcast_in_dim | solution.py:172
  2.2 10.6 %all-to-all-start = ((f32[32,32,128]{2,1,0:T(8,128)}), f32[32,32,128]{2,1,0:T(8,128)S(1)}, u32[]{:S(2)}, u32[]{:S(2)}) async-start(f32[32,32,128]{2,1,0:T(8,128)} %broadcast_in_dim.7), calls=%async_computation | async-start | bytes 1048576 | tf_op jit(solution)/shard_map/all_to_all | solution.py:173
  12.8 2.7 %pack_faces.1 = (f32[72,256]{1,0:T(8,128)}, f32[72,256]{1,0:T(8,128)}, f32[544,128]{1,0:T(8,128)}, f32[544,128]{1,0:T(8,128)}, f32[32,128]{1,0:T(8,128)}, /*inde...) custom-call(f32[1024,256]{1,0:T(8,128)} %bitcast.42, f32[1024,256]{1,0:T(8,128)} %bitcast.43, f32[32,256]{1,0:T(8,128)} %k_ref.3), custom_call_target="tpu_custom_call" | custom-call | tf_op jit(solution)/shard_map/pack_faces/pallas_call | solution.py:48
  15.6 1.3 collective-permute-start.2
  16.9 4.0 %collective-permute-start.3 = (f32[544,128]{1,0:T(8,128)}, f32[544,128]{1,0:T(8,128)S(1)}, u32[]{:S(2)}, u32[]{:S(2)}) collective-permute-start(f32[544,128]{1,0:T(8,128)} %get-tuple-element.15), channel_id=1, source_target_pairs={{0,1},{1,2},{2,3},{3,4},{4,5},{5,6},{6,7},{7,8},{8,9},{9,10},{10,1... | collective-permute-start | bytes 835592 | tf_op jit(solution)/shard_map/ppermute | solution.py:181
  20.9 2.7 %collective-permute-start = (f32[72,256]{1,0:T(8,128)}, f32[72,256]{1,0:T(8,128)S(1)}, u32[]{:S(2)}, u32[]{:S(2)}) collective-permute-start(f32[72,256]{1,0:T(8,128)} %get-tuple-element.12), channel_id=1, source_target_pairs={{16,0},{32,16},{48,32},{64,48},{80,64},{96,80},{112,96},{128,112},... | collective-permute-start | bytes 221192 | tf_op jit(solution)/shard_map/ppermute | solution.py:179
  23.6 3.3 %collective-permute-start.1 = (f32[72,256]{1,0:T(8,128)}, f32[72,256]{1,0:T(8,128)S(1)}, u32[]{:S(2)}, u32[]{:S(2)}) collective-permute-start(f32[72,256]{1,0:T(8,128)} %get-tuple-element.13), channel_id=1, source_target_pairs={{0,16},{16,32},{32,48},{48,64},{64,80},{80,96},{96,112},{112,128},... | collective-permute-start | bytes 221192 | tf_op jit(solution)/shard_map/ppermute | solution.py:179
  26.9 1.3 collective-permute-start.4
  28.2 4.9 %collective-permute-done.4.mm_ref = f32[32,128]{1,0:T(8,128)S(1)} collective-permute-done((f32[32,128]{1,0:T(8,128)}, f32[32,128]{1,0:T(8,128)S(1)}, u32[]{:S(2)}, u32[]{:S(2)}) %collective-permute-start.4) | collective-permute-done | bytes 16416 | tf_op jit(solution)/shard_map/ppermute | solution.py:188
  33.1 1.9 %collective-permute-start.5 = (f32[32,128]{1,0:T(8,128)}, f32[32,128]{1,0:T(8,128)S(1)}, u32[]{:S(2)}, u32[]{:S(2)}) collective-permute-start(f32[32,128]{1,0:T(8,128)} %get-tuple-element.17), channel_id=1, source_target_pairs={{16,1},{17,2},{18,3},{19,4},{20,5},{21,6},{22,7},{23,8},{24,9},{25... | collective-permute-start | bytes 49160 | tf_op jit(solution)/shard_map/ppermute | solution.py:188
  35.0 1.1 collective-permute-done.5.mp_ref
  36.1 1.3 collective-permute-start.6
  37.4 4.0 %collective-permute-done.6.pm_ref = f32[32,128]{1,0:T(8,128)S(1)} collective-permute-done((f32[32,128]{1,0:T(8,128)}, f32[32,128]{1,0:T(8,128)S(1)}, u32[]{:S(2)}, u32[]{:S(2)}) %collective-permute-start.6) | collective-permute-done | bytes 16416 | tf_op jit(solution)/shard_map/ppermute | solution.py:188
  41.4 12.3 %collective-permute-start.7 = (f32[32,128]{1,0:T(8,128)}, f32[32,128]{1,0:T(8,128)S(1)}, u32[]{:S(2)}, u32[]{:S(2)}) collective-permute-start(f32[32,128]{1,0:T(8,128)} %get-tuple-element.19), channel_id=1, source_target_pairs={{0,17},{1,18},{2,19},{3,20},{4,21},{5,22},{6,23},{7,24},{8,25},{9,... | collective-permute-start | bytes 49160 | tf_op jit(solution)/shard_map/ppermute | solution.py:188
  53.8 1.0 collective-permute-done.7.pp_ref
  54.8 11.6 %advance_twice.1 = (f32[1024,256]{1,0:T(8,128)}, f32[1024,128]{1,0:T(8,128)S(1)}) custom-call(f32[1024,256]{1,0:T(8,128)S(1)} %bitcast.44, f32[1024,256]{1,0:T(8,128)S(1)} %bitcast.45, f32[32,256]{1,0:T(8,128)S(1)} %copy-done.1, f32[32,1]{1,0:T(8,128)S(1)} %copy.20.rate_ref, f32[16,32]{1,0:T(8,128)S(1)} %bitcast.49, ...), custom_call_target="tpu_custom_call" | custom-call | tf_op jit(solution)/shard_map/advance_twice/pallas_call | solution.py:152
  66.4 25.5 %all_to_all.20 = f32[32,32,128]{2,1,0:T(8,128)S(1)} all-to-all(f32[32,32,128]{2,1,0:T(8,128)S(1)} %bitcast.48), channel_id=1, replica_groups=mesh['tx'=32,'ty'=16] {'tx'}, dimensions={0} | all-to-all | bytes 1048576 | tf_op jit(solution)/shard_map/all_to_all | solution.py:204
  92.1 0.6 convolution_bitcast_fusion.1
  92.8 28.5 %all_to_all.21 = f32[16,16,128]{2,1,0:T(8,128)S(1)} all-to-all(f32[16,16,128]{2,1,0:T(8,128)S(1)} %copy.22), channel_id=1, replica_groups=mesh['tx'=32,'ty'=16] {'ty'}, dimensions={0} | all-to-all | bytes 262144 | tf_op jit(solution)/shard_map/all_to_all | solution.py:208
  121.6 0.5 convolution_bitcast_fusion
  122.0 0.2 copy.27
  122.3 0.3 reshape.48
  122.7 29.4 %all_to_all.22 = f32[512,1,32]{2,1,0:T(1,128)S(1)} all-to-all(f32[512,1,32]{2,1,0:T(1,128)S(1)} %copy.28), channel_id=1, replica_groups=mesh['tx'=32,'ty'=16] {'tx','ty'}, dimensions={0} | all-to-all | bytes 131072 | tf_op jit(solution)/shard_map/all_to_all | solution.py:215
  152.4 0.8 copy.30
  (26 shorter events, 1.0 us)
Async XLA Ops:
  2.2 52.6 %all-to-all-start = ((f32[32,32,128]{2,1,0:T(8,128)}), f32[32,32,128]{2,1,0:T(8,128)S(1)}, u32[]{:S(2)}, u32[]{:S(2)}) async-start(f32[32,32,128]{2,1,0:T(8,128)} %broadcast_in_dim.7), calls=%async_computation | async-start | bytes 1048576 | tf_op jit(solution)/shard_map/all_to_all | solution.py:173
  12.8 40.9 %copy-start.4 = (f32[32]{0:T(128)S(1)}, f32[32]{0:T(128)}, u32[]{:S(2)}) copy-start(f32[32]{0:T(128)} %param.8) | copy-start | bytes 388
  12.8 42.0 %copy-start = (f32[32,32,256]{2,1,0:T(8,128)S(1)}, f32[32,32,256]{2,1,0:T(8,128)}, u32[]{:S(2)}) copy-start(f32[32,32,256]{2,1,0:T(8,128)} %param.6) | copy-start | bytes 3145732
  12.8 42.0 %copy-start.2 = (f32[32,16]{0,1:T(8,128)S(1)}, f32[32,16]{0,1:T(8,128)}, u32[]{:S(2)}) copy-start(f32[32,16]{0,1:T(8,128)} %param.11) | copy-start | bytes 6148
  15.6 39.2 %copy-start.1 = (f32[32,256]{1,0:T(8,128)S(1)}, f32[32,256]{1,0:T(8,128)}, u32[]{:S(2)}) copy-start(f32[32,256]{1,0:T(8,128)} %k_ref.3) | copy-start | bytes 98308
  15.6 39.2 %collective-permute-start.2 = (f32[544,128]{1,0:T(8,128)}, f32[544,128]{1,0:T(8,128)S(1)}, u32[]{:S(2)}, u32[]{:S(2)}) collective-permute-start(f32[544,128]{1,0:T(8,128)} %get-tuple-element.14), channel_id=1, source_target_pairs={{1,0},{2,1},{3,2},{4,3},{5,4},{6,5},{7,6},{8,7},{9,8},{10,9},{11,1... | collective-permute-start | bytes 835592 | tf_op jit(solution)/shard_map/ppermute | solution.py:181
  16.9 37.9 %collective-permute-start.3 = (f32[544,128]{1,0:T(8,128)}, f32[544,128]{1,0:T(8,128)S(1)}, u32[]{:S(2)}, u32[]{:S(2)}) collective-permute-start(f32[544,128]{1,0:T(8,128)} %get-tuple-element.15), channel_id=1, source_target_pairs={{0,1},{1,2},{2,3},{3,4},{4,5},{5,6},{6,7},{7,8},{8,9},{9,10},{10,1... | collective-permute-start | bytes 835592 | tf_op jit(solution)/shard_map/ppermute | solution.py:181
  20.9 33.9 %collective-permute-start = (f32[72,256]{1,0:T(8,128)}, f32[72,256]{1,0:T(8,128)S(1)}, u32[]{:S(2)}, u32[]{:S(2)}) collective-permute-start(f32[72,256]{1,0:T(8,128)} %get-tuple-element.12), channel_id=1, source_target_pairs={{16,0},{32,16},{48,32},{64,48},{80,64},{96,80},{112,96},{128,112},... | collective-permute-start | bytes 221192 | tf_op jit(solution)/shard_map/ppermute | solution.py:179
  23.6 31.1 %collective-permute-start.1 = (f32[72,256]{1,0:T(8,128)}, f32[72,256]{1,0:T(8,128)S(1)}, u32[]{:S(2)}, u32[]{:S(2)}) collective-permute-start(f32[72,256]{1,0:T(8,128)} %get-tuple-element.13), channel_id=1, source_target_pairs={{0,16},{16,32},{32,48},{48,64},{64,80},{80,96},{96,112},{112,128},... | collective-permute-start | bytes 221192 | tf_op jit(solution)/shard_map/ppermute | solution.py:179
  26.9 6.2 %collective-permute-start.4 = (f32[32,128]{1,0:T(8,128)}, f32[32,128]{1,0:T(8,128)S(1)}, u32[]{:S(2)}, u32[]{:S(2)}) collective-permute-start(f32[32,128]{1,0:T(8,128)} %get-tuple-element.16), channel_id=1, source_target_pairs={{17,0},{18,1},{19,2},{20,3},{21,4},{22,5},{23,6},{24,7},{25,8},{26... | collective-permute-start | bytes 49160 | tf_op jit(solution)/shard_map/ppermute | solution.py:188
  33.1 3.0 %collective-permute-start.5 = (f32[32,128]{1,0:T(8,128)}, f32[32,128]{1,0:T(8,128)S(1)}, u32[]{:S(2)}, u32[]{:S(2)}) collective-permute-start(f32[32,128]{1,0:T(8,128)} %get-tuple-element.17), channel_id=1, source_target_pairs={{16,1},{17,2},{18,3},{19,4},{20,5},{21,6},{22,7},{23,8},{24,9},{25... | collective-permute-start | bytes 49160 | tf_op jit(solution)/shard_map/ppermute | solution.py:188
  36.1 5.3 %collective-permute-start.6 = (f32[32,128]{1,0:T(8,128)}, f32[32,128]{1,0:T(8,128)S(1)}, u32[]{:S(2)}, u32[]{:S(2)}) collective-permute-start(f32[32,128]{1,0:T(8,128)} %get-tuple-element.18), channel_id=1, source_target_pairs={{1,16},{2,17},{3,18},{4,19},{5,20},{6,21},{7,22},{8,23},{9,24},{10... | collective-permute-start | bytes 49160 | tf_op jit(solution)/shard_map/ppermute | solution.py:188
  41.4 13.4 %collective-permute-start.7 = (f32[32,128]{1,0:T(8,128)}, f32[32,128]{1,0:T(8,128)S(1)}, u32[]{:S(2)}, u32[]{:S(2)}) collective-permute-start(f32[32,128]{1,0:T(8,128)} %get-tuple-element.19), channel_id=1, source_target_pairs={{0,17},{1,18},{2,19},{3,20},{4,21},{5,22},{6,23},{7,24},{8,25},{9,... | collective-permute-start | bytes 49160 | tf_op jit(solution)/shard_map/ppermute | solution.py:188
  92.1 0.7 copy-start.3

commit v3 on v2

--- a/solution.py
+++ b/solution.py
@@ -14,7 +14,7 @@
     return lax.broadcasted_iota(jnp.int32, (rows, 128), 1)
 
 
-def pack_kernel(c0_ref, c1_ref, k_ref, xl_ref, xh_ref, yl_ref, yh_ref, mm_ref, mp_ref, pm_ref, pp_ref):
+def pack_kernel(c0_ref, c1_ref, k_ref, fx_ref, xl_ref, xh_ref, yl_ref, yh_ref, copies_ref):
     low = lanes(NS // 2) < 64
 
     def row(x):
@@ -24,8 +24,6 @@
         ref[at : at + NS, :128], ref[at : at + NS, 128:] = row(x)
     xl_ref[2 * NS :, :] = jnp.broadcast_to(k_ref[0:1, :], (8, NV))
     xh_ref[2 * NS :, :] = jnp.broadcast_to(k_ref[NX - 1 : NX, :], (8, NV))
-    mm_ref[...], mp_ref[...] = row(0)
-    pm_ref[...], pp_ref[...] = row(NX - 1)
     half = NS // 2
     for x in range(NX):
         t0, t1 = row(x)
@@ -33,26 +31,45 @@
         yh_ref[x * half : (x + 1) * half, :] = jnp.where(low, pltpu.roll(t1[half:], 64, 1), t1[:half])
     yl_ref[NX * half :, :] = k_ref[:, :128]
     yh_ref[NX * half :, :] = k_ref[:, 128:]
+    copies_ref[...] = jnp.broadcast_to(fx_ref[...][None], copies_ref.shape)
 
 
 def whole_block(shape):
-    return pl.BlockSpec(shape, lambda i: (0, 0))
+    return pl.BlockSpec(shape, lambda i: (0,) * len(shape))
 
 
 def halves(v):
     return [pl.BlockSpec((v.shape[0], 128), lambda i, side=side: (0, side)) for side in range(2)]
 
 
-def pack(c2d, k):
-    shapes = [(2 * NS + 8, NV)] * 2 + [(NX * NS // 2 + NX, 128)] * 2 + [(NS, 128)] * 4
+def pack(c2d, k, factor_x, copies):
+    shapes = [(2 * NS + 8, NV)] * 2 + [(NX * NS // 2 + NX, 128)] * 2 + [(copies,) + factor_x.shape]
     return pl.pallas_call(
         pack_kernel,
         grid=(1,),
         out_shape=[jax.ShapeDtypeStruct(s, f32) for s in shapes],
-        in_specs=halves(c2d) + [whole_block(k.shape)],
+        in_specs=halves(c2d) + [whole_block(k.shape), whole_block(factor_x.shape)],
         out_specs=[whole_block(s) for s in shapes],
         name="pack_faces",
-    )(c2d, c2d, k)
+    )(c2d, c2d, k, factor_x)
+
+
+def corner_kernel(xl_ref, xh_ref, lo_ref, hi_ref):
+    for at, ref in ((0, xh_ref), (NS, xl_ref)):
+        lo_ref[at : at + NS, :] = ref[0:NS, :128]
+        hi_ref[at : at + NS, :] = ref[0:NS, 128:]
+
+
+def corners(xl, xh):
+    shape = (2 * NS, 128)
+    return pl.pallas_call(
+        corner_kernel,
+        grid=(1,),
+        out_shape=[jax.ShapeDtypeStruct(shape, f32)] * 2,
+        in_specs=[whole_block(xl.shape)] * 2,
+        out_specs=[whole_block(shape)] * 2,
+        name="corner_columns",
+    )(xl, xh)
 
 
 def split_2(v):
@@ -60,7 +77,7 @@
     return hi, (v - hi.astype(f32)).astype(bf16)
 
 
-def advance_kernel(c0_ref, c1_ref, k_ref, rate_ref, fs_ref, xl_ref, xh_ref, yl_ref, yh_ref, mm_ref, mp_ref, pm_ref, pp_ref, whole_ref,
+def advance_kernel(c0_ref, c1_ref, k_ref, rate_ref, fs_ref, xl_ref, xh_ref, yl_ref, yh_ref, cl_ref, ch_ref, whole_ref,
                    adv_ref, planes_ref, e0, e1, ke, left, right):
     half = NS // 2
     lane_s, lane_h, lane_q = lanes(NS), lanes(half), lanes(NQ)
@@ -71,9 +88,9 @@
     low_s, low_h = lane_s < 64, lane_h < 64
     e0[0, :, :NV] = xh_ref[NS : 2 * NS, :]
     e0[1, :, :NV] = xh_ref[0:NS, :]
-    e0[1, :, NV:] = jnp.where(low_s, pm_ref[...], pp_ref[...])
+    e0[1, :, NV:] = jnp.where(low_s, cl_ref[:NS, :], ch_ref[:NS, :])
     e0[NX + 2, :, :NV] = xl_ref[0:NS, :]
-    e0[NX + 2, :, NV:] = jnp.where(low_s, mm_ref[...], mp_ref[...])
+    e0[NX + 2, :, NV:] = jnp.where(low_s, cl_ref[NS:, :], ch_ref[NS:, :])
     e0[NX + 3, :, :NV] = xl_ref[NS : 2 * NS, :]
     e0[0, :, NV:] = jnp.zeros((NS, NH), f32)
     e0[NX + 3, :, NV:] = jnp.zeros((NS, NH), f32)
@@ -167,25 +184,10 @@
     )(c2d, c2d, *small, whole)
 
 
-def whole_of(block, axis):
+def shift_to(v, dx, dy):
+    axis, step = ("tx", dx) if dx else ("ty", dy)
     count = lax.axis_size(axis)
-    copies = jnp.broadcast_to(block[None], (count,) + block.shape)
-    return lax.all_to_all(copies, axis, 0, 0, tiled=True).reshape((-1,) + block.shape[1:])
-
-
-def shift_to(v, dx, dy):
-    n_tx, n_ty = lax.axis_size("tx"), lax.axis_size("ty")
-    if dy == 0:
-        return lax.ppermute(v, "tx", [(i, i + dx) for i in range(n_tx) if 0 <= i + dx < n_tx])
-    if dx == 0:
-        return lax.ppermute(v, "ty", [(j, j + dy) for j in range(n_ty) if 0 <= j + dy < n_ty])
-    pairs = [
-        (i * n_ty + j, (i + dx) * n_ty + j + dy)
-        for i in range(n_tx)
-        for j in range(n_ty)
-        if 0 <= i + dx < n_tx and 0 <= j + dy < n_ty
-    ]
-    return lax.ppermute(v, ("tx", "ty"), pairs)
+    return lax.ppermute(v, axis, [(i, i + step) for i in range(count) if 0 <= i + step < count])
 
 
 def body(species, cell_factor, species_rate, factor_x, factor_y, factor_species):
@@ -194,11 +196,12 @@
     depth = merged // cells_y
     n_tx, n_ty = lax.axis_size("tx"), lax.axis_size("ty")
     ranks_q = factor_species.shape[1]
-    whole_x = whole_of(factor_x, "tx")
     c2d = species.reshape(nspec * cells_x, merged)
-    faces = pack(c2d, cell_factor)
-    ways = [(-1, 0), (1, 0), (0, -1), (0, 1), (-1, -1), (-1, 1), (1, -1), (1, 1)]
-    faces = [shift_to(v, dx, dy) for v, (dx, dy) in zip(faces, ways)]
+    *faces, copies = pack(c2d, cell_factor, factor_x, n_tx)
+    xl, xh, yl, yh = (shift_to(v, dx, dy) for v, (dx, dy) in zip(faces, [(-1, 0), (1, 0), (0, -1), (0, 1)]))
+    lo, hi = corners(xl, xh)
+    faces = xl, xh, yl, yh, shift_to(lo, 0, -1), shift_to(hi, 0, 1)
+    whole_x = lax.all_to_all(copies, "tx", 0, 0, tiled=True).reshape(-1, factor_x.shape[1])
     advanced, planes = advance(c2d, cell_factor, species_rate[:, None], factor_species.T, faces, whole_x)
     planes = planes.reshape(depth, cells_x, cells_y * ranks_q)
     planes = lax.all_to_all(planes, "tx", 0, 0, tiled=True).reshape(-1, cells_y * ranks_q)

time: 154 us -> 140 us (0.909)
  starting transfers between devices: 38.7 us -> 27.3 us
  waiting for transfers between devices: 10.9 us -> 4.62 us
  Pallas kernels: 14.3 us -> 15.9 us
    ppermute x8 -> x6, starting transfers between devices: 28.1 us -> 16.6 us  [shift_to(): lax.ppermute(v, axis, [(i, i + step) for i in range(count) if 0 <= i + st...]
    ppermute x8 -> x6, waiting for transfers between devices: 10.9 us -> 4.62 us  [shift_to(): lax.ppermute(v, axis, [(i, i + step) for i in range(count) if 0 <= i + st...]
    unnamed x11 -> x19, local copies, waits for them, and re-layouts: 0.86 us -> 3.87 us
    broadcast_in_dim x1 -> x0, local copies, waits for them, and re-layouts: 1.57 us -> none  [whole_of(): copies = jnp.broadcast_to(block[None], (count,) + block.shape)]
    pallas_call x0 -> x1, Pallas kernels: none -> 1.56 us  [corners(): pl.pallas_call(corner_kernel, grid=(1,), out_shape=[jax.ShapeDtypeStruct(...]
  transfers between devices with their start and end apart: 9 -> 7, of which waited for: 4 -> 2; matrix products, arithmetic and copies ran while one was open for 0% -> 0% of each run, Pallas kernels for 2% -> 1%
where the time goes in v3:
time: 140 us; the launch traced here: 139 us
  blocking collectives  83.8 us (60%)
  starting transfers between devices  27.3 us (20%)
  Pallas kernels  15.9 us (11%)
  local copies, waits for them, and re-layouts  5.32 us (4%)
  waiting for transfers between devices  4.62 us (3%)
    all_to_all x1, blocking collectives, body(): core = lax.all_to_all(plane, ('tx', 'ty'), 0, 0, tiled=True)  29.4 us
    all_to_all x1, blocking collectives, body(): came = lax.all_to_all(sent, 'ty', 0, 0, tiled=True)  29 us
    all_to_all x1, blocking collectives, body(): lax.all_to_all(planes, 'tx', 0, 0, tiled=True)  25.3 us
    ppermute x6, starting transfers between devices, shift_to(): lax.ppermute(v, axis, [(i, i + step) for i in range(count) if 0 <= i + st...  16.6 us
    pallas_call x1, Pallas kernels, advance(): pl.pallas_call(advance_kernel, grid=(1,), out_shape=[jax.ShapeDtypeStruct...  11.6 us
    all_to_all x1, starting transfers between devices, body(): lax.all_to_all(copies, 'tx', 0, 0, tiled=True)  10.7 us
    ppermute x6, waiting for transfers between devices, shift_to(): lax.ppermute(v, axis, [(i, i + step) for i in range(count) if 0 <= i + st...  4.62 us
    unnamed x19, local copies, waits for them, and re-layouts  3.87 us
  transfers between devices with their start and end apart: 7, of which 2 were waited for; matrix products, arithmetic and copies ran while one was open for 0% of the time, Pallas kernels for 1%

profile of v3, /device:TPU:1, one launch (start us, length us, event | category | flops | bytes accessed | tf_op | source)
XLA Modules:
  0.0 138.9 jit_solution(1714753350644128490)
XLA Ops:
  0.6 2.8 %pack_faces.1 = (f32[72,256]{1,0:T(8,128)}, f32[72,256]{1,0:T(8,128)}, f32[544,128]{1,0:T(8,128)}, f32[544,128]{1,0:T(8,128)}, f32[32,32,128]{2,1,0:T(8,128)}) custom-call(f32[1024,256]{1,0:T(8,128)} %bitcast.42, f32[1024,256]{1,0:T(8,128)} %bitcast.43, f32[32,256]{1,0:T(8,128)} %k_ref.3, f32[32,128]{1,0:T(8,128)} %fx_ref.1), custom_call_target="tpu_custom_call" | custom-call | tf_op jit(solution)/shard_map/pack_faces/pallas_call | solution.py:47
  3.4 10.7 %all-to-all-start = ((f32[32,32,128]{2,1,0:T(8,128)}), f32[32,32,128]{2,1,0:T(8,128)S(1)}, u32[]{:S(2)}, u32[]{:S(2)}) async-start(f32[32,32,128]{2,1,0:T(8,128)} %get-tuple-element.17), calls=%async_computation | async-start | bytes 1048576 | tf_op jit(solution)/shard_map/all_to_all | solution.py:204
  14.2 1.3 collective-permute-start.2
  15.5 4.0 %collective-permute-start.3 = (f32[544,128]{1,0:T(8,128)}, f32[544,128]{1,0:T(8,128)S(1)}, u32[]{:S(2)}, u32[]{:S(2)}) collective-permute-start(f32[544,128]{1,0:T(8,128)} %get-tuple-element.14), channel_id=1, source_target_pairs={{0,1},{1,2},{2,3},{3,4},{4,5},{5,6},{6,7},{7,8},{8,9},{9,10},{10,1... | collective-permute-start | bytes 835592 | tf_op jit(solution)/shard_map/ppermute | solution.py:190
  19.5 2.7 %collective-permute-start = (f32[72,256]{1,0:T(8,128)}, f32[72,256]{1,0:T(8,128)S(1)}, u32[]{:S(2)}, u32[]{:S(2)}) collective-permute-start(f32[72,256]{1,0:T(8,128)} %get-tuple-element.11), channel_id=1, source_target_pairs={{16,0},{32,16},{48,32},{64,48},{80,64},{96,80},{112,96},{128,112},... | collective-permute-start | bytes 221192 | tf_op jit(solution)/shard_map/ppermute | solution.py:190
  22.2 3.3 %collective-permute-start.1 = (f32[72,256]{1,0:T(8,128)}, f32[72,256]{1,0:T(8,128)S(1)}, u32[]{:S(2)}, u32[]{:S(2)}) collective-permute-start(f32[72,256]{1,0:T(8,128)} %get-tuple-element.12), channel_id=1, source_target_pairs={{0,16},{16,32},{32,48},{48,64},{64,80},{80,96},{96,112},{112,128},... | collective-permute-start | bytes 221192 | tf_op jit(solution)/shard_map/ppermute | solution.py:190
  25.5 3.4 %collective-permute-done.xl_ref = f32[72,256]{1,0:T(8,128)S(1)} collective-permute-done((f32[72,256]{1,0:T(8,128)}, f32[72,256]{1,0:T(8,128)S(1)}, u32[]{:S(2)}, u32[]{:S(2)}) %collective-permute-start) | collective-permute-done | bytes 73760 | tf_op jit(solution)/shard_map/ppermute | solution.py:190
  28.9 0.6 copy-done.1
  29.5 0.6 copy-done.3
  30.2 1.6 %corner_columns.1 = (f32[64,128]{1,0:T(8,128)}, f32[64,128]{1,0:T(8,128)}) custom-call(f32[72,256]{1,0:T(8,128)} %copy-done.1, f32[72,256]{1,0:T(8,128)} %copy-done.3), custom_call_target="tpu_custom_call" | custom-call | tf_op jit(solution)/shard_map/corner_columns/pallas_call | solution.py:65
  31.7 1.3 collective-permute-start.4
  33.0 4.0 %collective-permute-start.5 = (f32[64,128]{1,0:T(8,128)}, f32[64,128]{1,0:T(8,128)S(1)}, u32[]{:S(2)}, u32[]{:S(2)}) collective-permute-start(f32[64,128]{1,0:T(8,128)} %get-tuple-element.16), channel_id=1, source_target_pairs={{0,1},{1,2},{2,3},{3,4},{4,5},{5,6},{6,7},{7,8},{8,9},{9,10},{10,1... | collective-permute-start | bytes 98312 | tf_op jit(solution)/shard_map/ppermute | solution.py:190
  37.1 1.2 collective-permute-done.5.ch_ref
  38.4 0.9 copy-done.2
  39.3 0.9 copy-done.4
  40.1 11.6 %advance_twice.1 = (f32[1024,256]{1,0:T(8,128)}, f32[1024,128]{1,0:T(8,128)S(1)}) custom-call(f32[1024,256]{1,0:T(8,128)S(1)} %bitcast.44, f32[1024,256]{1,0:T(8,128)S(1)} %bitcast.45, f32[32,256]{1,0:T(8,128)S(1)} %copy-done.5, f32[32,1]{1,0:T(8,128)S(1)} %copy.20.rate_ref, f32[16,32]{1,0:T(8,128)S(1)} %bitcast.49, f32[72,256]{1,0:T(8,128)S(1)} %copy-done.2, ...), custom_call_target="tpu_custom_call" | custom-call | tf_op jit(solution)/shard_map/advance_twice/pallas_call | solution.py:169
  51.7 25.3 %all_to_all.20 = f32[32,32,128]{2,1,0:T(8,128)S(1)} all-to-all(f32[32,32,128]{2,1,0:T(8,128)S(1)} %bitcast.48), channel_id=1, replica_groups=mesh['tx'=32,'ty'=16] {'tx'}, dimensions={0} | all-to-all | bytes 1048576 | tf_op jit(solution)/shard_map/all_to_all | solution.py:207
  77.3 0.6 convolution_bitcast_fusion.1
  78.0 29.0 %all_to_all.21 = f32[16,16,128]{2,1,0:T(8,128)S(1)} all-to-all(f32[16,16,128]{2,1,0:T(8,128)S(1)} %copy.22), channel_id=1, replica_groups=mesh['tx'=32,'ty'=16] {'ty'}, dimensions={0} | all-to-all | bytes 262144 | tf_op jit(solution)/shard_map/all_to_all | solution.py:211
  107.2 0.5 convolution_bitcast_fusion
  107.7 0.2 copy.27
  107.9 0.3 reshape.47
  108.3 29.4 %all_to_all.22 = f32[512,1,32]{2,1,0:T(1,128)S(1)} all-to-all(f32[512,1,32]{2,1,0:T(1,128)S(1)} %copy.28), channel_id=1, replica_groups=mesh['tx'=32,'ty'=16] {'tx','ty'}, dimensions={0} | all-to-all | bytes 131072 | tf_op jit(solution)/shard_map/all_to_all | solution.py:218
  138.1 0.8 copy.30
  (30 shorter events, 1.1 us)
Async XLA Ops:
  3.4 34.9 %copy-start = (f32[32,32,256]{2,1,0:T(8,128)S(1)}, f32[32,32,256]{2,1,0:T(8,128)}, u32[]{:S(2)}) copy-start(f32[32,32,256]{2,1,0:T(8,128)} %param.6) | copy-start | bytes 3145732
  3.4 34.9 %all-to-all-start = ((f32[32,32,128]{2,1,0:T(8,128)}), f32[32,32,128]{2,1,0:T(8,128)S(1)}, u32[]{:S(2)}, u32[]{:S(2)}) async-start(f32[32,32,128]{2,1,0:T(8,128)} %get-tuple-element.17), calls=%async_computation | async-start | bytes 1048576 | tf_op jit(solution)/shard_map/all_to_all | solution.py:204
  14.2 24.2 %collective-permute-start.2 = (f32[544,128]{1,0:T(8,128)}, f32[544,128]{1,0:T(8,128)S(1)}, u32[]{:S(2)}, u32[]{:S(2)}) collective-permute-start(f32[544,128]{1,0:T(8,128)} %get-tuple-element.13), channel_id=1, source_target_pairs={{1,0},{2,1},{3,2},{4,3},{5,4},{6,5},{7,6},{8,7},{9,8},{10,9},{11,1... | collective-permute-start | bytes 835592 | tf_op jit(solution)/shard_map/ppermute | solution.py:190
  15.5 22.9 %collective-permute-start.3 = (f32[544,128]{1,0:T(8,128)}, f32[544,128]{1,0:T(8,128)S(1)}, u32[]{:S(2)}, u32[]{:S(2)}) collective-permute-start(f32[544,128]{1,0:T(8,128)} %get-tuple-element.14), channel_id=1, source_target_pairs={{0,1},{1,2},{2,3},{3,4},{4,5},{5,6},{6,7},{7,8},{8,9},{9,10},{10,1... | collective-permute-start | bytes 835592 | tf_op jit(solution)/shard_map/ppermute | solution.py:190
  19.5 9.4 %collective-permute-start = (f32[72,256]{1,0:T(8,128)}, f32[72,256]{1,0:T(8,128)S(1)}, u32[]{:S(2)}, u32[]{:S(2)}) collective-permute-start(f32[72,256]{1,0:T(8,128)} %get-tuple-element.11), channel_id=1, source_target_pairs={{16,0},{32,16},{48,32},{64,48},{80,64},{96,80},{112,96},{128,112},... | collective-permute-start | bytes 221192 | tf_op jit(solution)/shard_map/ppermute | solution.py:190
  22.2 6.7 %collective-permute-start.1 = (f32[72,256]{1,0:T(8,128)}, f32[72,256]{1,0:T(8,128)S(1)}, u32[]{:S(2)}, u32[]{:S(2)}) collective-permute-start(f32[72,256]{1,0:T(8,128)} %get-tuple-element.12), channel_id=1, source_target_pairs={{0,16},{16,32},{32,48},{48,64},{64,80},{80,96},{96,112},{112,128},... | collective-permute-start | bytes 221192 | tf_op jit(solution)/shard_map/ppermute | solution.py:190
  28.9 0.6 copy-start.1
  29.5 0.6 copy-start.3
  30.2 8.2 %copy-start.5 = (f32[32,256]{1,0:T(8,128)S(1)}, f32[32,256]{1,0:T(8,128)}, u32[]{:S(2)}) copy-start(f32[32,256]{1,0:T(8,128)} %k_ref.3) | copy-start | bytes 98308
  31.7 5.4 %collective-permute-start.4 = (f32[64,128]{1,0:T(8,128)}, f32[64,128]{1,0:T(8,128)S(1)}, u32[]{:S(2)}, u32[]{:S(2)}) collective-permute-start(f32[64,128]{1,0:T(8,128)} %get-tuple-element.15), channel_id=1, source_target_pairs={{1,0},{2,1},{3,2},{4,3},{5,4},{6,5},{7,6},{8,7},{9,8},{10,9},{11,1... | collective-permute-start | bytes 98312 | tf_op jit(solution)/shard_map/ppermute | solution.py:190
  33.0 4.0 %copy-start.8 = (f32[32]{0:T(128)S(1)}, f32[32]{0:T(128)}, u32[]{:S(2)}) copy-start(f32[32]{0:T(128)} %param.8) | copy-start | bytes 388
  33.0 5.3 %collective-permute-start.5 = (f32[64,128]{1,0:T(8,128)}, f32[64,128]{1,0:T(8,128)S(1)}, u32[]{:S(2)}, u32[]{:S(2)}) collective-permute-start(f32[64,128]{1,0:T(8,128)} %get-tuple-element.16), channel_id=1, source_target_pairs={{0,1},{1,2},{2,3},{3,4},{4,5},{5,6},{6,7},{7,8},{8,9},{9,10},{10,1... | collective-permute-start | bytes 98312 | tf_op jit(solution)/shard_map/ppermute | solution.py:190
  37.0 1.3 copy-start.6
  38.4 0.9 copy-start.2
  39.3 0.9 copy-start.4
  77.2 0.7 copy-start.7

commit v4 on v3

--- a/solution.py
+++ b/solution.py
@@ -7,6 +7,7 @@
 
 exact_mode = lax.Precision.HIGHEST
 f32, bf16 = jnp.float32, jnp.bfloat16
+U1, U2, U3 = 2, 8, 8
 NS, NX, NV, NH, NZ, NQ = 32, 32, 256, 128, 32, 16
 
 
@@ -14,7 +15,7 @@
     return lax.broadcasted_iota(jnp.int32, (rows, 128), 1)
 
 
-def pack_kernel(c0_ref, c1_ref, k_ref, fx_ref, xl_ref, xh_ref, yl_ref, yh_ref, copies_ref):
+def pack_kernel(c0_ref, c1_ref, k_ref, xl_ref, xh_ref, yl_ref, yh_ref):
     low = lanes(NS // 2) < 64
 
     def row(x):
@@ -31,7 +32,6 @@
         yh_ref[x * half : (x + 1) * half, :] = jnp.where(low, pltpu.roll(t1[half:], 64, 1), t1[:half])
     yl_ref[NX * half :, :] = k_ref[:, :128]
     yh_ref[NX * half :, :] = k_ref[:, 128:]
-    copies_ref[...] = jnp.broadcast_to(fx_ref[...][None], copies_ref.shape)
 
 
 def whole_block(shape):
@@ -42,34 +42,35 @@
     return [pl.BlockSpec((v.shape[0], 128), lambda i, side=side: (0, side)) for side in range(2)]
 
 
-def pack(c2d, k, factor_x, copies):
-    shapes = [(2 * NS + 8, NV)] * 2 + [(NX * NS // 2 + NX, 128)] * 2 + [(copies,) + factor_x.shape]
+def pack(c2d, k):
+    shapes = [(2 * NS + 8, NV)] * 2 + [(NX * NS // 2 + NX, 128)] * 2
     return pl.pallas_call(
         pack_kernel,
         grid=(1,),
         out_shape=[jax.ShapeDtypeStruct(s, f32) for s in shapes],
-        in_specs=halves(c2d) + [whole_block(k.shape), whole_block(factor_x.shape)],
+        in_specs=halves(c2d) + [whole_block(k.shape)],
         out_specs=[whole_block(s) for s in shapes],
         name="pack_faces",
-    )(c2d, c2d, k, factor_x)
-
-
-def corner_kernel(xl_ref, xh_ref, lo_ref, hi_ref):
+    )(c2d, c2d, k)
+
+
+def corner_kernel(xl_ref, xh_ref, fx_ref, lo_ref, hi_ref, copies_ref):
     for at, ref in ((0, xh_ref), (NS, xl_ref)):
         lo_ref[at : at + NS, :] = ref[0:NS, :128]
         hi_ref[at : at + NS, :] = ref[0:NS, 128:]
-
-
-def corners(xl, xh):
-    shape = (2 * NS, 128)
+    copies_ref[...] = jnp.broadcast_to(fx_ref[...][None], copies_ref.shape)
+
+
+def corners(xl, xh, factor_x, copies):
+    shapes = [(2 * NS, 128)] * 2 + [(copies,) + factor_x.shape]
     return pl.pallas_call(
         corner_kernel,
         grid=(1,),
-        out_shape=[jax.ShapeDtypeStruct(shape, f32)] * 2,
-        in_specs=[whole_block(xl.shape)] * 2,
-        out_specs=[whole_block(shape)] * 2,
+        out_shape=[jax.ShapeDtypeStruct(s, f32) for s in shapes],
+        in_specs=[whole_block(v.shape) for v in (xl, xh, factor_x)],
+        out_specs=[whole_block(s) for s in shapes],
         name="corner_columns",
-    )(xl, xh)
+    )(xl, xh, factor_x)
 
 
 def split_2(v):
@@ -77,10 +78,9 @@
     return hi, (v - hi.astype(f32)).astype(bf16)
 
 
-def advance_kernel(c0_ref, c1_ref, k_ref, rate_ref, fs_ref, xl_ref, xh_ref, yl_ref, yh_ref, cl_ref, ch_ref, whole_ref,
-                   adv_ref, planes_ref, e0, e1, ke, left, right):
+def advance_kernel(c0_ref, c1_ref, k_ref, rate_ref, xl_ref, xh_ref, yl_ref, yh_ref, cl_ref, ch_ref, adv_ref, e0, e1, ke, left, right):
     half = NS // 2
-    lane_s, lane_h, lane_q = lanes(NS), lanes(half), lanes(NQ)
+    lane_s, lane_h = lanes(NS), lanes(half)
     z = lane_s % NZ
     not_first, not_last = z > 0, z < NZ - 1
     below, above = lane_s >= 32, lane_s < 96
@@ -128,21 +128,50 @@
             e1[x, :, i * 128 : (i + 1) * 128] = v
         return carry
 
-    lax.fori_loop(0, NX + 2, first_step, 0)
-
+    lax.fori_loop(0, NX + 2, first_step, 0, unroll=U1)
+
+    def second_step(x, carry):
+        done = step(e1, x + 1, ke[pl.ds(x + 8, 1), :], 2)
+        left[pl.ds(x, NS, stride=NX), :], right[pl.ds(x, NS, stride=NX), :] = done
+        return carry
+
+    lax.fori_loop(0, NX, second_step, 0, unroll=U2)
+    adv_ref[:, :128] = left[...]
+    adv_ref[:, 128:] = right[...]
+
+
+def advance(c2d, k, rate, faces):
+    small = (k, rate, *faces)
+    return pl.pallas_call(
+        advance_kernel,
+        grid=(1,),
+        out_shape=jax.ShapeDtypeStruct((NS * NX, NV), f32),
+        in_specs=halves(c2d) + [whole_block(v.shape) for v in small],
+        out_specs=whole_block((NS * NX, NV)),
+        scratch_shapes=[
+            pltpu.VMEM((NX + 4, NS, NV + NH), f32),
+            pltpu.VMEM((NX + 2, NS, NV + NH), f32),
+            pltpu.VMEM((NX + 16, NV + NH), f32),
+            pltpu.VMEM((NS * NX, 128), f32),
+            pltpu.VMEM((NS * NX, 128), f32),
+        ],
+        compiler_params=pltpu.CompilerParams(vmem_limit_bytes=40 * 1024 * 1024),
+        cost_estimate=pl.CostEstimate(flops=40000000000, bytes_accessed=4 * 2**20, transcendentals=0),
+        name="advance_twice",
+    )(c2d, c2d, *small)
+
+
+def reduce_kernel(a0_ref, a1_ref, fs_ref, whole_ref, planes_ref):
+    lane_q = lanes(NQ)
+    low_q, even_q = lane_q < 64, (lane_q & 32) == 0
     fs_hi, fs_lo = split_2(fs_ref[...])
     weights = jnp.concatenate([fs_hi, fs_hi, fs_lo, fs_lo], axis=1)
 
-    low_q, even_q = lane_q < 64, (lane_q & 32) == 0
-
-    def second_step(group, carry):
+    def four_rows(group, carry):
         rows = []
         for g in range(4):
-            x = group * 4 + g
-            done = step(e1, x + 1, ke[pl.ds(x + 8, 1), :], 2)
-            left[pl.ds(x, NS, stride=NX), :], right[pl.ds(x, NS, stride=NX), :] = done
-            v = jnp.concatenate(done, axis=1)
-            hi, lo = split_2(v)
+            cut = pl.ds(group * 4 + g, NS, stride=NX)
+            hi, lo = split_2(jnp.concatenate([a0_ref[cut, :], a1_ref[cut, :]], axis=1))
             stacked = jnp.concatenate([hi, lo, hi, lo], axis=0)
             rows.append(jnp.dot(weights, stacked, preferred_element_type=f32))
         swapped = []
@@ -158,30 +187,18 @@
             planes_ref[pl.ds(group * 4 + g, NZ, stride=NX), :] = turned[g * NZ : (g + 1) * NZ, :]
         return carry
 
-    lax.fori_loop(0, NX // 4, second_step, 0)
-    adv_ref[:, :128] = left[...]
-    adv_ref[:, 128:] = right[...]
-
-
-def advance(c2d, k, rate, fs, faces, whole):
-    small = (k, rate, fs, *faces)
-    shapes = [(NS * NX, NV), (NZ * NX, 128)]
-    return pl.pallas_call(
-        advance_kernel,
-        grid=(1,),
-        out_shape=[jax.ShapeDtypeStruct(s, f32) for s in shapes],
-        in_specs=halves(c2d) + [whole_block(v.shape) for v in small] + [pl.BlockSpec(memory_space=pl.ANY)],
-        out_specs=[whole_block(s) for s in shapes],
-        scratch_shapes=[
-            pltpu.VMEM((NX + 4, NS, NV + NH), f32),
-            pltpu.VMEM((NX + 2, NS, NV + NH), f32),
-            pltpu.VMEM((NX + 16, NV + NH), f32),
-            pltpu.VMEM((NS * NX, 128), f32),
-            pltpu.VMEM((NS * NX, 128), f32),
-        ],
-        compiler_params=pltpu.CompilerParams(vmem_limit_bytes=40 * 1024 * 1024),
-        name="advance_twice",
-    )(c2d, c2d, *small, whole)
+    lax.fori_loop(0, NX // 4, four_rows, 0, unroll=U3)
+
+
+def reduce_species(advanced, fs, whole):
+    return pl.pallas_call(
+        reduce_kernel,
+        grid=(1,),
+        out_shape=jax.ShapeDtypeStruct((NZ * NX, 128), f32),
+        in_specs=halves(advanced) + [whole_block(fs.shape), pl.BlockSpec(memory_space=pl.ANY)],
+        out_specs=whole_block((NZ * NX, 128)),
+        name="reduce_species",
+    )(advanced, advanced, fs, whole)
 
 
 def shift_to(v, dx, dy):
@@ -197,12 +214,13 @@
     n_tx, n_ty = lax.axis_size("tx"), lax.axis_size("ty")
     ranks_q = factor_species.shape[1]
     c2d = species.reshape(nspec * cells_x, merged)
-    *faces, copies = pack(c2d, cell_factor, factor_x, n_tx)
+    faces = pack(c2d, cell_factor)
     xl, xh, yl, yh = (shift_to(v, dx, dy) for v, (dx, dy) in zip(faces, [(-1, 0), (1, 0), (0, -1), (0, 1)]))
-    lo, hi = corners(xl, xh)
+    lo, hi, copies = corners(xl, xh, factor_x, n_tx)
     faces = xl, xh, yl, yh, shift_to(lo, 0, -1), shift_to(hi, 0, 1)
     whole_x = lax.all_to_all(copies, "tx", 0, 0, tiled=True).reshape(-1, factor_x.shape[1])
-    advanced, planes = advance(c2d, cell_factor, species_rate[:, None], factor_species.T, faces, whole_x)
+    advanced = advance(c2d, cell_factor, species_rate[:, None], faces)
+    planes = reduce_species(advanced, factor_species.T, whole_x)
     planes = planes.reshape(depth, cells_x, cells_y * ranks_q)
     planes = lax.all_to_all(planes, "tx", 0, 0, tiled=True).reshape(-1, cells_y * ranks_q)
     first = lax.dot_general(planes, whole_x, (((0,), (0,)), ((), ())), precision=exact_mode)

time: 140 us -> 141 us (level)
  waiting for transfers between devices: 4.62 us -> 11.2 us
  blocking collectives: 83.8 us -> 78.2 us
  starting transfers between devices: 27.3 us -> 29.8 us
    all_to_all x1, waiting for transfers between devices: 0.01 us -> 9.51 us  [body(): lax.all_to_all(copies, 'tx', 0, 0, tiled=True)]
    ppermute x6, starting transfers between devices: 16.6 us -> 21.9 us  [shift_to(): lax.ppermute(v, axis, [(i, i + step) for i in range(count) if 0 <= i + st...]
    all_to_all x1, blocking collectives: 25.3 us -> 22.4 us  [body(): lax.all_to_all(planes, 'tx', 0, 0, tiled=True)]
    ppermute x6, waiting for transfers between devices: 4.62 us -> 1.7 us  [shift_to(): lax.ppermute(v, axis, [(i, i + step) for i in range(count) if 0 <= i + st...]
    all_to_all x1, starting transfers between devices: 10.7 us -> 7.87 us  [body(): lax.all_to_all(copies, 'tx', 0, 0, tiled=True)]
    all_to_all x1, blocking collectives: 29 us -> 26.5 us  [body(): came = lax.all_to_all(sent, 'ty', 0, 0, tiled=True)]
    pallas_call x1 -> x2, Pallas kernels: 11.6 us -> 10.3 us  [the longest x1 6.98 us: advance(): pl.pallas_call(advance_kernel, grid=(1,), out_shape=jax.ShapeDtypeStruct(...]
    unnamed x19 -> x21, local copies, waits for them, and re-layouts: 3.87 us -> 3.13 us
  transfers between devices with their start and end apart: 7 -> 7, of which waited for: 2 -> 2; matrix products, arithmetic and copies ran while one was open for 0% -> 0% of each run, Pallas kernels for 1% -> 6%
where the time goes in v4:
time: 141 us
  blocking collectives  78.2 us (55%)
  starting transfers between devices  29.8 us (21%)
  Pallas kernels  14.7 us (10%)
  waiting for transfers between devices  11.2 us (8%)
  local copies, waits for them, and re-layouts  4.58 us (3%)
    all_to_all x1, blocking collectives, body(): core = lax.all_to_all(plane, ('tx', 'ty'), 0, 0, tiled=True)  29.4 us
    all_to_all x1, blocking collectives, body(): came = lax.all_to_all(sent, 'ty', 0, 0, tiled=True)  26.5 us
    all_to_all x1, blocking collectives, body(): lax.all_to_all(planes, 'tx', 0, 0, tiled=True)  22.4 us
    ppermute x6, starting transfers between devices, shift_to(): lax.ppermute(v, axis, [(i, i + step) for i in range(count) if 0 <= i + st...  21.9 us
    all_to_all x1, waiting for transfers between devices, body(): lax.all_to_all(copies, 'tx', 0, 0, tiled=True)  9.51 us
    all_to_all x1, starting transfers between devices, body(): lax.all_to_all(copies, 'tx', 0, 0, tiled=True)  7.87 us
    pallas_call x1, Pallas kernels, advance(): pl.pallas_call(advance_kernel, grid=(1,), out_shape=jax.ShapeDtypeStruct(...  6.98 us
    pallas_call x1, Pallas kernels, reduce_species(): pl.pallas_call(reduce_kernel, grid=(1,), out_shape=jax.ShapeDtypeStruct((...  3.31 us
  transfers between devices with their start and end apart: 7, of which 2 were waited for; matrix products, arithmetic and copies ran while one was open for 0% of the time, Pallas kernels for 6%

profile of v4, /device:TPU:1, one launch (start us, length us, event | category | flops | bytes accessed | tf_op | source)
XLA Modules:
  0.0 140.5 jit_solution(9155600842450826714)
XLA Ops:
  0.6 2.6 %pack_faces.1 = (f32[72,256]{1,0:T(8,128)}, f32[72,256]{1,0:T(8,128)}, f32[544,128]{1,0:T(8,128)}, f32[544,128]{1,0:T(8,128)}) custom-call(f32[1024,256]{1,0:T(8,128)} %bitcast.42, f32[1024,256]{1,0:T(8,128)} %bitcast.43, f32[32,256]{1,0:T(8,128)} %k_ref.3), custom_call_target="tpu_custom_call" | custom-call | tf_op jit(solution)/shard_map/pack_faces/pallas_call | solution.py:47
  3.3 1.4 %collective-permute-start.2 = (f32[544,128]{1,0:T(8,128)}, f32[544,128]{1,0:T(8,128)S(1)}, u32[]{:S(2)}, u32[]{:S(2)}) collective-permute-start(f32[544,128]{1,0:T(8,128)} %get-tuple-element.11), channel_id=1, source_target_pairs={{1,0},{2,1},{3,2},{4,3},{5,4},{6,5},{7,6},{8,7},{9,8},{10,9},{11,1... | collective-permute-start | bytes 835592 | tf_op jit(solution)/shard_map/ppermute | solution.py:207
  4.7 4.6 %collective-permute-start.3 = (f32[544,128]{1,0:T(8,128)}, f32[544,128]{1,0:T(8,128)S(1)}, u32[]{:S(2)}, u32[]{:S(2)}) collective-permute-start(f32[544,128]{1,0:T(8,128)} %get-tuple-element.12), channel_id=1, source_target_pairs={{0,1},{1,2},{2,3},{3,4},{4,5},{5,6},{6,7},{7,8},{8,9},{9,10},{10,1... | collective-permute-start | bytes 835592 | tf_op jit(solution)/shard_map/ppermute | solution.py:207
  9.3 8.8 %collective-permute-start = (f32[72,256]{1,0:T(8,128)}, f32[72,256]{1,0:T(8,128)S(1)}, u32[]{:S(2)}, u32[]{:S(2)}) collective-permute-start(f32[72,256]{1,0:T(8,128)} %get-tuple-element.9), channel_id=1, source_target_pairs={{16,0},{32,16},{48,32},{64,48},{80,64},{96,80},{112,96},{128,112},... | collective-permute-start | bytes 221192 | tf_op jit(solution)/shard_map/ppermute | solution.py:207
  18.1 1.9 %collective-permute-start.1 = (f32[72,256]{1,0:T(8,128)}, f32[72,256]{1,0:T(8,128)S(1)}, u32[]{:S(2)}, u32[]{:S(2)}) collective-permute-start(f32[72,256]{1,0:T(8,128)} %get-tuple-element.10), channel_id=1, source_target_pairs={{0,16},{16,32},{32,48},{48,64},{64,80},{80,96},{96,112},{112,128},... | collective-permute-start | bytes 221192 | tf_op jit(solution)/shard_map/ppermute | solution.py:207
  20.0 1.7 %collective-permute-done.1.xh_ref = f32[72,256]{1,0:T(8,128)S(1)} collective-permute-done((f32[72,256]{1,0:T(8,128)}, f32[72,256]{1,0:T(8,128)S(1)}, u32[]{:S(2)}, u32[]{:S(2)}) %collective-permute-start.1) | collective-permute-done | bytes 73760 | tf_op jit(solution)/shard_map/ppermute | solution.py:207
  21.7 0.6 copy-done.3
  22.3 1.8 %corner_columns.1 = (f32[64,128]{1,0:T(8,128)}, f32[64,128]{1,0:T(8,128)}, f32[32,32,128]{2,1,0:T(8,128)}) custom-call(f32[72,256]{1,0:T(8,128)} %copy-done.1, f32[72,256]{1,0:T(8,128)} %copy-done.3, f32[32,128]{1,0:T(8,128)} %fx_ref.1), custom_call_target="tpu_custom_call" | custom-call | tf_op jit(solution)/shard_map/corner_columns/pallas_call | solution.py:66
  24.1 1.3 collective-permute-start.4
  25.4 4.0 %collective-permute-start.5 = (f32[64,128]{1,0:T(8,128)}, f32[64,128]{1,0:T(8,128)S(1)}, u32[]{:S(2)}, u32[]{:S(2)}) collective-permute-start(f32[64,128]{1,0:T(8,128)} %get-tuple-element.14), channel_id=1, source_target_pairs={{0,1},{1,2},{2,3},{3,4},{4,5},{5,6},{6,7},{7,8},{8,9},{9,10},{10,1... | collective-permute-start | bytes 98312 | tf_op jit(solution)/shard_map/ppermute | solution.py:207
  29.5 7.9 %all-to-all-start = ((f32[32,32,128]{2,1,0:T(8,128)}), f32[32,32,128]{2,1,0:T(8,128)S(1)}, u32[]{:S(2)}, u32[]{:S(2)}) async-start(f32[32,32,128]{2,1,0:T(8,128)} %get-tuple-element.15), calls=%async_computation | async-start | bytes 1048576 | tf_op jit(solution)/shard_map/all_to_all | solution.py:221
  37.5 7.0 %advance_twice.1.a0_ref.a1_ref = f32[1024,256]{1,0:T(8,128)} custom-call(f32[1024,256]{1,0:T(8,128)S(1)} %bitcast.44, f32[1024,256]{1,0:T(8,128)S(1)} %bitcast.45, f32[32,256]{1,0:T(8,128)S(1)} %copy-done.5, f32[32,1]{1,0:T(8,128)S(1)} %copy.20.rate_ref, f32[72,256]{1,0:T(8,128)S(1)} %copy-done.2, f32[72,256]{1,0:T(8,128)S(1)} %copy-done.4, ...), custom_call_target="tpu_custom_call" | custom-call | flops 40000000000 | bytes 4194304 | tf_op jit(solution)/shard_map/advance_twice/pallas_call | solution.py:145
  44.4 9.5 %all-to-all-done = f32[32,32,128]{2,1,0:T(8,128)S(1)} async-done(((f32[32,32,128]{2,1,0:T(8,128)}), f32[32,32,128]{2,1,0:T(8,128)S(1)}, u32[]{:S(2)}, u32[]{:S(2)}) %all-to-all-start) | async-done | bytes 524320 | tf_op jit(solution)/shard_map/all_to_all | solution.py:221
  54.0 0.8 copy-done.6
  54.7 3.3 %reduce_species.1 = f32[1024,128]{1,0:T(8,128)} custom-call(f32[1024,256]{1,0:T(8,128)} %advance_twice.1.a0_ref.a1_ref, f32[1024,256]{1,0:T(8,128)} %advance_twice.1.a0_ref.a1_ref, f32[16,32]{1,0:T(8,128)} %bitcast.55, f32[1024,128]{1,0:T(8,128)} %bitcast.46), custom_call_target="tpu_custom_call" | custom-call | tf_op jit(solution)/shard_map/reduce_species/pallas_call | solution.py:194
  58.0 22.4 %all_to_all.20 = f32[32,32,128]{2,1,0:T(8,128)S(1)} all-to-all(f32[32,32,128]{2,1,0:T(8,128)} %bitcast.52), channel_id=1, replica_groups=mesh['tx'=32,'ty'=16] {'tx'}, dimensions={0} | all-to-all | bytes 1048576 | tf_op jit(solution)/shard_map/all_to_all | solution.py:225
  80.6 0.8 copy-done.7
  81.5 0.6 convolution_bitcast_fusion.1
  82.2 26.5 %all_to_all.21 = f32[16,16,128]{2,1,0:T(8,128)S(1)} all-to-all(f32[16,16,128]{2,1,0:T(8,128)S(1)} %copy.22), channel_id=1, replica_groups=mesh['tx'=32,'ty'=16] {'ty'}, dimensions={0} | all-to-all | bytes 262144 | tf_op jit(solution)/shard_map/all_to_all | solution.py:229
  108.9 0.5 convolution_bitcast_fusion
  109.4 0.2 copy.27
  109.6 0.3 reshape.47
  110.0 29.4 %all_to_all.22 = f32[512,1,32]{2,1,0:T(1,128)S(1)} all-to-all(f32[512,1,32]{2,1,0:T(1,128)S(1)} %copy.28), channel_id=1, replica_groups=mesh['tx'=32,'ty'=16] {'tx','ty'}, dimensions={0} | all-to-all | bytes 131072 | tf_op jit(solution)/shard_map/all_to_all | solution.py:236
  139.7 0.8 copy.30
  (33 shorter events, 1.1 us)
Async XLA Ops:
  0.6 28.8 %copy-start.9 = (f32[32]{0:T(128)S(1)}, f32[32]{0:T(128)}, u32[]{:S(2)}) copy-start(f32[32]{0:T(128)} %param.8) | copy-start | bytes 388
  3.3 34.1 %copy-start = (f32[32,32,256]{2,1,0:T(8,128)S(1)}, f32[32,32,256]{2,1,0:T(8,128)}, u32[]{:S(2)}) copy-start(f32[32,32,256]{2,1,0:T(8,128)} %param.6) | copy-start | bytes 3145732
  3.3 34.1 %collective-permute-start.2 = (f32[544,128]{1,0:T(8,128)}, f32[544,128]{1,0:T(8,128)S(1)}, u32[]{:S(2)}, u32[]{:S(2)}) collective-permute-start(f32[544,128]{1,0:T(8,128)} %get-tuple-element.11), channel_id=1, source_target_pairs={{1,0},{2,1},{3,2},{4,3},{5,4},{6,5},{7,6},{8,7},{9,8},{10,9},{11,1... | collective-permute-start | bytes 835592 | tf_op jit(solution)/shard_map/ppermute | solution.py:207
  4.7 32.7 %collective-permute-start.3 = (f32[544,128]{1,0:T(8,128)}, f32[544,128]{1,0:T(8,128)S(1)}, u32[]{:S(2)}, u32[]{:S(2)}) collective-permute-start(f32[544,128]{1,0:T(8,128)} %get-tuple-element.12), channel_id=1, source_target_pairs={{0,1},{1,2},{2,3},{3,4},{4,5},{5,6},{6,7},{7,8},{8,9},{9,10},{10,1... | collective-permute-start | bytes 835592 | tf_op jit(solution)/shard_map/ppermute | solution.py:207
  9.3 10.7 %collective-permute-start = (f32[72,256]{1,0:T(8,128)}, f32[72,256]{1,0:T(8,128)S(1)}, u32[]{:S(2)}, u32[]{:S(2)}) collective-permute-start(f32[72,256]{1,0:T(8,128)} %get-tuple-element.9), channel_id=1, source_target_pairs={{16,0},{32,16},{48,32},{64,48},{80,64},{96,80},{112,96},{128,112},... | collective-permute-start | bytes 221192 | tf_op jit(solution)/shard_map/ppermute | solution.py:207
  18.1 3.6 %collective-permute-start.1 = (f32[72,256]{1,0:T(8,128)}, f32[72,256]{1,0:T(8,128)S(1)}, u32[]{:S(2)}, u32[]{:S(2)}) collective-permute-start(f32[72,256]{1,0:T(8,128)} %get-tuple-element.10), channel_id=1, source_target_pairs={{0,16},{16,32},{32,48},{48,64},{64,80},{80,96},{96,112},{112,128},... | collective-permute-start | bytes 221192 | tf_op jit(solution)/shard_map/ppermute | solution.py:207
  20.0 1.7 %copy-start.1 = (f32[72,256]{1,0:T(8,128)}, f32[72,256]{1,0:T(8,128)S(1)}, u32[]{:S(2)}) copy-start(f32[72,256]{1,0:T(8,128)S(1)} %collective-permute-done.xl_ref) | copy-start | bytes 221188
  21.7 0.6 copy-start.3
  24.1 13.3 %collective-permute-start.4 = (f32[64,128]{1,0:T(8,128)}, f32[64,128]{1,0:T(8,128)S(1)}, u32[]{:S(2)}, u32[]{:S(2)}) collective-permute-start(f32[64,128]{1,0:T(8,128)} %get-tuple-element.13), channel_id=1, source_target_pairs={{1,0},{2,1},{3,2},{4,3},{5,4},{6,5},{7,6},{8,7},{9,8},{10,9},{11,1... | collective-permute-start | bytes 98312 | tf_op jit(solution)/shard_map/ppermute | solution.py:207
  25.4 12.0 %collective-permute-start.5 = (f32[64,128]{1,0:T(8,128)}, f32[64,128]{1,0:T(8,128)S(1)}, u32[]{:S(2)}, u32[]{:S(2)}) collective-permute-start(f32[64,128]{1,0:T(8,128)} %get-tuple-element.14), channel_id=1, source_target_pairs={{0,1},{1,2},{2,3},{3,4},{4,5},{5,6},{6,7},{7,8},{8,9},{9,10},{10,1... | collective-permute-start | bytes 98312 | tf_op jit(solution)/shard_map/ppermute | solution.py:207
  29.5 7.9 %copy-start.2 = (f32[72,256]{1,0:T(8,128)S(1)}, f32[72,256]{1,0:T(8,128)}, u32[]{:S(2)}) copy-start(f32[72,256]{1,0:T(8,128)} %copy-done.1) | copy-start | bytes 221188
  29.5 7.9 %copy-start.4 = (f32[72,256]{1,0:T(8,128)S(1)}, f32[72,256]{1,0:T(8,128)}, u32[]{:S(2)}) copy-start(f32[72,256]{1,0:T(8,128)} %copy-done.3) | copy-start | bytes 221188
  29.5 8.0 %copy-start.5 = (f32[32,256]{1,0:T(8,128)S(1)}, f32[32,256]{1,0:T(8,128)}, u32[]{:S(2)}) copy-start(f32[32,256]{1,0:T(8,128)} %k_ref.3) | copy-start | bytes 98308
  29.5 24.4 %all-to-all-start = ((f32[32,32,128]{2,1,0:T(8,128)}), f32[32,32,128]{2,1,0:T(8,128)S(1)}, u32[]{:S(2)}, u32[]{:S(2)}) async-start(f32[32,32,128]{2,1,0:T(8,128)} %get-tuple-element.15), calls=%async_computation | async-start | bytes 1048576 | tf_op jit(solution)/shard_map/all_to_all | solution.py:221
  53.9 0.8 copy-start.6
  80.4 1.0 copy-start.7
  81.5 0.7 copy-start.8

commit v5 on v4

--- a/solution.py
+++ b/solution.py
@@ -50,27 +50,44 @@
         out_shape=[jax.ShapeDtypeStruct(s, f32) for s in shapes],
         in_specs=halves(c2d) + [whole_block(k.shape)],
         out_specs=[whole_block(s) for s in shapes],
+        compiler_params=pltpu.CompilerParams(vmem_limit_bytes=8 * 2**20),
         name="pack_faces",
     )(c2d, c2d, k)
 
 
-def corner_kernel(xl_ref, xh_ref, fx_ref, lo_ref, hi_ref, copies_ref):
+def corner_kernel(xl_ref, xh_ref, lo_ref, hi_ref):
     for at, ref in ((0, xh_ref), (NS, xl_ref)):
         lo_ref[at : at + NS, :] = ref[0:NS, :128]
         hi_ref[at : at + NS, :] = ref[0:NS, 128:]
-    copies_ref[...] = jnp.broadcast_to(fx_ref[...][None], copies_ref.shape)
-
-
-def corners(xl, xh, factor_x, copies):
-    shapes = [(2 * NS, 128)] * 2 + [(copies,) + factor_x.shape]
+
+
+def corners(xl, xh):
+    shapes = [(2 * NS, 128)] * 2
     return pl.pallas_call(
         corner_kernel,
         grid=(1,),
         out_shape=[jax.ShapeDtypeStruct(s, f32) for s in shapes],
-        in_specs=[whole_block(v.shape) for v in (xl, xh, factor_x)],
+        in_specs=[whole_block(v.shape) for v in (xl, xh)],
         out_specs=[whole_block(s) for s in shapes],
+        compiler_params=pltpu.CompilerParams(vmem_limit_bytes=4 * 2**20),
         name="corner_columns",
-    )(xl, xh, factor_x)
+    )(xl, xh)
+
+
+def copies_kernel(v_ref, after_ref, out_ref):
+    out_ref[...] = jnp.broadcast_to(v_ref[...][None], out_ref.shape)
+
+
+def copies_of(v, count, after):
+    return pl.pallas_call(
+        copies_kernel,
+        grid=(1,),
+        out_shape=jax.ShapeDtypeStruct((count,) + v.shape, f32),
+        in_specs=[whole_block(v.shape), pl.BlockSpec(memory_space=pl.ANY)],
+        out_specs=whole_block((count,) + v.shape),
+        compiler_params=pltpu.CompilerParams(vmem_limit_bytes=4 * 2**20),
+        name="copies_of_factor",
+    )(v, after)
 
 
 def split_2(v):
@@ -155,8 +172,8 @@
             pltpu.VMEM((NS * NX, 128), f32),
             pltpu.VMEM((NS * NX, 128), f32),
         ],
-        compiler_params=pltpu.CompilerParams(vmem_limit_bytes=40 * 1024 * 1024),
-        cost_estimate=pl.CostEstimate(flops=40000000000, bytes_accessed=4 * 2**20, transcendentals=0),
+        compiler_params=pltpu.CompilerParams(vmem_limit_bytes=16 * 2**20),
+        cost_estimate=pl.CostEstimate(flops=10000000000, bytes_accessed=4 * 2**20, transcendentals=0),
         name="advance_twice",
     )(c2d, c2d, *small)
 
@@ -197,6 +214,7 @@
         out_shape=jax.ShapeDtypeStruct((NZ * NX, 128), f32),
         in_specs=halves(advanced) + [whole_block(fs.shape), pl.BlockSpec(memory_space=pl.ANY)],
         out_specs=whole_block((NZ * NX, 128)),
+        compiler_params=pltpu.CompilerParams(vmem_limit_bytes=8 * 2**20),
         name="reduce_species",
     )(advanced, advanced, fs, whole)
 
@@ -216,7 +234,8 @@
     c2d = species.reshape(nspec * cells_x, merged)
     faces = pack(c2d, cell_factor)
     xl, xh, yl, yh = (shift_to(v, dx, dy) for v, (dx, dy) in zip(faces, [(-1, 0), (1, 0), (0, -1), (0, 1)]))
-    lo, hi, copies = corners(xl, xh, factor_x, n_tx)
+    lo, hi = corners(xl, xh)
+    copies = copies_of(factor_x, n_tx, xh)
     faces = xl, xh, yl, yh, shift_to(lo, 0, -1), shift_to(hi, 0, 1)
     whole_x = lax.all_to_all(copies, "tx", 0, 0, tiled=True).reshape(-1, factor_x.shape[1])
     advanced = advance(c2d, cell_factor, species_rate[:, None], faces)

time: 141 us -> 132 us (0.936)
  waiting for transfers between devices: 11.2 us -> 4.12 us
  Pallas kernels: 14.7 us -> 10 us
  blocking collectives: 78.2 us -> 81.2 us
    all_to_all x1, waiting for transfers between devices: 9.51 us -> 3.2 us  [body(): lax.all_to_all(copies, 'tx', 0, 0, tiled=True)]
    all_to_all x1, blocking collectives: 26.5 us -> 29.1 us  [body(): came = lax.all_to_all(sent, 'ty', 0, 0, tiled=True)]
    pallas_call x1, Pallas kernels: 2.64 us -> 0.73 us  [pack(): pl.pallas_call(pack_kernel, grid=(1,), out_shape=[jax.ShapeDtypeStruct(s,...]
    pallas_call x1, Pallas kernels: 3.31 us -> 1.43 us  [reduce_species(): pl.pallas_call(reduce_kernel, grid=(1,), out_shape=jax.ShapeDtypeStruct((...]
    pallas_call x1, Pallas kernels: 1.78 us -> 0.01 us  [corners(): pl.pallas_call(corner_kernel, grid=(1,), out_shape=[jax.ShapeDtypeStruct(...]
    unnamed x21 -> x19, local copies, waits for them, and re-layouts: 3.13 us -> 4.07 us
where the time goes in v5:
time: 132 us
  blocking collectives  81.2 us (62%)
  starting transfers between devices  28.7 us (22%)
  Pallas kernels  10 us (8%)
  local copies, waits for them, and re-layouts  5.52 us (4%)
  waiting for transfers between devices  4.12 us (3%)
    all_to_all x1, blocking collectives, body(): core = lax.all_to_all(plane, ('tx', 'ty'), 0, 0, tiled=True)  29.4 us
    all_to_all x1, blocking collectives, body(): came = lax.all_to_all(sent, 'ty', 0, 0, tiled=True)  29.1 us
    all_to_all x1, blocking collectives, body(): lax.all_to_all(planes, 'tx', 0, 0, tiled=True)  22.6 us
    ppermute x6, starting transfers between devices, shift_to(): lax.ppermute(v, axis, [(i, i + step) for i in range(count) if 0 <= i + st...  21.3 us
    all_to_all x1, starting transfers between devices, body(): lax.all_to_all(copies, 'tx', 0, 0, tiled=True)  7.34 us
    pallas_call x1, Pallas kernels, advance(): pl.pallas_call(advance_kernel, grid=(1,), out_shape=jax.ShapeDtypeStruct(...  6.98 us
    unnamed x19, local copies, waits for them, and re-layouts  4.07 us
    all_to_all x1, waiting for transfers between devices, body(): lax.all_to_all(copies, 'tx', 0, 0, tiled=True)  3.2 us
  transfers between devices with their start and end apart: 7, of which 2 were waited for; matrix products, arithmetic and copies ran while one was open for 0% of the time, Pallas kernels for 6%

profile of v5, /device:TPU:1, one launch (start us, length us, event | category | flops | bytes accessed | tf_op | source)
XLA Modules:
  0.0 131.5 jit_solution(4040897448992995479)
XLA Ops:
  0.6 1.2 copy-done.1
  1.9 0.8 copy-done.3
  2.6 0.7 pack_faces.1
  3.4 1.4 %collective-permute-start.2 = (f32[544,128]{1,0:T(8,128)S(1)}, f32[544,128]{1,0:T(8,128)S(1)}, u32[]{:S(2)}, u32[]{:S(2)}) collective-permute-start(f32[544,128]{1,0:T(8,128)S(1)} %get-tuple-element.10), channel_id=1, source_target_pairs={{1,0},{2,1},{3,2},{4,3},{5,4},{6,5},{7,6},{8,7},{9,8},{10,9},{11,1... | collective-permute-start | bytes 835592 | tf_op jit(solution)/shard_map/ppermute | solution.py:225
  4.8 4.6 %collective-permute-start.3 = (f32[544,128]{1,0:T(8,128)S(1)}, f32[544,128]{1,0:T(8,128)S(1)}, u32[]{:S(2)}, u32[]{:S(2)}) collective-permute-start(f32[544,128]{1,0:T(8,128)S(1)} %get-tuple-element.11), channel_id=1, source_target_pairs={{0,1},{1,2},{2,3},{3,4},{4,5},{5,6},{6,7},{7,8},{8,9},{9,10},{10,1... | collective-permute-start | bytes 835592 | tf_op jit(solution)/shard_map/ppermute | solution.py:225
  9.4 4.6 %collective-permute-start.1 = (f32[72,256]{1,0:T(8,128)S(1)}, f32[72,256]{1,0:T(8,128)S(1)}, u32[]{:S(2)}, u32[]{:S(2)}) collective-permute-start(f32[72,256]{1,0:T(8,128)S(1)} %get-tuple-element.9), channel_id=1, source_target_pairs={{0,16},{16,32},{32,48},{48,64},{64,80},{80,96},{96,112},{112,128},... | collective-permute-start | bytes 221192 | tf_op jit(solution)/shard_map/ppermute | solution.py:225
  14.0 5.5 %collective-permute-start = (f32[72,256]{1,0:T(8,128)S(1)}, f32[72,256]{1,0:T(8,128)S(1)}, u32[]{:S(2)}, u32[]{:S(2)}) collective-permute-start(f32[72,256]{1,0:T(8,128)S(1)} %get-tuple-element.8), channel_id=1, source_target_pairs={{16,0},{32,16},{48,32},{64,48},{80,64},{96,80},{112,96},{128,112},... | collective-permute-start | bytes 221192 | tf_op jit(solution)/shard_map/ppermute | solution.py:225
  19.5 0.9 copies_of_factor.1
  20.4 7.3 %all-to-all-start = ((f32[32,32,128]{2,1,0:T(8,128)}), f32[32,32,128]{2,1,0:T(8,128)S(1)}, u32[]{:S(2)}, u32[]{:S(2)}) async-start(f32[32,32,128]{2,1,0:T(8,128)} %copies_of_factor.1), calls=%async_computation | async-start | bytes 1048576 | tf_op jit(solution)/shard_map/all_to_all | solution.py:240
  27.7 1.3 collective-permute-start.4
  29.0 4.0 %collective-permute-start.5 = (f32[64,128]{1,0:T(8,128)S(1)}, f32[64,128]{1,0:T(8,128)S(1)}, u32[]{:S(2)}, u32[]{:S(2)}) collective-permute-start(f32[64,128]{1,0:T(8,128)S(1)} %get-tuple-element.13), channel_id=1, source_target_pairs={{0,1},{1,2},{2,3},{3,4},{4,5},{5,6},{6,7},{7,8},{8,9},{9,10},{10,1... | collective-permute-start | bytes 98312 | tf_op jit(solution)/shard_map/ppermute | solution.py:225
  33.1 0.9 collective-permute-done.5.ch_ref
  34.1 7.0 %advance_twice.1.a0_ref.a1_ref = f32[1024,256]{1,0:T(8,128)} custom-call(f32[1024,256]{1,0:T(8,128)S(1)} %bitcast.47, f32[1024,256]{1,0:T(8,128)S(1)} %bitcast.48, f32[32,256]{1,0:T(8,128)S(1)} %copy-done.4, f32[32,1]{1,0:T(8,128)S(1)} %copy.20.rate_ref, f32[72,256]{1,0:T(8,128)S(1)} %collective-permute-done.xl_ref, ...), custom_call_target="tpu_custom_call" | custom-call | flops 10000000000 | bytes 4194304 | tf_op jit(solution)/shard_map/advance_twice/pallas_call | solution.py:162
  41.1 3.2 %all-to-all-done = f32[32,32,128]{2,1,0:T(8,128)S(1)} async-done(((f32[32,32,128]{2,1,0:T(8,128)}), f32[32,32,128]{2,1,0:T(8,128)S(1)}, u32[]{:S(2)}, u32[]{:S(2)}) %all-to-all-start) | async-done | bytes 524320 | tf_op jit(solution)/shard_map/all_to_all | solution.py:240
  44.3 1.2 copy-done
  45.5 1.4 %reduce_species.1 = f32[1024,128]{1,0:T(8,128)S(1)} custom-call(f32[1024,256]{1,0:T(8,128)S(1)} %copy-done, f32[1024,256]{1,0:T(8,128)S(1)} %copy-done, f32[16,32]{1,0:T(8,128)S(1)} %bitcast.50, f32[1024,128]{1,0:T(8,128)S(1)} %bitcast.42), custom_call_target="tpu_custom_call" | custom-call | tf_op jit(solution)/shard_map/reduce_species/pallas_call | solution.py:211
  46.9 22.6 %all_to_all.20 = f32[32,32,128]{2,1,0:T(8,128)S(1)} all-to-all(f32[32,32,128]{2,1,0:T(8,128)S(1)} %bitcast.49), channel_id=1, replica_groups=mesh['tx'=32,'ty'=16] {'tx'}, dimensions={0} | all-to-all | bytes 1048576 | tf_op jit(solution)/shard_map/all_to_all | solution.py:244
  69.8 0.6 convolution_bitcast_fusion.1
  70.5 29.1 %all_to_all.21 = f32[16,16,128]{2,1,0:T(8,128)S(1)} all-to-all(f32[16,16,128]{2,1,0:T(8,128)S(1)} %copy.22), channel_id=1, replica_groups=mesh['tx'=32,'ty'=16] {'ty'}, dimensions={0} | all-to-all | bytes 262144 | tf_op jit(solution)/shard_map/all_to_all | solution.py:248
  99.9 0.5 convolution_bitcast_fusion
  100.3 0.2 copy.27
  100.5 0.3 reshape.47
  101.0 29.4 %all_to_all.22 = f32[512,1,32]{2,1,0:T(1,128)S(1)} all-to-all(f32[512,1,32]{2,1,0:T(1,128)S(1)} %copy.28), channel_id=1, replica_groups=mesh['tx'=32,'ty'=16] {'tx','ty'}, dimensions={0} | all-to-all | bytes 131072 | tf_op jit(solution)/shard_map/all_to_all | solution.py:255
  130.7 0.8 copy.30
  (32 shorter events, 1.1 us)
Async XLA Ops:
  0.6 1.2 copy-start.1
  1.9 0.8 copy-start.3
  2.6 16.9 %copy-start.5 = (f32[32,128]{1,0:T(8,128)S(1)}, f32[32,128]{1,0:T(8,128)}, u32[]{:S(2)}) copy-start(f32[32,128]{1,0:T(8,128)} %v_ref.1) | copy-start | bytes 49156
  3.4 30.7 %copy-start.2 = (f32[32,32,256]{2,1,0:T(8,128)S(1)}, f32[32,32,256]{2,1,0:T(8,128)}, u32[]{:S(2)}) copy-start(f32[32,32,256]{2,1,0:T(8,128)} %param.6) | copy-start | bytes 3145732
  3.4 30.7 %collective-permute-start.2 = (f32[544,128]{1,0:T(8,128)S(1)}, f32[544,128]{1,0:T(8,128)S(1)}, u32[]{:S(2)}, u32[]{:S(2)}) collective-permute-start(f32[544,128]{1,0:T(8,128)S(1)} %get-tuple-element.10), channel_id=1, source_target_pairs={{1,0},{2,1},{3,2},{4,3},{5,4},{6,5},{7,6},{8,7},{9,8},{10,9},{11,1... | collective-permute-start | bytes 835592 | tf_op jit(solution)/shard_map/ppermute | solution.py:225
  4.8 29.2 %collective-permute-start.3 = (f32[544,128]{1,0:T(8,128)S(1)}, f32[544,128]{1,0:T(8,128)S(1)}, u32[]{:S(2)}, u32[]{:S(2)}) collective-permute-start(f32[544,128]{1,0:T(8,128)S(1)} %get-tuple-element.11), channel_id=1, source_target_pairs={{0,1},{1,2},{2,3},{3,4},{4,5},{5,6},{6,7},{7,8},{8,9},{9,10},{10,1... | collective-permute-start | bytes 835592 | tf_op jit(solution)/shard_map/ppermute | solution.py:225
  9.4 10.1 %collective-permute-start.1 = (f32[72,256]{1,0:T(8,128)S(1)}, f32[72,256]{1,0:T(8,128)S(1)}, u32[]{:S(2)}, u32[]{:S(2)}) collective-permute-start(f32[72,256]{1,0:T(8,128)S(1)} %get-tuple-element.9), channel_id=1, source_target_pairs={{0,16},{16,32},{32,48},{48,64},{64,80},{80,96},{96,112},{112,128},... | collective-permute-start | bytes 221192 | tf_op jit(solution)/shard_map/ppermute | solution.py:225
  14.0 13.7 %collective-permute-start = (f32[72,256]{1,0:T(8,128)S(1)}, f32[72,256]{1,0:T(8,128)S(1)}, u32[]{:S(2)}, u32[]{:S(2)}) collective-permute-start(f32[72,256]{1,0:T(8,128)S(1)} %get-tuple-element.8), channel_id=1, source_target_pairs={{16,0},{32,16},{48,32},{64,48},{80,64},{96,80},{112,96},{128,112},... | collective-permute-start | bytes 221192 | tf_op jit(solution)/shard_map/ppermute | solution.py:225
  20.4 23.9 %all-to-all-start = ((f32[32,32,128]{2,1,0:T(8,128)}), f32[32,32,128]{2,1,0:T(8,128)S(1)}, u32[]{:S(2)}, u32[]{:S(2)}) async-start(f32[32,32,128]{2,1,0:T(8,128)} %copies_of_factor.1), calls=%async_computation | async-start | bytes 1048576 | tf_op jit(solution)/shard_map/all_to_all | solution.py:240
  27.7 6.4 %copy-start.4 = (f32[32,256]{1,0:T(8,128)S(1)}, f32[32,256]{1,0:T(8,128)}, u32[]{:S(2)}) copy-start(f32[32,256]{1,0:T(8,128)} %k_ref.3) | copy-start | bytes 98308
  27.7 5.4 %collective-permute-start.4 = (f32[64,128]{1,0:T(8,128)S(1)}, f32[64,128]{1,0:T(8,128)S(1)}, u32[]{:S(2)}, u32[]{:S(2)}) collective-permute-start(f32[64,128]{1,0:T(8,128)S(1)} %get-tuple-element.12), channel_id=1, source_target_pairs={{1,0},{2,1},{3,2},{4,3},{5,4},{6,5},{7,6},{8,7},{9,8},{10,9},{11,1... | collective-permute-start | bytes 98312 | tf_op jit(solution)/shard_map/ppermute | solution.py:225
  29.0 4.0 %copy-start.8 = (f32[32]{0:T(128)S(1)}, f32[32]{0:T(128)}, u32[]{:S(2)}) copy-start(f32[32]{0:T(128)} %param.8) | copy-start | bytes 388
  29.0 5.0 %collective-permute-start.5 = (f32[64,128]{1,0:T(8,128)S(1)}, f32[64,128]{1,0:T(8,128)S(1)}, u32[]{:S(2)}, u32[]{:S(2)}) collective-permute-start(f32[64,128]{1,0:T(8,128)S(1)} %get-tuple-element.13), channel_id=1, source_target_pairs={{0,1},{1,2},{2,3},{3,4},{4,5},{5,6},{6,7},{7,8},{8,9},{9,10},{10,1... | collective-permute-start | bytes 98312 | tf_op jit(solution)/shard_map/ppermute | solution.py:225
  34.1 10.2 %copy-start.6 = (f32[32,16]{0,1:T(8,128)S(1)}, f32[32,16]{0,1:T(8,128)}, u32[]{:S(2)}) copy-start(f32[32,16]{0,1:T(8,128)} %param.11) | copy-start | bytes 6148
  44.3 1.2 copy-start
  69.7 0.7 copy-start.7

commit v6 on v5

--- a/solution.py
+++ b/solution.py
@@ -95,22 +95,20 @@
     return hi, (v - hi.astype(f32)).astype(bf16)
 
 
-def advance_kernel(c0_ref, c1_ref, k_ref, rate_ref, xl_ref, xh_ref, yl_ref, yh_ref, cl_ref, ch_ref, adv_ref, e0, e1, ke, left, right):
+def advance_kernel(c0_ref, c1_ref, k_ref, rate_ref, xl_ref, xh_ref, yl_ref, yh_ref, left, right, e0, e1, ke):
     half = NS // 2
     lane_s, lane_h = lanes(NS), lanes(half)
     z = lane_s % NZ
     not_first, not_last = z > 0, z < NZ - 1
     below, above = lane_s >= 32, lane_s < 96
 
-    low_s, low_h = lane_s < 64, lane_h < 64
+    low_h = lane_h < 64
     e0[0, :, :NV] = xh_ref[NS : 2 * NS, :]
     e0[1, :, :NV] = xh_ref[0:NS, :]
-    e0[1, :, NV:] = jnp.where(low_s, cl_ref[:NS, :], ch_ref[:NS, :])
     e0[NX + 2, :, :NV] = xl_ref[0:NS, :]
-    e0[NX + 2, :, NV:] = jnp.where(low_s, cl_ref[NS:, :], ch_ref[NS:, :])
     e0[NX + 3, :, :NV] = xl_ref[NS : 2 * NS, :]
-    e0[0, :, NV:] = jnp.zeros((NS, NH), f32)
-    e0[NX + 3, :, NV:] = jnp.zeros((NS, NH), f32)
+    for row in (0, 1, NX + 2, NX + 3):
+        e0[row, :, NV:] = jnp.zeros((NS, NH), f32)
     for x in range(NX):
         after, before = yl_ref[x * half : (x + 1) * half, :], yh_ref[x * half : (x + 1) * half, :]
         e0[x + 2, :, :128] = c0_ref[pl.ds(x, NS, stride=NX), :]
@@ -153,8 +151,6 @@
         return carry
 
     lax.fori_loop(0, NX, second_step, 0, unroll=U2)
-    adv_ref[:, :128] = left[...]
-    adv_ref[:, 128:] = right[...]
 
 
 def advance(c2d, k, rate, faces):
@@ -162,15 +158,13 @@
     return pl.pallas_call(
         advance_kernel,
         grid=(1,),
-        out_shape=jax.ShapeDtypeStruct((NS * NX, NV), f32),
+        out_shape=[jax.ShapeDtypeStruct((NS * NX, 128), f32)] * 2,
         in_specs=halves(c2d) + [whole_block(v.shape) for v in small],
-        out_specs=whole_block((NS * NX, NV)),
+        out_specs=[whole_block((NS * NX, 128))] * 2,
         scratch_shapes=[
             pltpu.VMEM((NX + 4, NS, NV + NH), f32),
             pltpu.VMEM((NX + 2, NS, NV + NH), f32),
             pltpu.VMEM((NX + 16, NV + NH), f32),
-            pltpu.VMEM((NS * NX, 128), f32),
-            pltpu.VMEM((NS * NX, 128), f32),
         ],
         compiler_params=pltpu.CompilerParams(vmem_limit_bytes=16 * 2**20),
         cost_estimate=pl.CostEstimate(flops=10000000000, bytes_accessed=4 * 2**20, transcendentals=0),
@@ -178,7 +172,23 @@
     )(c2d, c2d, *small)
 
 
-def reduce_kernel(a0_ref, a1_ref, fs_ref, whole_ref, planes_ref):
+def reduce_kernel(a0_ref, a1_ref, k_ref, rate_ref, kxl_ref, kxh_ref, kyl_ref, kyh_ref, cl_ref, ch_ref, fs_ref, whole_ref,
+                  adv_ref, planes_ref, left, right):
+    left[...], right[...] = a0_ref[...], a1_ref[...]
+    rate = jnp.broadcast_to(rate_ref[...], (NS, 128))
+    first_y, last_y = lanes(NS) < NZ, lanes(NS) >= 128 - NZ
+    for x, at, kx_ref in ((0, 0, kxh_ref), (NX - 1, NS, kxl_ref)):
+        cut = pl.ds(x, NS, stride=NX)
+        for ref, own, corner_ref, ky_ref, turn, mask in (
+            (left, slice(0, 128), ch_ref, kyh_ref, 32, first_y),
+            (right, slice(128, 256), cl_ref, kyl_ref, 96, last_y),
+        ):
+            paths = kx_ref[0:1, own] + pltpu.roll(jnp.broadcast_to(ky_ref[x : x + 1, :], (8, 128)), turn, 1)[0:1, :]
+            term = (rate * k_ref[x : x + 1, own]) * (rate * paths) * pltpu.roll(corner_ref[at : at + NS, :], turn, 1)
+            ref[cut, :] = ref[cut, :] + jnp.where(mask, term, 0.0)
+    adv_ref[:, :128] = left[...]
+    adv_ref[:, 128:] = right[...]
+
     lane_q = lanes(NQ)
     low_q, even_q = lane_q < 64, (lane_q & 32) == 0
     fs_hi, fs_lo = split_2(fs_ref[...])
@@ -188,7 +198,7 @@
         rows = []
         for g in range(4):
             cut = pl.ds(group * 4 + g, NS, stride=NX)
-            hi, lo = split_2(jnp.concatenate([a0_ref[cut, :], a1_ref[cut, :]], axis=1))
+            hi, lo = split_2(jnp.concatenate([left[cut, :], right[cut, :]], axis=1))
             stacked = jnp.concatenate([hi, lo, hi, lo], axis=0)
             rows.append(jnp.dot(weights, stacked, preferred_element_type=f32))
         swapped = []
@@ -207,16 +217,23 @@
     lax.fori_loop(0, NX // 4, four_rows, 0, unroll=U3)
 
 
-def reduce_species(advanced, fs, whole):
+def reduce_species(sides, k, rate, faces, corner, fs, whole):
+    xl, xh, yl, yh = faces
+    tail_x, tail_y = pl.BlockSpec((8, NV), lambda i: (2 * NS // 8, 0)), pl.BlockSpec((NX, 128), lambda i: (NS // 2, 0))
+    shapes = [(NS * NX, NV), (NZ * NX, 128)]
     return pl.pallas_call(
         reduce_kernel,
         grid=(1,),
-        out_shape=jax.ShapeDtypeStruct((NZ * NX, 128), f32),
-        in_specs=halves(advanced) + [whole_block(fs.shape), pl.BlockSpec(memory_space=pl.ANY)],
-        out_specs=whole_block((NZ * NX, 128)),
-        compiler_params=pltpu.CompilerParams(vmem_limit_bytes=8 * 2**20),
+        out_shape=[jax.ShapeDtypeStruct(s, f32) for s in shapes],
+        in_specs=[whole_block(v.shape) for v in (*sides, k, rate)]
+        + [tail_x, tail_x, tail_y, tail_y]
+        + [whole_block(v.shape) for v in (*corner, fs)]
+        + [pl.BlockSpec(memory_space=pl.ANY)],
+        out_specs=[whole_block(s) for s in shapes],
+        scratch_shapes=[pltpu.VMEM((NS * NX, 128), f32)] * 2,
+        compiler_params=pltpu.CompilerParams(vmem_limit_bytes=12 * 2**20),
         name="reduce_species",
-    )(advanced, advanced, fs, whole)
+    )(*sides, k, rate, xl, xh, yl, yh, *corner, fs, whole)
 
 
 def shift_to(v, dx, dy):
@@ -236,10 +253,11 @@
     xl, xh, yl, yh = (shift_to(v, dx, dy) for v, (dx, dy) in zip(faces, [(-1, 0), (1, 0), (0, -1), (0, 1)]))
     lo, hi = corners(xl, xh)
     copies = copies_of(factor_x, n_tx, xh)
-    faces = xl, xh, yl, yh, shift_to(lo, 0, -1), shift_to(hi, 0, 1)
+    corner = shift_to(lo, 0, -1), shift_to(hi, 0, 1)
     whole_x = lax.all_to_all(copies, "tx", 0, 0, tiled=True).reshape(-1, factor_x.shape[1])
-    advanced = advance(c2d, cell_factor, species_rate[:, None], faces)
-    planes = reduce_species(advanced, factor_species.T, whole_x)
+    faces, rate = (xl, xh, yl, yh), species_rate[:, None]
+    sides = advance(c2d, cell_factor, rate, faces)
+    advanced, planes = reduce_species(sides, cell_factor, rate, faces, corner, factor_species.T, whole_x)
     planes = planes.reshape(depth, cells_x, cells_y * ranks_q)
     planes = lax.all_to_all(planes, "tx", 0, 0, tiled=True).reshape(-1, cells_y * ranks_q)
     first = lax.dot_general(planes, whole_x, (((0,), (0,)), ((), ())), precision=exact_mode)

time: 132 us -> 138 us (1.045)
  waiting for transfers between devices: 4.12 us -> 16.8 us
  starting transfers between devices: 28.7 us -> 26.5 us
  blocking collectives: 81.2 us -> 79.1 us
    ppermute x6, waiting for transfers between devices: 0.92 us -> 16.8 us  [shift_to(): lax.ppermute(v, axis, [(i, i + step) for i in range(count) if 0 <= i + st...]
    ppermute x6, starting transfers between devices: 21.3 us -> 18 us  [shift_to(): lax.ppermute(v, axis, [(i, i + step) for i in range(count) if 0 <= i + st...]
    all_to_all x1, waiting for transfers between devices: 3.2 us -> 0.01 us  [body(): lax.all_to_all(copies, 'tx', 0, 0, tiled=True)]
    all_to_all x1, blocking collectives: 29.1 us -> 26.5 us  [body(): came = lax.all_to_all(sent, 'ty', 0, 0, tiled=True)]
    unnamed x19 -> x17, local copies, waits for them, and re-layouts: 4.07 us -> 2.84 us
  transfers between devices with their start and end apart: 7 -> 7, of which waited for: 2 -> 2; matrix products, arithmetic and copies ran while one was open for 0% -> 0% of each run, Pallas kernels for 6% -> 5%
where the time goes in v6:
time: 138 us
  blocking collectives  79.1 us (57%)
  starting transfers between devices  26.5 us (19%)
  waiting for transfers between devices  16.8 us (12%)
  Pallas kernels  9.14 us (7%)
  local copies, waits for them, and re-layouts  4.29 us (3%)
    all_to_all x1, blocking collectives, body(): core = lax.all_to_all(plane, ('tx', 'ty'), 0, 0, tiled=True)  29.4 us
    all_to_all x1, blocking collectives, body(): came = lax.all_to_all(sent, 'ty', 0, 0, tiled=True)  26.5 us
    all_to_all x1, blocking collectives, body(): lax.all_to_all(planes, 'tx', 0, 0, tiled=True)  23.2 us
    ppermute x6, starting transfers between devices, shift_to(): lax.ppermute(v, axis, [(i, i + step) for i in range(count) if 0 <= i + st...  18 us
    ppermute x6, waiting for transfers between devices, shift_to(): lax.ppermute(v, axis, [(i, i + step) for i in range(count) if 0 <= i + st...  16.8 us
    all_to_all x1, starting transfers between devices, body(): lax.all_to_all(copies, 'tx', 0, 0, tiled=True)  8.54 us
    pallas_call x1, Pallas kernels, advance(): pl.pallas_call(advance_kernel, grid=(1,), out_shape=[jax.ShapeDtypeStruct...  5.93 us
    unnamed x17, local copies, waits for them, and re-layouts  2.84 us
  transfers between devices with their start and end apart: 7, of which 2 were waited for; matrix products, arithmetic and copies ran while one was open for 0% of the time, Pallas kernels for 5%

profile of v6, /device:TPU:1, one launch (start us, length us, event | category | flops | bytes accessed | tf_op | source)
XLA Modules:
  0.0 137.9 jit_solution(8048166156814563932)
XLA Ops:
  0.6 1.2 copy-done
  1.9 0.8 copy-done.2
  2.6 0.7 pack_faces.1
  3.4 1.4 %collective-permute-start.2 = (f32[544,128]{1,0:T(8,128)S(1)}, f32[544,128]{1,0:T(8,128)S(1)}, u32[]{:S(2)}, u32[]{:S(2)}) collective-permute-start(f32[544,128]{1,0:T(8,128)S(1)} %get-tuple-element.14), channel_id=1, source_target_pairs={{1,0},{2,1},{3,2},{4,3},{5,4},{6,5},{7,6},{8,7},{9,8},{10,9},{11,1... | collective-permute-start | bytes 835592 | tf_op jit(solution)/shard_map/ppermute | solution.py:242
  4.8 4.6 %collective-permute-start.3 = (f32[544,128]{1,0:T(8,128)S(1)}, f32[544,128]{1,0:T(8,128)S(1)}, u32[]{:S(2)}, u32[]{:S(2)}) collective-permute-start(f32[544,128]{1,0:T(8,128)S(1)} %get-tuple-element.15), channel_id=1, source_target_pairs={{0,1},{1,2},{2,3},{3,4},{4,5},{5,6},{6,7},{7,8},{8,9},{9,10},{10,1... | collective-permute-start | bytes 835592 | tf_op jit(solution)/shard_map/ppermute | solution.py:242
  9.4 4.6 %collective-permute-start.1 = (f32[72,256]{1,0:T(8,128)S(1)}, f32[72,256]{1,0:T(8,128)S(1)}, u32[]{:S(2)}, u32[]{:S(2)}) collective-permute-start(f32[72,256]{1,0:T(8,128)S(1)} %get-tuple-element.13), channel_id=1, source_target_pairs={{0,16},{16,32},{32,48},{48,64},{64,80},{80,96},{96,112},{112,128},... | collective-permute-start | bytes 221192 | tf_op jit(solution)/shard_map/ppermute | solution.py:242
  14.0 4.3 %collective-permute-done.1.xh_ref.after_ref.kxh_ref = f32[72,256]{1,0:T(8,128)S(1)} collective-permute-done((f32[72,256]{1,0:T(8,128)S(1)}, f32[72,256]{1,0:T(8,128)S(1)}, u32[]{:S(2)}, u32[]{:S(2)}) %collective-permute-start.1) | collective-permute-done | bytes 73760 | tf_op jit(solution)/shard_map/ppermute | solution.py:242
  18.3 0.9 copies_of_factor.1
  19.1 8.5 %all-to-all-start = ((f32[32,32,128]{2,1,0:T(8,128)}), f32[32,32,128]{2,1,0:T(8,128)S(1)}, u32[]{:S(2)}, u32[]{:S(2)}) async-start(f32[32,32,128]{2,1,0:T(8,128)} %copies_of_factor.1), calls=%async_computation | async-start | bytes 1048576 | tf_op jit(solution)/shard_map/all_to_all | solution.py:257
  27.7 2.1 %collective-permute-start = (f32[72,256]{1,0:T(8,128)S(1)}, f32[72,256]{1,0:T(8,128)S(1)}, u32[]{:S(2)}, u32[]{:S(2)}) collective-permute-start(f32[72,256]{1,0:T(8,128)S(1)} %get-tuple-element.12), channel_id=1, source_target_pairs={{16,0},{32,16},{48,32},{64,48},{80,64},{96,80},{112,96},{128,112},... | collective-permute-start | bytes 221192 | tf_op jit(solution)/shard_map/ppermute | solution.py:242
  30.0 12.5 %collective-permute-done.xl_ref.kxl_ref = f32[72,256]{1,0:T(8,128)S(1)} collective-permute-done((f32[72,256]{1,0:T(8,128)S(1)}, f32[72,256]{1,0:T(8,128)S(1)}, u32[]{:S(2)}, u32[]{:S(2)}) %collective-permute-start) | collective-permute-done | bytes 73760 | tf_op jit(solution)/shard_map/ppermute | solution.py:242
  42.4 1.3 collective-permute-start.4
  43.7 4.0 %collective-permute-start.5 = (f32[64,128]{1,0:T(8,128)S(1)}, f32[64,128]{1,0:T(8,128)S(1)}, u32[]{:S(2)}, u32[]{:S(2)}) collective-permute-start(f32[64,128]{1,0:T(8,128)S(1)} %get-tuple-element.19), channel_id=1, source_target_pairs={{0,1},{1,2},{2,3},{3,4},{4,5},{5,6},{6,7},{7,8},{8,9},{9,10},{10,1... | collective-permute-start | bytes 98312 | tf_op jit(solution)/shard_map/ppermute | solution.py:242
  47.8 5.9 %advance_twice.1 = (f32[1024,128]{1,0:T(8,128)S(1)}, f32[1024,128]{1,0:T(8,128)S(1)}) custom-call(f32[1024,256]{1,0:T(8,128)S(1)} %bitcast.46, f32[1024,256]{1,0:T(8,128)S(1)} %bitcast.47, f32[32,256]{1,0:T(8,128)S(1)} %copy-done.3, f32[32,1]{1,0:T(8,128)S(1)} %copy.22.rate_ref, f32[72,256]{1,0:T(8,128)S(1)} %collective-permute-done.xl_ref.kxl_ref, ...), custom_call_target="tpu_custom_call" | custom-call | flops 10000000000 | bytes 4194304 | tf_op jit(solution)/shard_map/advance_twice/pallas_call | solution.py:158
  53.8 1.6 %reduce_species.1 = (f32[1024,256]{1,0:T(8,128)}, f32[1024,128]{1,0:T(8,128)S(1)}) custom-call(f32[1024,128]{1,0:T(8,128)S(1)} %get-tuple-element.16.a0_ref, f32[1024,128]{1,0:T(8,128)S(1)} %get-tuple-element.17.a1_ref, f32[32,256]{1,0:T(8,128)S(1)} %copy-done.3, f32[32,1]{1,0:T(8,128)S(1)} %copy.22.rate_ref, ...), custom_call_target="tpu_custom_call" | custom-call | tf_op jit(solution)/shard_map/reduce_species/pallas_call | solution.py:224
  55.4 23.2 %all_to_all.20 = f32[32,32,128]{2,1,0:T(8,128)S(1)} all-to-all(f32[32,32,128]{2,1,0:T(8,128)S(1)} %bitcast.48), channel_id=1, replica_groups=mesh['tx'=32,'ty'=16] {'tx'}, dimensions={0} | all-to-all | bytes 1048576 | tf_op jit(solution)/shard_map/all_to_all | solution.py:262
  78.8 0.6 convolution_bitcast_fusion.1
  79.5 26.5 %all_to_all.21 = f32[16,16,128]{2,1,0:T(8,128)S(1)} all-to-all(f32[16,16,128]{2,1,0:T(8,128)S(1)} %copy.25), channel_id=1, replica_groups=mesh['tx'=32,'ty'=16] {'ty'}, dimensions={0} | all-to-all | bytes 262144 | tf_op jit(solution)/shard_map/all_to_all | solution.py:266
  106.2 0.5 convolution_bitcast_fusion
  106.7 0.2 copy.30
  106.9 0.3 reshape.47
  107.3 29.4 %all_to_all.22 = f32[512,1,32]{2,1,0:T(1,128)S(1)} all-to-all(f32[512,1,32]{2,1,0:T(1,128)S(1)} %copy.31), channel_id=1, replica_groups=mesh['tx'=32,'ty'=16] {'tx','ty'}, dimensions={0} | all-to-all | bytes 131072 | tf_op jit(solution)/shard_map/all_to_all | solution.py:273
  136.8 0.2 reshape.48
  137.1 0.8 copy.33
  (30 shorter events, 0.8 us)
Async XLA Ops:
  0.6 1.2 copy-start
  1.9 0.8 copy-start.2
  2.6 15.7 %copy-start.4 = (f32[32,128]{1,0:T(8,128)S(1)}, f32[32,128]{1,0:T(8,128)}, u32[]{:S(2)}) copy-start(f32[32,128]{1,0:T(8,128)} %v_ref.1) | copy-start | bytes 49156
  3.4 44.4 %copy-start.1 = (f32[32,32,256]{2,1,0:T(8,128)S(1)}, f32[32,32,256]{2,1,0:T(8,128)}, u32[]{:S(2)}) copy-start(f32[32,32,256]{2,1,0:T(8,128)} %param.6) | copy-start | bytes 3145732
  3.4 44.4 %collective-permute-start.2 = (f32[544,128]{1,0:T(8,128)S(1)}, f32[544,128]{1,0:T(8,128)S(1)}, u32[]{:S(2)}, u32[]{:S(2)}) collective-permute-start(f32[544,128]{1,0:T(8,128)S(1)} %get-tuple-element.14), channel_id=1, source_target_pairs={{1,0},{2,1},{3,2},{4,3},{5,4},{6,5},{7,6},{8,7},{9,8},{10,9},{11,1... | collective-permute-start | bytes 835592 | tf_op jit(solution)/shard_map/ppermute | solution.py:242
  4.8 42.9 %collective-permute-start.3 = (f32[544,128]{1,0:T(8,128)S(1)}, f32[544,128]{1,0:T(8,128)S(1)}, u32[]{:S(2)}, u32[]{:S(2)}) collective-permute-start(f32[544,128]{1,0:T(8,128)S(1)} %get-tuple-element.15), channel_id=1, source_target_pairs={{0,1},{1,2},{2,3},{3,4},{4,5},{5,6},{6,7},{7,8},{8,9},{9,10},{10,1... | collective-permute-start | bytes 835592 | tf_op jit(solution)/shard_map/ppermute | solution.py:242
  9.4 8.9 %collective-permute-start.1 = (f32[72,256]{1,0:T(8,128)S(1)}, f32[72,256]{1,0:T(8,128)S(1)}, u32[]{:S(2)}, u32[]{:S(2)}) collective-permute-start(f32[72,256]{1,0:T(8,128)S(1)} %get-tuple-element.13), channel_id=1, source_target_pairs={{0,16},{16,32},{32,48},{48,64},{64,80},{80,96},{96,112},{112,128},... | collective-permute-start | bytes 221192 | tf_op jit(solution)/shard_map/ppermute | solution.py:242
  19.1 34.6 %all-to-all-start = ((f32[32,32,128]{2,1,0:T(8,128)}), f32[32,32,128]{2,1,0:T(8,128)S(1)}, u32[]{:S(2)}, u32[]{:S(2)}) async-start(f32[32,32,128]{2,1,0:T(8,128)} %copies_of_factor.1), calls=%async_computation | async-start | bytes 1048576 | tf_op jit(solution)/shard_map/all_to_all | solution.py:257
  27.7 2.2 %copy-start.7 = (f32[32]{0:T(128)S(1)}, f32[32]{0:T(128)}, u32[]{:S(2)}) copy-start(f32[32]{0:T(128)} %param.8) | copy-start | bytes 388
  27.7 14.7 %collective-permute-start = (f32[72,256]{1,0:T(8,128)S(1)}, f32[72,256]{1,0:T(8,128)S(1)}, u32[]{:S(2)}, u32[]{:S(2)}) collective-permute-start(f32[72,256]{1,0:T(8,128)S(1)} %get-tuple-element.12), channel_id=1, source_target_pairs={{16,0},{32,16},{48,32},{64,48},{80,64},{96,80},{112,96},{128,112},... | collective-permute-start | bytes 221192 | tf_op jit(solution)/shard_map/ppermute | solution.py:242
  30.0 17.8 %copy-start.3 = (f32[32,256]{1,0:T(8,128)S(1)}, f32[32,256]{1,0:T(8,128)}, u32[]{:S(2)}) copy-start(f32[32,256]{1,0:T(8,128)} %k_ref.5) | copy-start | bytes 98308
  42.4 11.3 %collective-permute-start.4 = (f32[64,128]{1,0:T(8,128)S(1)}, f32[64,128]{1,0:T(8,128)S(1)}, u32[]{:S(2)}, u32[]{:S(2)}) collective-permute-start(f32[64,128]{1,0:T(8,128)S(1)} %get-tuple-element.18), channel_id=1, source_target_pairs={{1,0},{2,1},{3,2},{4,3},{5,4},{6,5},{7,6},{8,7},{9,8},{10,9},{11,1... | collective-permute-start | bytes 98312 | tf_op jit(solution)/shard_map/ppermute | solution.py:242
  43.7 10.0 %collective-permute-start.5 = (f32[64,128]{1,0:T(8,128)S(1)}, f32[64,128]{1,0:T(8,128)S(1)}, u32[]{:S(2)}, u32[]{:S(2)}) collective-permute-start(f32[64,128]{1,0:T(8,128)S(1)} %get-tuple-element.19), channel_id=1, source_target_pairs={{0,1},{1,2},{2,3},{3,4},{4,5},{5,6},{6,7},{7,8},{8,9},{9,10},{10,1... | collective-permute-start | bytes 98312 | tf_op jit(solution)/shard_map/ppermute | solution.py:242
  47.8 6.0 %copy-start.5 = (f32[32,16]{0,1:T(8,128)S(1)}, f32[32,16]{0,1:T(8,128)}, u32[]{:S(2)}) copy-start(f32[32,16]{0,1:T(8,128)} %param.11) | copy-start | bytes 6148
  78.8 0.7 copy-start.6

commit v7 on v6

--- a/solution.py
+++ b/solution.py
@@ -74,7 +74,7 @@
     )(xl, xh)
 
 
-def copies_kernel(v_ref, after_ref, out_ref):
+def copies_kernel(v_ref, after0_ref, after1_ref, out_ref):
     out_ref[...] = jnp.broadcast_to(v_ref[...][None], out_ref.shape)
 
 
@@ -83,11 +83,11 @@
         copies_kernel,
         grid=(1,),
         out_shape=jax.ShapeDtypeStruct((count,) + v.shape, f32),
-        in_specs=[whole_block(v.shape), pl.BlockSpec(memory_space=pl.ANY)],
+        in_specs=[whole_block(v.shape)] + [pl.BlockSpec(memory_space=pl.ANY)] * 2,
         out_specs=whole_block((count,) + v.shape),
         compiler_params=pltpu.CompilerParams(vmem_limit_bytes=4 * 2**20),
         name="copies_of_factor",
-    )(v, after)
+    )(v, *after)
 
 
 def split_2(v):
@@ -252,7 +252,7 @@
     faces = pack(c2d, cell_factor)
     xl, xh, yl, yh = (shift_to(v, dx, dy) for v, (dx, dy) in zip(faces, [(-1, 0), (1, 0), (0, -1), (0, 1)]))
     lo, hi = corners(xl, xh)
-    copies = copies_of(factor_x, n_tx, xh)
+    copies = copies_of(factor_x, n_tx, (xl, xh))
     corner = shift_to(lo, 0, -1), shift_to(hi, 0, 1)
     whole_x = lax.all_to_all(copies, "tx", 0, 0, tiled=True).reshape(-1, factor_x.shape[1])
     faces, rate = (xl, xh, yl, yh), species_rate[:, None]

time: 138 us -> 128 us (0.928)
  waiting for transfers between devices: 16.8 us -> 5.88 us
  starting transfers between devices: 26.5 us -> 29.2 us
  blocking collectives: 79.1 us -> 76.7 us
    ppermute x6, waiting for transfers between devices: 16.8 us -> 1.39 us  [shift_to(): lax.ppermute(v, axis, [(i, i + step) for i in range(count) if 0 <= i + st...]
    all_to_all x1, waiting for transfers between devices: 0.01 us -> 4.5 us  [body(): lax.all_to_all(copies, 'tx', 0, 0, tiled=True)]
    ppermute x6, starting transfers between devices: 18 us -> 22 us  [shift_to(): lax.ppermute(v, axis, [(i, i + step) for i in range(count) if 0 <= i + st...]
    all_to_all x1, blocking collectives: 23.2 us -> 21.5 us  [body(): lax.all_to_all(planes, 'tx', 0, 0, tiled=True)]
where the time goes in v7:
time: 128 us
  blocking collectives  76.7 us (60%)
  starting transfers between devices  29.2 us (23%)
  Pallas kernels  9.13 us (7%)
  waiting for transfers between devices  5.88 us (5%)
  local copies, waits for them, and re-layouts  4.94 us (4%)
    all_to_all x1, blocking collectives, body(): core = lax.all_to_all(plane, ('tx', 'ty'), 0, 0, tiled=True)  29.4 us
    all_to_all x1, blocking collectives, body(): came = lax.all_to_all(sent, 'ty', 0, 0, tiled=True)  25.7 us
    ppermute x6, starting transfers between devices, shift_to(): lax.ppermute(v, axis, [(i, i + step) for i in range(count) if 0 <= i + st...  22 us
    all_to_all x1, blocking collectives, body(): lax.all_to_all(planes, 'tx', 0, 0, tiled=True)  21.5 us
    all_to_all x1, starting transfers between devices, body(): lax.all_to_all(copies, 'tx', 0, 0, tiled=True)  7.27 us
    pallas_call x1, Pallas kernels, advance(): pl.pallas_call(advance_kernel, grid=(1,), out_shape=[jax.ShapeDtypeStruct...  5.94 us
    all_to_all x1, waiting for transfers between devices, body(): lax.all_to_all(copies, 'tx', 0, 0, tiled=True)  4.5 us
    unnamed x17, local copies, waits for them, and re-layouts  3.49 us
  transfers between devices with their start and end apart: 7, of which 2 were waited for; matrix products, arithmetic and copies ran while one was open for 0% of the time, Pallas kernels for 5%

profile of v7, /device:TPU:1, one launch (start us, length us, event | category | flops | bytes accessed | tf_op | source)
XLA Modules:
  0.0 127.9 jit_solution(11050576056306955137)
XLA Ops:
  0.6 1.2 copy-done
  1.9 0.8 copy-done.2
  2.6 0.7 pack_faces.1
  3.4 1.4 %collective-permute-start.2 = (f32[544,128]{1,0:T(8,128)S(1)}, f32[544,128]{1,0:T(8,128)S(1)}, u32[]{:S(2)}, u32[]{:S(2)}) collective-permute-start(f32[544,128]{1,0:T(8,128)S(1)} %get-tuple-element.14), channel_id=1, source_target_pairs={{1,0},{2,1},{3,2},{4,3},{5,4},{6,5},{7,6},{8,7},{9,8},{10,9},{11,1... | collective-permute-start | bytes 835592 | tf_op jit(solution)/shard_map/ppermute | solution.py:242
  4.8 4.6 %collective-permute-start.3 = (f32[544,128]{1,0:T(8,128)S(1)}, f32[544,128]{1,0:T(8,128)S(1)}, u32[]{:S(2)}, u32[]{:S(2)}) collective-permute-start(f32[544,128]{1,0:T(8,128)S(1)} %get-tuple-element.15), channel_id=1, source_target_pairs={{0,1},{1,2},{2,3},{3,4},{4,5},{5,6},{6,7},{7,8},{8,9},{9,10},{10,1... | collective-permute-start | bytes 835592 | tf_op jit(solution)/shard_map/ppermute | solution.py:242
  9.4 8.8 %collective-permute-start = (f32[72,256]{1,0:T(8,128)S(1)}, f32[72,256]{1,0:T(8,128)S(1)}, u32[]{:S(2)}, u32[]{:S(2)}) collective-permute-start(f32[72,256]{1,0:T(8,128)S(1)} %get-tuple-element.12), channel_id=1, source_target_pairs={{16,0},{32,16},{48,32},{64,48},{80,64},{96,80},{112,96},{128,112},... | collective-permute-start | bytes 221192 | tf_op jit(solution)/shard_map/ppermute | solution.py:242
  18.2 1.9 %collective-permute-start.1 = (f32[72,256]{1,0:T(8,128)S(1)}, f32[72,256]{1,0:T(8,128)S(1)}, u32[]{:S(2)}, u32[]{:S(2)}) collective-permute-start(f32[72,256]{1,0:T(8,128)S(1)} %get-tuple-element.13), channel_id=1, source_target_pairs={{0,16},{16,32},{32,48},{48,64},{64,80},{80,96},{96,112},{112,128},... | collective-permute-start | bytes 221192 | tf_op jit(solution)/shard_map/ppermute | solution.py:242
  20.1 1.4 %collective-permute-done.1.xh_ref.after1_ref.kxh_ref = f32[72,256]{1,0:T(8,128)S(1)} collective-permute-done((f32[72,256]{1,0:T(8,128)S(1)}, f32[72,256]{1,0:T(8,128)S(1)}, u32[]{:S(2)}, u32[]{:S(2)}) %collective-permute-start.1) | collective-permute-done | bytes 73760 | tf_op jit(solution)/shard_map/ppermute | solution.py:242
  21.5 0.9 copies_of_factor.1
  22.3 7.3 %all-to-all-start = ((f32[32,32,128]{2,1,0:T(8,128)}), f32[32,32,128]{2,1,0:T(8,128)S(1)}, u32[]{:S(2)}, u32[]{:S(2)}) async-start(f32[32,32,128]{2,1,0:T(8,128)} %copies_of_factor.1), calls=%async_computation | async-start | bytes 1048576 | tf_op jit(solution)/shard_map/all_to_all | solution.py:257
  29.6 0.6 copy-done.7
  30.4 1.3 %collective-permute-start.4 = (f32[64,128]{1,0:T(8,128)S(1)}, f32[64,128]{1,0:T(8,128)S(1)}, u32[]{:S(2)}, u32[]{:S(2)}) collective-permute-start(f32[64,128]{1,0:T(8,128)S(1)} %get-tuple-element.18), channel_id=1, source_target_pairs={{1,0},{2,1},{3,2},{4,3},{5,4},{6,5},{7,6},{8,7},{9,8},{10,9},{11,1... | collective-permute-start | bytes 98312 | tf_op jit(solution)/shard_map/ppermute | solution.py:242
  31.7 4.0 %collective-permute-start.5 = (f32[64,128]{1,0:T(8,128)S(1)}, f32[64,128]{1,0:T(8,128)S(1)}, u32[]{:S(2)}, u32[]{:S(2)}) collective-permute-start(f32[64,128]{1,0:T(8,128)S(1)} %get-tuple-element.19), channel_id=1, source_target_pairs={{0,1},{1,2},{2,3},{3,4},{4,5},{5,6},{6,7},{7,8},{8,9},{9,10},{10,1... | collective-permute-start | bytes 98312 | tf_op jit(solution)/shard_map/ppermute | solution.py:242
  35.7 5.9 %advance_twice.1 = (f32[1024,128]{1,0:T(8,128)S(1)}, f32[1024,128]{1,0:T(8,128)S(1)}) custom-call(f32[1024,256]{1,0:T(8,128)S(1)} %bitcast.46, f32[1024,256]{1,0:T(8,128)S(1)} %bitcast.47, f32[32,256]{1,0:T(8,128)S(1)} %copy-done.3, f32[32,1]{1,0:T(8,128)S(1)} %copy.22.rate_ref, f32[72,256]{1,0:T(8,128)S(1)} %collective-permute-done.xl_ref.after0_ref.kxl_ref, ...), custom_call_target="tpu_custom_call" | custom-call | flops 10000000000 | bytes 4194304 | tf_op jit(solution)/shard_map/advance_twice/pallas_call | solution.py:158
  41.7 4.5 %all-to-all-done = f32[32,32,128]{2,1,0:T(8,128)S(1)} async-done(((f32[32,32,128]{2,1,0:T(8,128)}), f32[32,32,128]{2,1,0:T(8,128)S(1)}, u32[]{:S(2)}, u32[]{:S(2)}) %all-to-all-start) | async-done | bytes 524320 | tf_op jit(solution)/shard_map/all_to_all | solution.py:257
  46.2 1.6 %reduce_species.1 = (f32[1024,256]{1,0:T(8,128)}, f32[1024,128]{1,0:T(8,128)S(1)}) custom-call(f32[1024,128]{1,0:T(8,128)S(1)} %get-tuple-element.16.a0_ref, f32[1024,128]{1,0:T(8,128)S(1)} %get-tuple-element.17.a1_ref, f32[32,256]{1,0:T(8,128)S(1)} %copy-done.3, f32[32,1]{1,0:T(8,128)S(1)} %copy.22.rate_ref, ...), custom_call_target="tpu_custom_call" | custom-call | tf_op jit(solution)/shard_map/reduce_species/pallas_call | solution.py:224
  47.8 21.5 %all_to_all.20 = f32[32,32,128]{2,1,0:T(8,128)S(1)} all-to-all(f32[32,32,128]{2,1,0:T(8,128)S(1)} %bitcast.48), channel_id=1, replica_groups=mesh['tx'=32,'ty'=16] {'tx'}, dimensions={0} | all-to-all | bytes 1048576 | tf_op jit(solution)/shard_map/all_to_all | solution.py:262
  69.5 0.6 convolution_bitcast_fusion.1
  70.3 25.7 %all_to_all.21 = f32[16,16,128]{2,1,0:T(8,128)S(1)} all-to-all(f32[16,16,128]{2,1,0:T(8,128)S(1)} %copy.25), channel_id=1, replica_groups=mesh['tx'=32,'ty'=16] {'ty'}, dimensions={0} | all-to-all | bytes 262144 | tf_op jit(solution)/shard_map/all_to_all | solution.py:266
  96.2 0.5 convolution_bitcast_fusion
  96.7 0.2 copy.30
  96.9 0.3 reshape.47
  97.3 29.4 %all_to_all.22 = f32[512,1,32]{2,1,0:T(1,128)S(1)} all-to-all(f32[512,1,32]{2,1,0:T(1,128)S(1)} %copy.31), channel_id=1, replica_groups=mesh['tx'=32,'ty'=16] {'tx','ty'}, dimensions={0} | all-to-all | bytes 131072 | tf_op jit(solution)/shard_map/all_to_all | solution.py:273
  127.1 0.8 copy.33
  (30 shorter events, 1.1 us)
Async XLA Ops:
  0.6 1.2 copy-start
  1.9 0.8 copy-start.2
  2.6 18.9 %copy-start.4 = (f32[32,128]{1,0:T(8,128)S(1)}, f32[32,128]{1,0:T(8,128)}, u32[]{:S(2)}) copy-start(f32[32,128]{1,0:T(8,128)} %v_ref.1) | copy-start | bytes 49156
  3.4 32.3 %copy-start.1 = (f32[32,32,256]{2,1,0:T(8,128)S(1)}, f32[32,32,256]{2,1,0:T(8,128)}, u32[]{:S(2)}) copy-start(f32[32,32,256]{2,1,0:T(8,128)} %param.6) | copy-start | bytes 3145732
  3.4 32.3 %collective-permute-start.2 = (f32[544,128]{1,0:T(8,128)S(1)}, f32[544,128]{1,0:T(8,128)S(1)}, u32[]{:S(2)}, u32[]{:S(2)}) collective-permute-start(f32[544,128]{1,0:T(8,128)S(1)} %get-tuple-element.14), channel_id=1, source_target_pairs={{1,0},{2,1},{3,2},{4,3},{5,4},{6,5},{7,6},{8,7},{9,8},{10,9},{11,1... | collective-permute-start | bytes 835592 | tf_op jit(solution)/shard_map/ppermute | solution.py:242
  4.8 30.9 %collective-permute-start.3 = (f32[544,128]{1,0:T(8,128)S(1)}, f32[544,128]{1,0:T(8,128)S(1)}, u32[]{:S(2)}, u32[]{:S(2)}) collective-permute-start(f32[544,128]{1,0:T(8,128)S(1)} %get-tuple-element.15), channel_id=1, source_target_pairs={{0,1},{1,2},{2,3},{3,4},{4,5},{5,6},{6,7},{7,8},{8,9},{9,10},{10,1... | collective-permute-start | bytes 835592 | tf_op jit(solution)/shard_map/ppermute | solution.py:242
  9.4 10.7 %collective-permute-start = (f32[72,256]{1,0:T(8,128)S(1)}, f32[72,256]{1,0:T(8,128)S(1)}, u32[]{:S(2)}, u32[]{:S(2)}) collective-permute-start(f32[72,256]{1,0:T(8,128)S(1)} %get-tuple-element.12), channel_id=1, source_target_pairs={{16,0},{32,16},{48,32},{64,48},{80,64},{96,80},{112,96},{128,112},... | collective-permute-start | bytes 221192 | tf_op jit(solution)/shard_map/ppermute | solution.py:242
  18.2 3.3 %collective-permute-start.1 = (f32[72,256]{1,0:T(8,128)S(1)}, f32[72,256]{1,0:T(8,128)S(1)}, u32[]{:S(2)}, u32[]{:S(2)}) collective-permute-start(f32[72,256]{1,0:T(8,128)S(1)} %get-tuple-element.13), channel_id=1, source_target_pairs={{0,16},{16,32},{32,48},{48,64},{64,80},{80,96},{96,112},{112,128},... | collective-permute-start | bytes 221192 | tf_op jit(solution)/shard_map/ppermute | solution.py:242
  22.3 23.8 %all-to-all-start = ((f32[32,32,128]{2,1,0:T(8,128)}), f32[32,32,128]{2,1,0:T(8,128)S(1)}, u32[]{:S(2)}, u32[]{:S(2)}) async-start(f32[32,32,128]{2,1,0:T(8,128)} %copies_of_factor.1), calls=%async_computation | async-start | bytes 1048576 | tf_op jit(solution)/shard_map/all_to_all | solution.py:257
  29.6 0.7 copy-start.7
  30.4 5.3 %copy-start.3 = (f32[32,256]{1,0:T(8,128)S(1)}, f32[32,256]{1,0:T(8,128)}, u32[]{:S(2)}) copy-start(f32[32,256]{1,0:T(8,128)} %k_ref.5) | copy-start | bytes 98308
  30.4 11.3 %collective-permute-start.4 = (f32[64,128]{1,0:T(8,128)S(1)}, f32[64,128]{1,0:T(8,128)S(1)}, u32[]{:S(2)}, u32[]{:S(2)}) collective-permute-start(f32[64,128]{1,0:T(8,128)S(1)} %get-tuple-element.18), channel_id=1, source_target_pairs={{1,0},{2,1},{3,2},{4,3},{5,4},{6,5},{7,6},{8,7},{9,8},{10,9},{11,1... | collective-permute-start | bytes 98312 | tf_op jit(solution)/shard_map/ppermute | solution.py:242
  31.7 10.0 %collective-permute-start.5 = (f32[64,128]{1,0:T(8,128)S(1)}, f32[64,128]{1,0:T(8,128)S(1)}, u32[]{:S(2)}, u32[]{:S(2)}) collective-permute-start(f32[64,128]{1,0:T(8,128)S(1)} %get-tuple-element.19), channel_id=1, source_target_pairs={{0,1},{1,2},{2,3},{3,4},{4,5},{5,6},{6,7},{7,8},{8,9},{9,10},{10,1... | collective-permute-start | bytes 98312 | tf_op jit(solution)/shard_map/ppermute | solution.py:242
  35.7 10.5 %copy-start.5 = (f32[32,16]{0,1:T(8,128)S(1)}, f32[32,16]{0,1:T(8,128)}, u32[]{:S(2)}) copy-start(f32[32,16]{0,1:T(8,128)} %param.11) | copy-start | bytes 6148
  69.5 0.7 copy-start.6

commit v8 on v7

--- a/solution.py
+++ b/solution.py
@@ -7,7 +7,6 @@
 
 exact_mode = lax.Precision.HIGHEST
 f32, bf16 = jnp.float32, jnp.bfloat16
-U1, U2, U3 = 2, 8, 8
 NS, NX, NV, NH, NZ, NQ = 32, 32, 256, 128, 32, 16
 
 
@@ -55,39 +54,24 @@
     )(c2d, c2d, k)
 
 
-def corner_kernel(xl_ref, xh_ref, lo_ref, hi_ref):
+def corner_kernel(xl_ref, xh_ref, fx_ref, lo_ref, hi_ref, copies_ref):
     for at, ref in ((0, xh_ref), (NS, xl_ref)):
         lo_ref[at : at + NS, :] = ref[0:NS, :128]
         hi_ref[at : at + NS, :] = ref[0:NS, 128:]
-
-
-def corners(xl, xh):
-    shapes = [(2 * NS, 128)] * 2
+    copies_ref[...] = jnp.broadcast_to(fx_ref[...][None], copies_ref.shape)
+
+
+def corners(xl, xh, factor_x, count):
+    shapes = [(2 * NS, 128)] * 2 + [(count,) + factor_x.shape]
     return pl.pallas_call(
         corner_kernel,
         grid=(1,),
         out_shape=[jax.ShapeDtypeStruct(s, f32) for s in shapes],
-        in_specs=[whole_block(v.shape) for v in (xl, xh)],
+        in_specs=[whole_block(v.shape) for v in (xl, xh, factor_x)],
         out_specs=[whole_block(s) for s in shapes],
         compiler_params=pltpu.CompilerParams(vmem_limit_bytes=4 * 2**20),
         name="corner_columns",
-    )(xl, xh)
-
-
-def copies_kernel(v_ref, after0_ref, after1_ref, out_ref):
-    out_ref[...] = jnp.broadcast_to(v_ref[...][None], out_ref.shape)
-
-
-def copies_of(v, count, after):
-    return pl.pallas_call(
-        copies_kernel,
-        grid=(1,),
-        out_shape=jax.ShapeDtypeStruct((count,) + v.shape, f32),
-        in_specs=[whole_block(v.shape)] + [pl.BlockSpec(memory_space=pl.ANY)] * 2,
-        out_specs=whole_block((count,) + v.shape),
-        compiler_params=pltpu.CompilerParams(vmem_limit_bytes=4 * 2**20),
-        name="copies_of_factor",
-    )(v, *after)
+    )(xl, xh, factor_x)
 
 
 def split_2(v):
@@ -143,14 +127,14 @@
             e1[x, :, i * 128 : (i + 1) * 128] = v
         return carry
 
-    lax.fori_loop(0, NX + 2, first_step, 0, unroll=U1)
+    lax.fori_loop(0, NX + 2, first_step, 0, unroll=True)
 
     def second_step(x, carry):
         done = step(e1, x + 1, ke[pl.ds(x + 8, 1), :], 2)
         left[pl.ds(x, NS, stride=NX), :], right[pl.ds(x, NS, stride=NX), :] = done
         return carry
 
-    lax.fori_loop(0, NX, second_step, 0, unroll=U2)
+    lax.fori_loop(0, NX, second_step, 0, unroll=True)
 
 
 def advance(c2d, k, rate, faces):
@@ -214,7 +198,7 @@
             planes_ref[pl.ds(group * 4 + g, NZ, stride=NX), :] = turned[g * NZ : (g + 1) * NZ, :]
         return carry
 
-    lax.fori_loop(0, NX // 4, four_rows, 0, unroll=U3)
+    lax.fori_loop(0, NX // 4, four_rows, 0, unroll=True)
 
 
 def reduce_species(sides, k, rate, faces, corner, fs, whole):
@@ -251,8 +235,7 @@
     c2d = species.reshape(nspec * cells_x, merged)
     faces = pack(c2d, cell_factor)
     xl, xh, yl, yh = (shift_to(v, dx, dy) for v, (dx, dy) in zip(faces, [(-1, 0), (1, 0), (0, -1), (0, 1)]))
-    lo, hi = corners(xl, xh)
-    copies = copies_of(factor_x, n_tx, (xl, xh))
+    lo, hi, copies = corners(xl, xh, factor_x, n_tx)
     corner = shift_to(lo, 0, -1), shift_to(hi, 0, 1)
     whole_x = lax.all_to_all(copies, "tx", 0, 0, tiled=True).reshape(-1, factor_x.shape[1])
     faces, rate = (xl, xh, yl, yh), species_rate[:, None]

time: 128 us -> 127 us (level)
  waiting for transfers between devices: 5.88 us -> 7.8 us
  Pallas kernels: 9.13 us -> 7.24 us
  blocking collectives: 76.7 us -> 75 us
    all_to_all x1, waiting for transfers between devices: 4.5 us -> 6.41 us  [body(): lax.all_to_all(copies, 'tx', 0, 0, tiled=True)]
    pallas_call x1, Pallas kernels: 5.94 us -> 4.04 us  [advance(): pl.pallas_call(advance_kernel, grid=(1,), out_shape=[jax.ShapeDtypeStruct...]
    all_to_all x1, blocking collectives: 25.7 us -> 23.9 us  [body(): came = lax.all_to_all(sent, 'ty', 0, 0, tiled=True)]
  transfers between devices with their start and end apart: 7 -> 7, of which waited for: 2 -> 2; matrix products, arithmetic and copies ran while one was open for 0% -> 0% of each run, Pallas kernels for 5% -> 4%
where the time goes in v8:
time: 127 us; the launch traced here: 126 us
  blocking collectives  75 us (59%)
  starting transfers between devices  29.4 us (23%)
  waiting for transfers between devices  7.8 us (6%)
  Pallas kernels  7.24 us (6%)
  local copies, waits for them, and re-layouts  4.93 us (4%)
    all_to_all x1, blocking collectives, body(): core = lax.all_to_all(plane, ('tx', 'ty'), 0, 0, tiled=True)  29.6 us
    all_to_all x1, blocking collectives, body(): came = lax.all_to_all(sent, 'ty', 0, 0, tiled=True)  23.9 us
    ppermute x6, starting transfers between devices, shift_to(): lax.ppermute(v, axis, [(i, i + step) for i in range(count) if 0 <= i + st...  22 us
    all_to_all x1, blocking collectives, body(): lax.all_to_all(planes, 'tx', 0, 0, tiled=True)  21.5 us
    all_to_all x1, starting transfers between devices, body(): lax.all_to_all(copies, 'tx', 0, 0, tiled=True)  7.4 us
    all_to_all x1, waiting for transfers between devices, body(): lax.all_to_all(copies, 'tx', 0, 0, tiled=True)  6.41 us
    pallas_call x1, Pallas kernels, advance(): pl.pallas_call(advance_kernel, grid=(1,), out_shape=[jax.ShapeDtypeStruct...  4.04 us
    unnamed x17, local copies, waits for them, and re-layouts  3.49 us
  transfers between devices with their start and end apart: 7, of which 2 were waited for; matrix products, arithmetic and copies ran while one was open for 0% of the time, Pallas kernels for 4%

profile of v8, /device:TPU:1, one launch (start us, length us, event | category | flops | bytes accessed | tf_op | source)
XLA Modules:
  0.0 126.4 jit_solution(5330994156365103651)
XLA Ops:
  0.6 1.2 copy-done
  1.9 0.8 copy-done.2
  2.6 0.7 pack_faces.1
  3.4 1.4 %collective-permute-start.2 = (f32[544,128]{1,0:T(8,128)S(1)}, f32[544,128]{1,0:T(8,128)S(1)}, u32[]{:S(2)}, u32[]{:S(2)}) collective-permute-start(f32[544,128]{1,0:T(8,128)S(1)} %get-tuple-element.15), channel_id=1, source_target_pairs={{1,0},{2,1},{3,2},{4,3},{5,4},{6,5},{7,6},{8,7},{9,8},{10,9},{11,1... | collective-permute-start | bytes 835592 | tf_op jit(solution)/shard_map/ppermute | solution.py:226
  4.8 4.6 %collective-permute-start.3 = (f32[544,128]{1,0:T(8,128)S(1)}, f32[544,128]{1,0:T(8,128)S(1)}, u32[]{:S(2)}, u32[]{:S(2)}) collective-permute-start(f32[544,128]{1,0:T(8,128)S(1)} %get-tuple-element.16), channel_id=1, source_target_pairs={{0,1},{1,2},{2,3},{3,4},{4,5},{5,6},{6,7},{7,8},{8,9},{9,10},{10,1... | collective-permute-start | bytes 835592 | tf_op jit(solution)/shard_map/ppermute | solution.py:226
  9.4 8.8 %collective-permute-start = (f32[72,256]{1,0:T(8,128)S(1)}, f32[72,256]{1,0:T(8,128)S(1)}, u32[]{:S(2)}, u32[]{:S(2)}) collective-permute-start(f32[72,256]{1,0:T(8,128)S(1)} %get-tuple-element.13), channel_id=1, source_target_pairs={{16,0},{32,16},{48,32},{64,48},{80,64},{96,80},{112,96},{128,112},... | collective-permute-start | bytes 221192 | tf_op jit(solution)/shard_map/ppermute | solution.py:226
  18.2 1.9 %collective-permute-start.1 = (f32[72,256]{1,0:T(8,128)S(1)}, f32[72,256]{1,0:T(8,128)S(1)}, u32[]{:S(2)}, u32[]{:S(2)}) collective-permute-start(f32[72,256]{1,0:T(8,128)S(1)} %get-tuple-element.14), channel_id=1, source_target_pairs={{0,16},{16,32},{32,48},{48,64},{64,80},{80,96},{96,112},{112,128},... | collective-permute-start | bytes 221192 | tf_op jit(solution)/shard_map/ppermute | solution.py:226
  20.1 1.4 %collective-permute-done.1.xh_ref.kxh_ref = f32[72,256]{1,0:T(8,128)S(1)} collective-permute-done((f32[72,256]{1,0:T(8,128)S(1)}, f32[72,256]{1,0:T(8,128)S(1)}, u32[]{:S(2)}, u32[]{:S(2)}) %collective-permute-start.1) | collective-permute-done | bytes 73760 | tf_op jit(solution)/shard_map/ppermute | solution.py:226
  21.5 0.9 corner_columns.1
  22.3 7.4 %all-to-all-start = ((f32[32,32,128]{2,1,0:T(8,128)}), f32[32,32,128]{2,1,0:T(8,128)S(1)}, u32[]{:S(2)}, u32[]{:S(2)}) async-start(f32[32,32,128]{2,1,0:T(8,128)} %get-tuple-element.21), calls=%async_computation | async-start | bytes 1048576 | tf_op jit(solution)/shard_map/all_to_all | solution.py:240
  29.8 0.6 copy-done.7
  30.5 1.3 %collective-permute-start.4 = (f32[64,128]{1,0:T(8,128)S(1)}, f32[64,128]{1,0:T(8,128)S(1)}, u32[]{:S(2)}, u32[]{:S(2)}) collective-permute-start(f32[64,128]{1,0:T(8,128)S(1)} %get-tuple-element.19), channel_id=1, source_target_pairs={{1,0},{2,1},{3,2},{4,3},{5,4},{6,5},{7,6},{8,7},{9,8},{10,9},{11,1... | collective-permute-start | bytes 98312 | tf_op jit(solution)/shard_map/ppermute | solution.py:226
  31.8 4.0 %collective-permute-start.5 = (f32[64,128]{1,0:T(8,128)S(1)}, f32[64,128]{1,0:T(8,128)S(1)}, u32[]{:S(2)}, u32[]{:S(2)}) collective-permute-start(f32[64,128]{1,0:T(8,128)S(1)} %get-tuple-element.20), channel_id=1, source_target_pairs={{0,1},{1,2},{2,3},{3,4},{4,5},{5,6},{6,7},{7,8},{8,9},{9,10},{10,1... | collective-permute-start | bytes 98312 | tf_op jit(solution)/shard_map/ppermute | solution.py:226
  35.8 4.0 %advance_twice.1 = (f32[1024,128]{1,0:T(8,128)S(1)}, f32[1024,128]{1,0:T(8,128)S(1)}) custom-call(f32[1024,256]{1,0:T(8,128)S(1)} %bitcast.46, f32[1024,256]{1,0:T(8,128)S(1)} %bitcast.47, f32[32,256]{1,0:T(8,128)S(1)} %copy-done.3, f32[32,1]{1,0:T(8,128)S(1)} %copy.22.rate_ref, f32[72,256]{1,0:T(8,128)S(1)} %collective-permute-done.xl_ref.kxl_ref, ...), custom_call_target="tpu_custom_call" | custom-call | flops 10000000000 | bytes 4194304 | tf_op jit(solution)/shard_map/advance_twice/pallas_call | solution.py:142
  39.9 6.4 %all-to-all-done = f32[32,32,128]{2,1,0:T(8,128)S(1)} async-done(((f32[32,32,128]{2,1,0:T(8,128)}), f32[32,32,128]{2,1,0:T(8,128)S(1)}, u32[]{:S(2)}, u32[]{:S(2)}) %all-to-all-start) | async-done | bytes 524320 | tf_op jit(solution)/shard_map/all_to_all | solution.py:240
  46.3 1.6 %reduce_species.1 = (f32[1024,256]{1,0:T(8,128)}, f32[1024,128]{1,0:T(8,128)S(1)}) custom-call(f32[1024,128]{1,0:T(8,128)S(1)} %get-tuple-element.17.a0_ref, f32[1024,128]{1,0:T(8,128)S(1)} %get-tuple-element.18.a1_ref, f32[32,256]{1,0:T(8,128)S(1)} %copy-done.3, f32[32,1]{1,0:T(8,128)S(1)} %copy.22.rate_ref, ...), custom_call_target="tpu_custom_call" | custom-call | tf_op jit(solution)/shard_map/reduce_species/pallas_call | solution.py:208
  47.9 21.5 %all_to_all.20 = f32[32,32,128]{2,1,0:T(8,128)S(1)} all-to-all(f32[32,32,128]{2,1,0:T(8,128)S(1)} %bitcast.48), channel_id=1, replica_groups=mesh['tx'=32,'ty'=16] {'tx'}, dimensions={0} | all-to-all | bytes 1048576 | tf_op jit(solution)/shard_map/all_to_all | solution.py:245
  69.6 0.6 convolution_bitcast_fusion.1
  70.4 23.9 %all_to_all.21 = f32[16,16,128]{2,1,0:T(8,128)S(1)} all-to-all(f32[16,16,128]{2,1,0:T(8,128)S(1)} %copy.25), channel_id=1, replica_groups=mesh['tx'=32,'ty'=16] {'ty'}, dimensions={0} | all-to-all | bytes 262144 | tf_op jit(solution)/shard_map/all_to_all | solution.py:249
  94.5 0.5 convolution_bitcast_fusion
  95.0 0.2 copy.30
  95.2 0.3 reshape.47
  95.6 29.6 %all_to_all.22 = f32[512,1,32]{2,1,0:T(1,128)S(1)} all-to-all(f32[512,1,32]{2,1,0:T(1,128)S(1)} %copy.31), channel_id=1, replica_groups=mesh['tx'=32,'ty'=16] {'tx','ty'}, dimensions={0} | all-to-all | bytes 131072 | tf_op jit(solution)/shard_map/all_to_all | solution.py:256
  125.6 0.8 copy.33
  (29 shorter events, 1.1 us)
Async XLA Ops:
  0.6 1.2 copy-start
  1.9 0.8 copy-start.2
  2.6 18.9 %copy-start.4 = (f32[32,128]{1,0:T(8,128)S(1)}, f32[32,128]{1,0:T(8,128)}, u32[]{:S(2)}) copy-start(f32[32,128]{1,0:T(8,128)} %fx_ref.1) | copy-start | bytes 49156
  3.4 32.5 %copy-start.1 = (f32[32,32,256]{2,1,0:T(8,128)S(1)}, f32[32,32,256]{2,1,0:T(8,128)}, u32[]{:S(2)}) copy-start(f32[32,32,256]{2,1,0:T(8,128)} %param.6) | copy-start | bytes 3145732
  3.4 32.4 %collective-permute-start.2 = (f32[544,128]{1,0:T(8,128)S(1)}, f32[544,128]{1,0:T(8,128)S(1)}, u32[]{:S(2)}, u32[]{:S(2)}) collective-permute-start(f32[544,128]{1,0:T(8,128)S(1)} %get-tuple-element.15), channel_id=1, source_target_pairs={{1,0},{2,1},{3,2},{4,3},{5,4},{6,5},{7,6},{8,7},{9,8},{10,9},{11,1... | collective-permute-start | bytes 835592 | tf_op jit(solution)/shard_map/ppermute | solution.py:226
  4.8 31.0 %collective-permute-start.3 = (f32[544,128]{1,0:T(8,128)S(1)}, f32[544,128]{1,0:T(8,128)S(1)}, u32[]{:S(2)}, u32[]{:S(2)}) collective-permute-start(f32[544,128]{1,0:T(8,128)S(1)} %get-tuple-element.16), channel_id=1, source_target_pairs={{0,1},{1,2},{2,3},{3,4},{4,5},{5,6},{6,7},{7,8},{8,9},{9,10},{10,1... | collective-permute-start | bytes 835592 | tf_op jit(solution)/shard_map/ppermute | solution.py:226
  9.4 10.7 %collective-permute-start = (f32[72,256]{1,0:T(8,128)S(1)}, f32[72,256]{1,0:T(8,128)S(1)}, u32[]{:S(2)}, u32[]{:S(2)}) collective-permute-start(f32[72,256]{1,0:T(8,128)S(1)} %get-tuple-element.13), channel_id=1, source_target_pairs={{16,0},{32,16},{48,32},{64,48},{80,64},{96,80},{112,96},{128,112},... | collective-permute-start | bytes 221192 | tf_op jit(solution)/shard_map/ppermute | solution.py:226
  18.2 3.3 %collective-permute-start.1 = (f32[72,256]{1,0:T(8,128)S(1)}, f32[72,256]{1,0:T(8,128)S(1)}, u32[]{:S(2)}, u32[]{:S(2)}) collective-permute-start(f32[72,256]{1,0:T(8,128)S(1)} %get-tuple-element.14), channel_id=1, source_target_pairs={{0,16},{16,32},{32,48},{48,64},{64,80},{80,96},{96,112},{112,128},... | collective-permute-start | bytes 221192 | tf_op jit(solution)/shard_map/ppermute | solution.py:226
  22.3 13.5 %copy-start.3 = (f32[32,256]{1,0:T(8,128)S(1)}, f32[32,256]{1,0:T(8,128)}, u32[]{:S(2)}) copy-start(f32[32,256]{1,0:T(8,128)} %k_ref.5) | copy-start | bytes 98308
  22.3 24.0 %all-to-all-start = ((f32[32,32,128]{2,1,0:T(8,128)}), f32[32,32,128]{2,1,0:T(8,128)S(1)}, u32[]{:S(2)}, u32[]{:S(2)}) async-start(f32[32,32,128]{2,1,0:T(8,128)} %get-tuple-element.21), calls=%async_computation | async-start | bytes 1048576 | tf_op jit(solution)/shard_map/all_to_all | solution.py:240
  29.8 0.7 copy-start.7
  30.5 9.4 %collective-permute-start.4 = (f32[64,128]{1,0:T(8,128)S(1)}, f32[64,128]{1,0:T(8,128)S(1)}, u32[]{:S(2)}, u32[]{:S(2)}) collective-permute-start(f32[64,128]{1,0:T(8,128)S(1)} %get-tuple-element.19), channel_id=1, source_target_pairs={{1,0},{2,1},{3,2},{4,3},{5,4},{6,5},{7,6},{8,7},{9,8},{10,9},{11,1... | collective-permute-start | bytes 98312 | tf_op jit(solution)/shard_map/ppermute | solution.py:226
  31.8 8.1 %collective-permute-start.5 = (f32[64,128]{1,0:T(8,128)S(1)}, f32[64,128]{1,0:T(8,128)S(1)}, u32[]{:S(2)}, u32[]{:S(2)}) collective-permute-start(f32[64,128]{1,0:T(8,128)S(1)} %get-tuple-element.20), channel_id=1, source_target_pairs={{0,1},{1,2},{2,3},{3,4},{4,5},{5,6},{6,7},{7,8},{8,9},{9,10},{10,1... | collective-permute-start | bytes 98312 | tf_op jit(solution)/shard_map/ppermute | solution.py:226
  35.8 10.5 %copy-start.5 = (f32[32,16]{0,1:T(8,128)S(1)}, f32[32,16]{0,1:T(8,128)}, u32[]{:S(2)}) copy-start(f32[32,16]{0,1:T(8,128)} %param.11) | copy-start | bytes 6148
  69.6 0.7 copy-start.6

commit v9 on v8

--- a/solution.py
+++ b/solution.py
@@ -54,24 +54,23 @@
     )(c2d, c2d, k)
 
 
-def corner_kernel(xl_ref, xh_ref, fx_ref, lo_ref, hi_ref, copies_ref):
+def corner_kernel(xl_ref, xh_ref, lo_ref, hi_ref):
     for at, ref in ((0, xh_ref), (NS, xl_ref)):
         lo_ref[at : at + NS, :] = ref[0:NS, :128]
         hi_ref[at : at + NS, :] = ref[0:NS, 128:]
-    copies_ref[...] = jnp.broadcast_to(fx_ref[...][None], copies_ref.shape)
-
-
-def corners(xl, xh, factor_x, count):
-    shapes = [(2 * NS, 128)] * 2 + [(count,) + factor_x.shape]
+
+
+def corners(xl, xh):
+    shapes = [(2 * NS, 128)] * 2
     return pl.pallas_call(
         corner_kernel,
         grid=(1,),
         out_shape=[jax.ShapeDtypeStruct(s, f32) for s in shapes],
-        in_specs=[whole_block(v.shape) for v in (xl, xh, factor_x)],
+        in_specs=[whole_block(v.shape) for v in (xl, xh)],
         out_specs=[whole_block(s) for s in shapes],
         compiler_params=pltpu.CompilerParams(vmem_limit_bytes=4 * 2**20),
         name="corner_columns",
-    )(xl, xh, factor_x)
+    )(xl, xh)
 
 
 def split_2(v):
@@ -156,7 +155,7 @@
     )(c2d, c2d, *small)
 
 
-def reduce_kernel(a0_ref, a1_ref, k_ref, rate_ref, kxl_ref, kxh_ref, kyl_ref, kyh_ref, cl_ref, ch_ref, fs_ref, whole_ref,
+def reduce_kernel(a0_ref, a1_ref, k_ref, rate_ref, kxl_ref, kxh_ref, kyl_ref, kyh_ref, cl_ref, ch_ref, fs_ref, fx_ref,
                   adv_ref, planes_ref, left, right):
     left[...], right[...] = a0_ref[...], a1_ref[...]
     rate = jnp.broadcast_to(rate_ref[...], (NS, 128))
@@ -172,6 +171,8 @@
             ref[cut, :] = ref[cut, :] + jnp.where(mask, term, 0.0)
     adv_ref[:, :128] = left[...]
     adv_ref[:, 128:] = right[...]
+    for z in range(NZ):
+        planes_ref[(2 * z + 1) * NX : (2 * z + 2) * NX, :] = fx_ref[...]
 
     lane_q = lanes(NQ)
     low_q, even_q = lane_q < 64, (lane_q & 32) == 0
@@ -195,29 +196,28 @@
                 swapped.append(jnp.where(even_q, pltpu.roll(p, 96, 1), r))
         turned = jnp.concatenate(swapped, axis=0).T
         for g in range(4):
-            planes_ref[pl.ds(group * 4 + g, NZ, stride=NX), :] = turned[g * NZ : (g + 1) * NZ, :]
+            planes_ref[pl.ds(group * 4 + g, NZ, stride=2 * NX), :] = turned[g * NZ : (g + 1) * NZ, :]
         return carry
 
     lax.fori_loop(0, NX // 4, four_rows, 0, unroll=True)
 
 
-def reduce_species(sides, k, rate, faces, corner, fs, whole):
+def reduce_species(sides, k, rate, faces, corner, fs, factor_x):
     xl, xh, yl, yh = faces
     tail_x, tail_y = pl.BlockSpec((8, NV), lambda i: (2 * NS // 8, 0)), pl.BlockSpec((NX, 128), lambda i: (NS // 2, 0))
-    shapes = [(NS * NX, NV), (NZ * NX, 128)]
+    shapes = [(NS * NX, NV), (NZ * 2 * NX, 128)]
     return pl.pallas_call(
         reduce_kernel,
         grid=(1,),
         out_shape=[jax.ShapeDtypeStruct(s, f32) for s in shapes],
         in_specs=[whole_block(v.shape) for v in (*sides, k, rate)]
         + [tail_x, tail_x, tail_y, tail_y]
-        + [whole_block(v.shape) for v in (*corner, fs)]
-        + [pl.BlockSpec(memory_space=pl.ANY)],
+        + [whole_block(v.shape) for v in (*corner, fs, factor_x)],
         out_specs=[whole_block(s) for s in shapes],
         scratch_shapes=[pltpu.VMEM((NS * NX, 128), f32)] * 2,
         compiler_params=pltpu.CompilerParams(vmem_limit_bytes=12 * 2**20),
         name="reduce_species",
-    )(*sides, k, rate, xl, xh, yl, yh, *corner, fs, whole)
+    )(*sides, k, rate, xl, xh, yl, yh, *corner, fs, factor_x)
 
 
 def shift_to(v, dx, dy):
@@ -235,15 +235,16 @@
     c2d = species.reshape(nspec * cells_x, merged)
     faces = pack(c2d, cell_factor)
     xl, xh, yl, yh = (shift_to(v, dx, dy) for v, (dx, dy) in zip(faces, [(-1, 0), (1, 0), (0, -1), (0, 1)]))
-    lo, hi, copies = corners(xl, xh, factor_x, n_tx)
+    lo, hi = corners(xl, xh)
     corner = shift_to(lo, 0, -1), shift_to(hi, 0, 1)
-    whole_x = lax.all_to_all(copies, "tx", 0, 0, tiled=True).reshape(-1, factor_x.shape[1])
     faces, rate = (xl, xh, yl, yh), species_rate[:, None]
     sides = advance(c2d, cell_factor, rate, faces)
-    advanced, planes = reduce_species(sides, cell_factor, rate, faces, corner, factor_species.T, whole_x)
-    planes = planes.reshape(depth, cells_x, cells_y * ranks_q)
-    planes = lax.all_to_all(planes, "tx", 0, 0, tiled=True).reshape(-1, cells_y * ranks_q)
-    first = lax.dot_general(planes, whole_x, (((0,), (0,)), ((), ())), precision=exact_mode)
+    advanced, planes = reduce_species(sides, cell_factor, rate, faces, corner, factor_species.T, factor_x)
+    planes = planes.reshape(depth, 2 * cells_x, cells_y * ranks_q)
+    planes = lax.all_to_all(planes, "tx", 0, 0, tiled=True)
+    first = lax.dot_general(
+        planes[:, :cells_x], planes[:, cells_x:], (((0, 1), (0, 1)), ((), ())), precision=exact_mode
+    )
     first = first.reshape(cells_y, ranks_q, -1).transpose(1, 0, 2)
     sent = jnp.concatenate([first, jnp.broadcast_to(factor_y[None], (n_ty,) + factor_y.shape)], axis=1)
     came = lax.all_to_all(sent, "ty", 0, 0, tiled=True)

time: 127 us -> 126 us (level)
  blocking collectives: 75 us -> 90 us
  starting transfers between devices: 29.4 us -> 21.8 us
  waiting for transfers between devices: 7.8 us -> 1.3 us
    all_to_all x1, blocking collectives: 21.5 us -> 34.1 us  [body(): planes = lax.all_to_all(planes, 'tx', 0, 0, tiled=True)]
    all_to_all x1 -> x0, starting transfers between devices: 7.4 us -> none  [body(): lax.all_to_all(copies, 'tx', 0, 0, tiled=True)]
    all_to_all x1 -> x0, waiting for transfers between devices: 6.41 us -> none  [body(): lax.all_to_all(copies, 'tx', 0, 0, tiled=True)]
    all_to_all x1, blocking collectives: 23.9 us -> 26.5 us  [body(): came = lax.all_to_all(sent, 'ty', 0, 0, tiled=True)]
  transfers between devices with their start and end apart: 7 -> 6, of which waited for: 2 -> 1; matrix products, arithmetic and copies ran while one was open for 0% -> 0% of each run, Pallas kernels for 4% -> 3%
where the time goes in v9:
time: 126 us
  blocking collectives  90 us (71%)
  starting transfers between devices  21.8 us (17%)
  Pallas kernels  6.43 us (5%)
  local copies, waits for them, and re-layouts  4.04 us (3%)
  matrix products  1.49 us (1%)
  waiting for transfers between devices  1.3 us (1%)
    all_to_all x1, blocking collectives, body(): planes = lax.all_to_all(planes, 'tx', 0, 0, tiled=True)  34.1 us
    all_to_all x1, blocking collectives, body(): core = lax.all_to_all(plane, ('tx', 'ty'), 0, 0, tiled=True)  29.4 us
    all_to_all x1, blocking collectives, body(): came = lax.all_to_all(sent, 'ty', 0, 0, tiled=True)  26.5 us
    ppermute x6, starting transfers between devices, shift_to(): lax.ppermute(v, axis, [(i, i + step) for i in range(count) if 0 <= i + st...  21.8 us
    pallas_call x1, Pallas kernels, advance(): pl.pallas_call(advance_kernel, grid=(1,), out_shape=[jax.ShapeDtypeStruct...  4.05 us
    unnamed x17, local copies, waits for them, and re-layouts  2.81 us
  transfers between devices with their start and end apart: 6, of which 1 were waited for; matrix products, arithmetic and copies ran while one was open for 0% of the time, Pallas kernels for 3%

profile of v9, /device:TPU:1, one launch (start us, length us, event | category | flops | bytes accessed | tf_op | source)
XLA Modules:
  0.0 126.0 jit_solution(3801994585892300515)
XLA Ops:
  0.6 1.2 copy-done
  1.9 0.8 copy-done.2
  2.6 0.7 pack_faces.1
  3.4 1.3 %collective-permute-start.2 = (f32[544,128]{1,0:T(8,128)S(1)}, f32[544,128]{1,0:T(8,128)S(1)}, u32[]{:S(2)}, u32[]{:S(2)}) collective-permute-start(f32[544,128]{1,0:T(8,128)S(1)} %get-tuple-element.14), channel_id=1, source_target_pairs={{1,0},{2,1},{3,2},{4,3},{5,4},{6,5},{7,6},{8,7},{9,8},{10,9},{11,1... | collective-permute-start | bytes 835592 | tf_op jit(solution)/shard_map/ppermute | solution.py:226
  4.7 4.6 %collective-permute-start.3 = (f32[544,128]{1,0:T(8,128)S(1)}, f32[544,128]{1,0:T(8,128)S(1)}, u32[]{:S(2)}, u32[]{:S(2)}) collective-permute-start(f32[544,128]{1,0:T(8,128)S(1)} %get-tuple-element.15), channel_id=1, source_target_pairs={{0,1},{1,2},{2,3},{3,4},{4,5},{5,6},{6,7},{7,8},{8,9},{9,10},{10,1... | collective-permute-start | bytes 835592 | tf_op jit(solution)/shard_map/ppermute | solution.py:226
  9.3 8.8 %collective-permute-start = (f32[72,256]{1,0:T(8,128)S(1)}, f32[72,256]{1,0:T(8,128)S(1)}, u32[]{:S(2)}, u32[]{:S(2)}) collective-permute-start(f32[72,256]{1,0:T(8,128)S(1)} %get-tuple-element.12), channel_id=1, source_target_pairs={{16,0},{32,16},{48,32},{64,48},{80,64},{96,80},{112,96},{128,112},... | collective-permute-start | bytes 221192 | tf_op jit(solution)/shard_map/ppermute | solution.py:226
  18.0 1.9 %collective-permute-start.1 = (f32[72,256]{1,0:T(8,128)S(1)}, f32[72,256]{1,0:T(8,128)S(1)}, u32[]{:S(2)}, u32[]{:S(2)}) collective-permute-start(f32[72,256]{1,0:T(8,128)S(1)} %get-tuple-element.13), channel_id=1, source_target_pairs={{0,16},{16,32},{32,48},{48,64},{64,80},{80,96},{96,112},{112,128},... | collective-permute-start | bytes 221192 | tf_op jit(solution)/shard_map/ppermute | solution.py:226
  20.1 1.3 %collective-permute-done.1.xh_ref.kxh_ref = f32[72,256]{1,0:T(8,128)S(1)} collective-permute-done((f32[72,256]{1,0:T(8,128)S(1)}, f32[72,256]{1,0:T(8,128)S(1)}, u32[]{:S(2)}, u32[]{:S(2)}) %collective-permute-start.1) | collective-permute-done | bytes 73760 | tf_op jit(solution)/shard_map/ppermute | solution.py:226
  21.4 1.3 %collective-permute-start.4 = (f32[64,128]{1,0:T(8,128)S(1)}, f32[64,128]{1,0:T(8,128)S(1)}, u32[]{:S(2)}, u32[]{:S(2)}) collective-permute-start(f32[64,128]{1,0:T(8,128)S(1)} %get-tuple-element.18), channel_id=1, source_target_pairs={{1,0},{2,1},{3,2},{4,3},{5,4},{6,5},{7,6},{8,7},{9,8},{10,9},{11,1... | collective-permute-start | bytes 98312 | tf_op jit(solution)/shard_map/ppermute | solution.py:226
  22.6 4.0 %collective-permute-start.5 = (f32[64,128]{1,0:T(8,128)S(1)}, f32[64,128]{1,0:T(8,128)S(1)}, u32[]{:S(2)}, u32[]{:S(2)}) collective-permute-start(f32[64,128]{1,0:T(8,128)S(1)} %get-tuple-element.19), channel_id=1, source_target_pairs={{0,1},{1,2},{2,3},{3,4},{4,5},{5,6},{6,7},{7,8},{8,9},{9,10},{10,1... | collective-permute-start | bytes 98312 | tf_op jit(solution)/shard_map/ppermute | solution.py:226
  26.7 4.0 %advance_twice.1 = (f32[1024,128]{1,0:T(8,128)S(1)}, f32[1024,128]{1,0:T(8,128)S(1)}) custom-call(f32[1024,256]{1,0:T(8,128)S(1)} %bitcast.39, f32[1024,256]{1,0:T(8,128)S(1)} %bitcast.40, f32[32,256]{1,0:T(8,128)S(1)} %copy-done.3, f32[32,1]{1,0:T(8,128)S(1)} %copy.19.rate_ref, f32[72,256]{1,0:T(8,128)S(1)} %collective-permute-done.xl_ref.kxl_ref, ...), custom_call_target="tpu_custom_call" | custom-call | flops 10000000000 | bytes 4194304 | tf_op jit(solution)/shard_map/advance_twice/pallas_call | solution.py:141
  30.8 1.6 %reduce_species.1 = (f32[1024,256]{1,0:T(8,128)}, f32[2048,128]{1,0:T(8,128)S(1)}) custom-call(f32[1024,128]{1,0:T(8,128)S(1)} %get-tuple-element.16.a0_ref, f32[1024,128]{1,0:T(8,128)S(1)} %get-tuple-element.17.a1_ref, f32[32,256]{1,0:T(8,128)S(1)} %copy-done.3, f32[32,1]{1,0:T(8,128)S(1)} %copy.19.rate_ref, ...), custom_call_target="tpu_custom_call" | custom-call | tf_op jit(solution)/shard_map/reduce_species/pallas_call | solution.py:209
  32.5 34.1 %all_to_all.15 = f32[32,64,128]{2,1,0:T(8,128)S(1)} all-to-all(f32[32,64,128]{2,1,0:T(8,128)S(1)} %bitcast.41), channel_id=1, replica_groups=mesh['tx'=32,'ty'=16] {'tx'}, dimensions={0} | all-to-all | bytes 2097152 | tf_op jit(solution)/shard_map/all_to_all | solution.py:244
  66.5 1.0 fusion
  67.6 26.5 %all_to_all.16 = f32[16,16,128]{2,1,0:T(8,128)S(1)} all-to-all(f32[16,16,128]{2,1,0:T(8,128)S(1)} %pad_maximum_fusion), channel_id=1, replica_groups=mesh['tx'=32,'ty'=16] {'ty'}, dimensions={0} | all-to-all | bytes 262144 | tf_op jit(solution)/shard_map/all_to_all | solution.py:250
  94.3 0.1 copy.23
  94.4 0.5 convolution_bitcast_fusion
  94.8 0.2 copy.26
  95.0 0.3 reshape.41
  95.3 0.1 copy.27
  95.5 29.4 %all_to_all.17 = f32[512,1,32]{2,1,0:T(1,128)S(1)} all-to-all(f32[512,1,32]{2,1,0:T(1,128)S(1)} %copy.27), channel_id=1, replica_groups=mesh['tx'=32,'ty'=16] {'tx','ty'}, dimensions={0} | all-to-all | bytes 131072 | tf_op jit(solution)/shard_map/all_to_all | solution.py:257
  124.9 0.1 copy.28
  125.0 0.2 reshape.42
  125.2 0.8 copy.29
  (26 shorter events, 0.3 us)
Async XLA Ops:
  0.6 1.2 copy-start
  1.9 0.8 copy-start.2
  2.6 24.0 %copy-start.1 = (f32[32,32,256]{2,1,0:T(8,128)S(1)}, f32[32,32,256]{2,1,0:T(8,128)}, u32[]{:S(2)}) copy-start(f32[32,32,256]{2,1,0:T(8,128)} %param.6) | copy-start | bytes 3145732
  3.4 23.3 %collective-permute-start.2 = (f32[544,128]{1,0:T(8,128)S(1)}, f32[544,128]{1,0:T(8,128)S(1)}, u32[]{:S(2)}, u32[]{:S(2)}) collective-permute-start(f32[544,128]{1,0:T(8,128)S(1)} %get-tuple-element.14), channel_id=1, source_target_pairs={{1,0},{2,1},{3,2},{4,3},{5,4},{6,5},{7,6},{8,7},{9,8},{10,9},{11,1... | collective-permute-start | bytes 835592 | tf_op jit(solution)/shard_map/ppermute | solution.py:226
  4.7 22.0 %collective-permute-start.3 = (f32[544,128]{1,0:T(8,128)S(1)}, f32[544,128]{1,0:T(8,128)S(1)}, u32[]{:S(2)}, u32[]{:S(2)}) collective-permute-start(f32[544,128]{1,0:T(8,128)S(1)} %get-tuple-element.15), channel_id=1, source_target_pairs={{0,1},{1,2},{2,3},{3,4},{4,5},{5,6},{6,7},{7,8},{8,9},{9,10},{10,1... | collective-permute-start | bytes 835592 | tf_op jit(solution)/shard_map/ppermute | solution.py:226
  9.3 10.8 %collective-permute-start = (f32[72,256]{1,0:T(8,128)S(1)}, f32[72,256]{1,0:T(8,128)S(1)}, u32[]{:S(2)}, u32[]{:S(2)}) collective-permute-start(f32[72,256]{1,0:T(8,128)S(1)} %get-tuple-element.12), channel_id=1, source_target_pairs={{16,0},{32,16},{48,32},{64,48},{80,64},{96,80},{112,96},{128,112},... | collective-permute-start | bytes 221192 | tf_op jit(solution)/shard_map/ppermute | solution.py:226
  18.0 1.9 %copy-start.7 = (f32[32]{0:T(128)S(1)}, f32[32]{0:T(128)}, u32[]{:S(2)}) copy-start(f32[32]{0:T(128)} %param.8) | copy-start | bytes 388
  18.0 3.3 %collective-permute-start.1 = (f32[72,256]{1,0:T(8,128)S(1)}, f32[72,256]{1,0:T(8,128)S(1)}, u32[]{:S(2)}, u32[]{:S(2)}) collective-permute-start(f32[72,256]{1,0:T(8,128)S(1)} %get-tuple-element.13), channel_id=1, source_target_pairs={{0,16},{16,32},{32,48},{48,64},{64,80},{80,96},{96,112},{112,128},... | collective-permute-start | bytes 221192 | tf_op jit(solution)/shard_map/ppermute | solution.py:226
  20.1 6.6 %copy-start.3 = (f32[32,256]{1,0:T(8,128)S(1)}, f32[32,256]{1,0:T(8,128)}, u32[]{:S(2)}) copy-start(f32[32,256]{1,0:T(8,128)} %k_ref.5) | copy-start | bytes 98308
  21.4 9.4 %collective-permute-start.4 = (f32[64,128]{1,0:T(8,128)S(1)}, f32[64,128]{1,0:T(8,128)S(1)}, u32[]{:S(2)}, u32[]{:S(2)}) collective-permute-start(f32[64,128]{1,0:T(8,128)S(1)} %get-tuple-element.18), channel_id=1, source_target_pairs={{1,0},{2,1},{3,2},{4,3},{5,4},{6,5},{7,6},{8,7},{9,8},{10,9},{11,1... | collective-permute-start | bytes 98312 | tf_op jit(solution)/shard_map/ppermute | solution.py:226
  22.6 8.1 %collective-permute-start.5 = (f32[64,128]{1,0:T(8,128)S(1)}, f32[64,128]{1,0:T(8,128)S(1)}, u32[]{:S(2)}, u32[]{:S(2)}) collective-permute-start(f32[64,128]{1,0:T(8,128)S(1)} %get-tuple-element.19), channel_id=1, source_target_pairs={{0,1},{1,2},{2,3},{3,4},{4,5},{5,6},{6,7},{7,8},{8,9},{9,10},{10,1... | collective-permute-start | bytes 98312 | tf_op jit(solution)/shard_map/ppermute | solution.py:226
  26.7 4.1 %copy-start.4 = (f32[32,128]{1,0:T(8,128)S(1)}, f32[32,128]{1,0:T(8,128)}, u32[]{:S(2)}) copy-start(f32[32,128]{1,0:T(8,128)} %fx_ref.1) | copy-start | bytes 49156
  26.7 4.1 %copy-start.5 = (f32[32,16]{0,1:T(8,128)S(1)}, f32[32,16]{0,1:T(8,128)}, u32[]{:S(2)}) copy-start(f32[32,16]{0,1:T(8,128)} %param.11) | copy-start | bytes 6148
  66.5 1.1 copy-start.6

commit v10 on v9

--- a/solution.py
+++ b/solution.py
@@ -7,6 +7,7 @@
 
 exact_mode = lax.Precision.HIGHEST
 f32, bf16 = jnp.float32, jnp.bfloat16
+SENT = 48
 NS, NX, NV, NH, NZ, NQ = 32, 32, 256, 128, 32, 16
 
 
@@ -171,15 +172,16 @@
             ref[cut, :] = ref[cut, :] + jnp.where(mask, term, 0.0)
     adv_ref[:, :128] = left[...]
     adv_ref[:, 128:] = right[...]
-    for z in range(NZ):
-        planes_ref[(2 * z + 1) * NX : (2 * z + 2) * NX, :] = fx_ref[...]
+    for to in range(NZ):
+        side = to % 2
+        planes_ref[to * SENT + NX : (to + 1) * SENT, :] = fx_ref[side * (NX // 2) : (side + 1) * (NX // 2), :]
 
     lane_q = lanes(NQ)
     low_q, even_q = lane_q < 64, (lane_q & 32) == 0
     fs_hi, fs_lo = split_2(fs_ref[...])
     weights = jnp.concatenate([fs_hi, fs_hi, fs_lo, fs_lo], axis=1)
 
-    def four_rows(group, carry):
+    for group in range(NX // 4):
         rows = []
         for g in range(4):
             cut = pl.ds(group * 4 + g, NS, stride=NX)
@@ -196,16 +198,16 @@
                 swapped.append(jnp.where(even_q, pltpu.roll(p, 96, 1), r))
         turned = jnp.concatenate(swapped, axis=0).T
         for g in range(4):
-            planes_ref[pl.ds(group * 4 + g, NZ, stride=2 * NX), :] = turned[g * NZ : (g + 1) * NZ, :]
-        return carry
-
-    lax.fori_loop(0, NX // 4, four_rows, 0, unroll=True)
+            side, x = divmod(group * 4 + g, NX // 2)
+            for e in range(2):
+                to = pl.ds(side * SENT + e * (NX // 2) + x, NZ // 2, stride=2 * SENT)
+                planes_ref[to, :] = turned[g * NZ + e * (NZ // 2) : g * NZ + (e + 1) * (NZ // 2), :]
 
 
 def reduce_species(sides, k, rate, faces, corner, fs, factor_x):
     xl, xh, yl, yh = faces
     tail_x, tail_y = pl.BlockSpec((8, NV), lambda i: (2 * NS // 8, 0)), pl.BlockSpec((NX, 128), lambda i: (NS // 2, 0))
-    shapes = [(NS * NX, NV), (NZ * 2 * NX, 128)]
+    shapes = [(NS * NX, NV), (NZ * SENT, 128)]
     return pl.pallas_call(
         reduce_kernel,
         grid=(1,),
@@ -240,11 +242,16 @@
     faces, rate = (xl, xh, yl, yh), species_rate[:, None]
     sides = advance(c2d, cell_factor, rate, faces)
     advanced, planes = reduce_species(sides, cell_factor, rate, faces, corner, factor_species.T, factor_x)
-    planes = planes.reshape(depth, 2 * cells_x, cells_y * ranks_q)
+    planes = planes.reshape(n_tx, SENT, cells_y * ranks_q)
     planes = lax.all_to_all(planes, "tx", 0, 0, tiled=True)
-    first = lax.dot_general(
-        planes[:, :cells_x], planes[:, cells_x:], (((0, 1), (0, 1)), ((), ())), precision=exact_mode
-    )
+    side, half = lax.axis_index("tx") % 2, cells_x // 2
+
+    def over_x(which):
+        plane = lax.dynamic_slice_in_dim(planes, which * half, half, axis=1)
+        return lax.dot_general(plane, planes[:, cells_x:], (((0, 1), (0, 1)), ((), ())), precision=exact_mode)
+
+    came = lax.ppermute(over_x(1 - side), "tx", [(i, i ^ 1) for i in range(n_tx)])
+    first = over_x(side) + came
     first = first.reshape(cells_y, ranks_q, -1).transpose(1, 0, 2)
     sent = jnp.concatenate([first, jnp.broadcast_to(factor_y[None], (n_ty,) + factor_y.shape)], axis=1)
     came = lax.all_to_all(sent, "ty", 0, 0, tiled=True)
@@ -255,7 +262,7 @@
     plane = plane.reshape(n_tx, rank_a // n_tx, n_ty, rank_b // n_ty).transpose(0, 2, 1, 3)
     plane = plane.reshape(n_tx * n_ty, 1, -1)
     core = lax.all_to_all(plane, ("tx", "ty"), 0, 0, tiled=True)
-    core = core.reshape(depth, ranks_q, rank_a // n_tx, rank_b // n_ty).transpose(2, 1, 3, 0)
+    core = core.reshape(depth // 2, 2, ranks_q, rank_a // n_tx, rank_b // n_ty).transpose(3, 2, 4, 1, 0)
     return advanced.reshape(species.shape), core.reshape(rank_a // n_tx, ranks_q, -1)
 
 

time: 126 us -> 129 us (1.024)
  blocking collectives: 90 us -> 54.5 us
  waiting for transfers between devices: 1.3 us -> 23.4 us
  starting transfers between devices: 21.8 us -> 33.9 us
  local copies, waits for them, and re-layouts: 4.04 us -> 6.35 us
    all_to_all x1 -> x0, blocking collectives: 34.1 us -> none  [body(): planes = lax.all_to_all(planes, 'tx', 0, 0, tiled=True)]
    all_to_all x0 -> x1, waiting for transfers between devices: none -> 21.2 us  [body(): planes = lax.all_to_all(planes, 'tx', 0, 0, tiled=True)]
    all_to_all x0 -> x1, starting transfers between devices: none -> 7.83 us  [body(): planes = lax.all_to_all(planes, 'tx', 0, 0, tiled=True)]
    ppermute x0 -> x1, starting transfers between devices: none -> 4.22 us  [body(): lax.ppermute(over_x(1 - side), 'tx', [(i, i ^ 1) for i in range(n_tx)])]
    reshape x1 -> x2, local copies, waits for them, and re-layouts: 0.21 us -> 2.06 us  [the longest x1 1.35 us: body(): core.reshape(rank_a // n_tx, ranks_q, -1)]
    all_to_all x1, blocking collectives: 29.4 us -> 28 us  [body(): core = lax.all_to_all(plane, ('tx', 'ty'), 0, 0, tiled=True)]
    unnamed x17 -> x16, local copies, waits for them, and re-layouts: 2.81 us -> 2.65 us
  transfers between devices with their start and end apart: 6 -> 8, of which waited for: 1 -> 3; matrix products, arithmetic and copies ran while one was open for 0% -> 0% of each run, Pallas kernels for 3% -> 3%
where the time goes in v10:
time: 129 us; the launch traced here: 128 us
  blocking collectives  54.5 us (42%)
  starting transfers between devices  33.9 us (26%)
  waiting for transfers between devices  23.4 us (18%)
  Pallas kernels  7.48 us (6%)
  local copies, waits for them, and re-layouts  6.35 us (5%)
  matrix products  1.78 us (1%)
    all_to_all x1, blocking collectives, body(): core = lax.all_to_all(plane, ('tx', 'ty'), 0, 0, tiled=True)  28 us
    all_to_all x1, blocking collectives, body(): came = lax.all_to_all(sent, 'ty', 0, 0, tiled=True)  26.5 us
    ppermute x6, starting transfers between devices, shift_to(): lax.ppermute(v, axis, [(i, i + step) for i in range(count) if 0 <= i + st...  21.8 us
    all_to_all x1, waiting for transfers between devices, body(): planes = lax.all_to_all(planes, 'tx', 0, 0, tiled=True)  21.2 us
    all_to_all x1, starting transfers between devices, body(): planes = lax.all_to_all(planes, 'tx', 0, 0, tiled=True)  7.83 us
    ppermute x1, starting transfers between devices, body(): lax.ppermute(over_x(1 - side), 'tx', [(i, i ^ 1) for i in range(n_tx)])  4.22 us
    pallas_call x1, Pallas kernels, advance(): pl.pallas_call(advance_kernel, grid=(1,), out_shape=[jax.ShapeDtypeStruct...  4.05 us
    pallas_call x1, Pallas kernels, reduce_species(): pl.pallas_call(reduce_kernel, grid=(1,), out_shape=[jax.ShapeDtypeStruct(...  2.7 us
  transfers between devices with their start and end apart: 8, of which 3 were waited for; matrix products, arithmetic and copies ran while one was open for 0% of the time, Pallas kernels for 3%

profile of v10, /device:TPU:1, one launch (start us, length us, event | category | flops | bytes accessed | tf_op | source)
XLA Modules:
  0.0 128.3 jit_solution(17307352601052854320)
XLA Ops:
  0.6 1.2 copy-done
  1.9 0.8 copy-done.2
  2.6 0.7 pack_faces.1
  3.4 1.3 %collective-permute-start.2 = (f32[544,128]{1,0:T(8,128)S(1)}, f32[544,128]{1,0:T(8,128)S(1)}, u32[]{:S(2)}, u32[]{:S(2)}) collective-permute-start(f32[544,128]{1,0:T(8,128)S(1)} %get-tuple-element.14), channel_id=1, source_target_pairs={{1,0},{2,1},{3,2},{4,3},{5,4},{6,5},{7,6},{8,7},{9,8},{10,9},{11,1... | collective-permute-start | bytes 835592 | tf_op jit(solution)/shard_map/ppermute | solution.py:228
  4.7 4.6 %collective-permute-start.3 = (f32[544,128]{1,0:T(8,128)S(1)}, f32[544,128]{1,0:T(8,128)S(1)}, u32[]{:S(2)}, u32[]{:S(2)}) collective-permute-start(f32[544,128]{1,0:T(8,128)S(1)} %get-tuple-element.15), channel_id=1, source_target_pairs={{0,1},{1,2},{2,3},{3,4},{4,5},{5,6},{6,7},{7,8},{8,9},{9,10},{10,1... | collective-permute-start | bytes 835592 | tf_op jit(solution)/shard_map/ppermute | solution.py:228
  9.3 8.8 %collective-permute-start = (f32[72,256]{1,0:T(8,128)S(1)}, f32[72,256]{1,0:T(8,128)S(1)}, u32[]{:S(2)}, u32[]{:S(2)}) collective-permute-start(f32[72,256]{1,0:T(8,128)S(1)} %get-tuple-element.12), channel_id=1, source_target_pairs={{16,0},{32,16},{48,32},{64,48},{80,64},{96,80},{112,96},{128,112},... | collective-permute-start | bytes 221192 | tf_op jit(solution)/shard_map/ppermute | solution.py:228
  18.0 1.9 %collective-permute-start.1 = (f32[72,256]{1,0:T(8,128)S(1)}, f32[72,256]{1,0:T(8,128)S(1)}, u32[]{:S(2)}, u32[]{:S(2)}) collective-permute-start(f32[72,256]{1,0:T(8,128)S(1)} %get-tuple-element.13), channel_id=1, source_target_pairs={{0,16},{16,32},{32,48},{48,64},{64,80},{80,96},{96,112},{112,128},... | collective-permute-start | bytes 221192 | tf_op jit(solution)/shard_map/ppermute | solution.py:228
  20.1 1.3 %collective-permute-done.1.xh_ref.kxh_ref = f32[72,256]{1,0:T(8,128)S(1)} collective-permute-done((f32[72,256]{1,0:T(8,128)S(1)}, f32[72,256]{1,0:T(8,128)S(1)}, u32[]{:S(2)}, u32[]{:S(2)}) %collective-permute-start.1) | collective-permute-done | bytes 73760 | tf_op jit(solution)/shard_map/ppermute | solution.py:228
  21.4 1.3 collective-permute-start.4
  22.6 4.0 %collective-permute-start.5 = (f32[64,128]{1,0:T(8,128)S(1)}, f32[64,128]{1,0:T(8,128)S(1)}, u32[]{:S(2)}, u32[]{:S(2)}) collective-permute-start(f32[64,128]{1,0:T(8,128)S(1)} %get-tuple-element.19), channel_id=1, source_target_pairs={{0,1},{1,2},{2,3},{3,4},{4,5},{5,6},{6,7},{7,8},{8,9},{9,10},{10,1... | collective-permute-start | bytes 98312 | tf_op jit(solution)/shard_map/ppermute | solution.py:228
  26.7 4.0 %advance_twice.1 = (f32[1024,128]{1,0:T(8,128)S(1)}, f32[1024,128]{1,0:T(8,128)S(1)}) custom-call(f32[1024,256]{1,0:T(8,128)S(1)} %bitcast.41, f32[1024,256]{1,0:T(8,128)S(1)} %bitcast.42, f32[32,256]{1,0:T(8,128)S(1)} %copy-done.3, f32[32,1]{1,0:T(8,128)S(1)} %copy.30.rate_ref, f32[72,256]{1,0:T(8,128)S(1)} %collective-permute-done.xl_ref.kxl_ref, ...), custom_call_target="tpu_custom_call" | custom-call | flops 10000000000 | bytes 4194304 | tf_op jit(solution)/shard_map/advance_twice/pallas_call | solution.py:142
  30.8 2.7 %reduce_species.1 = (f32[1024,256]{1,0:T(8,128)}, f32[1536,128]{1,0:T(8,128)}) custom-call(f32[1024,128]{1,0:T(8,128)S(1)} %get-tuple-element.16.a0_ref, f32[1024,128]{1,0:T(8,128)S(1)} %get-tuple-element.17.a1_ref, f32[32,256]{1,0:T(8,128)S(1)} %copy-done.3, f32[32,1]{1,0:T(8,128)S(1)} %copy.30.rate_ref, f32[72,256]{1,0:T(8,128)S(1)} %collective-permute-done.xl_ref.kxl_ref, ...), custom_call_target="tpu_custom_call" | custom-call | tf_op jit(solution)/shard_map/reduce_species/pallas_call | solution.py:211
  33.5 7.8 %all-to-all-start = ((f32[32,48,128]{2,1,0:T(8,128)}), f32[32,48,128]{2,1,0:T(8,128)S(1)}, u32[]{:S(2)}, u32[]{:S(2)}) async-start(f32[32,48,128]{2,1,0:T(8,128)} %bitcast.4), calls=%async_computation | async-start | bytes 1572864 | tf_op jit(solution)/shard_map/all_to_all | solution.py:246
  41.4 21.2 %all-to-all-done = f32[32,48,128]{2,1,0:T(8,128)S(1)} async-done(((f32[32,48,128]{2,1,0:T(8,128)}), f32[32,48,128]{2,1,0:T(8,128)S(1)}, u32[]{:S(2)}, u32[]{:S(2)}) %all-to-all-start) | async-done | bytes 786464 | tf_op jit(solution)/shard_map/all_to_all | solution.py:246
  62.6 0.7 convolution_bitcast_fusion.1
  63.3 4.2 %collective-permute-start.6 = (f32[128,128]{1,0:T(8,128)S(1)}, f32[128,128]{1,0:T(8,128)S(1)}, u32[]{:S(2)}, u32[]{:S(2)}) collective-permute-start(f32[128,128]{1,0:T(8,128)S(1)} %convolution_bitcast_fusion.1), channel_id=1, source_target_pairs={{0,16},{16,0},{32,48},{48,32},{64,80},{80,64},{96,112},{112,96},{1... | collective-permute-start | bytes 196616 | tf_op jit(solution)/shard_map/ppermute | solution.py:253
  67.5 0.9 collective-permute-done.6
  68.4 0.7 fusion
  69.1 0.6 copy-done.6
  69.8 26.5 %all_to_all.15 = f32[16,16,128]{2,1,0:T(8,128)S(1)} all-to-all(f32[16,16,128]{2,1,0:T(8,128)S(1)} %pad_maximum_fusion), channel_id=1, replica_groups=mesh['tx'=32,'ty'=16] {'ty'}, dimensions={0} | all-to-all | bytes 262144 | tf_op jit(solution)/shard_map/all_to_all | solution.py:257
  97.6 28.0 %all_to_all.16 = f32[512,1,32]{2,1,0:T(1,128)S(1)} all-to-all(f32[512,1,32]{2,1,0:T(1,128)S(1)} %copy.41), channel_id=1, replica_groups=mesh['tx'=32,'ty'=16] {'tx','ty'}, dimensions={0} | all-to-all | bytes 131072 | tf_op jit(solution)/shard_map/all_to_all | solution.py:264
  125.6 0.7 reshape.42
  126.4 0.5 copy.43
  126.9 1.4 %reshape.43 = f32[4,16,256]{2,1,0:T(8,128)} reshape(f32[4,16,8,2,16]{4,3,2,1,0:T(2,128)S(1)} %copy.43) | data formatting | bytes 131072 | tf_op jit(solution)/shard_map/reshape | solution.py:266
  (32 shorter events, 1.6 us)
Async XLA Ops:
  0.6 1.2 copy-start
  1.9 0.8 copy-start.2
  2.6 24.0 %copy-start.1 = (f32[32,32,256]{2,1,0:T(8,128)S(1)}, f32[32,32,256]{2,1,0:T(8,128)}, u32[]{:S(2)}) copy-start(f32[32,32,256]{2,1,0:T(8,128)} %param.6) | copy-start | bytes 3145732
  3.4 23.3 %collective-permute-start.2 = (f32[544,128]{1,0:T(8,128)S(1)}, f32[544,128]{1,0:T(8,128)S(1)}, u32[]{:S(2)}, u32[]{:S(2)}) collective-permute-start(f32[544,128]{1,0:T(8,128)S(1)} %get-tuple-element.14), channel_id=1, source_target_pairs={{1,0},{2,1},{3,2},{4,3},{5,4},{6,5},{7,6},{8,7},{9,8},{10,9},{11,1... | collective-permute-start | bytes 835592 | tf_op jit(solution)/shard_map/ppermute | solution.py:228
  4.7 22.0 %collective-permute-start.3 = (f32[544,128]{1,0:T(8,128)S(1)}, f32[544,128]{1,0:T(8,128)S(1)}, u32[]{:S(2)}, u32[]{:S(2)}) collective-permute-start(f32[544,128]{1,0:T(8,128)S(1)} %get-tuple-element.15), channel_id=1, source_target_pairs={{0,1},{1,2},{2,3},{3,4},{4,5},{5,6},{6,7},{7,8},{8,9},{9,10},{10,1... | collective-permute-start | bytes 835592 | tf_op jit(solution)/shard_map/ppermute | solution.py:228
  9.3 10.8 %collective-permute-start = (f32[72,256]{1,0:T(8,128)S(1)}, f32[72,256]{1,0:T(8,128)S(1)}, u32[]{:S(2)}, u32[]{:S(2)}) collective-permute-start(f32[72,256]{1,0:T(8,128)S(1)} %get-tuple-element.12), channel_id=1, source_target_pairs={{16,0},{32,16},{48,32},{64,48},{80,64},{96,80},{112,96},{128,112},... | collective-permute-start | bytes 221192 | tf_op jit(solution)/shard_map/ppermute | solution.py:228
  18.0 1.9 %copy-start.7 = (f32[32]{0:T(128)S(1)}, f32[32]{0:T(128)}, u32[]{:S(2)}) copy-start(f32[32]{0:T(128)} %param.8) | copy-start | bytes 388
  18.0 3.3 %collective-permute-start.1 = (f32[72,256]{1,0:T(8,128)S(1)}, f32[72,256]{1,0:T(8,128)S(1)}, u32[]{:S(2)}, u32[]{:S(2)}) collective-permute-start(f32[72,256]{1,0:T(8,128)S(1)} %get-tuple-element.13), channel_id=1, source_target_pairs={{0,16},{16,32},{32,48},{48,64},{64,80},{80,96},{96,112},{112,128},... | collective-permute-start | bytes 221192 | tf_op jit(solution)/shard_map/ppermute | solution.py:228
  20.1 6.6 %copy-start.3 = (f32[32,256]{1,0:T(8,128)S(1)}, f32[32,256]{1,0:T(8,128)}, u32[]{:S(2)}) copy-start(f32[32,256]{1,0:T(8,128)} %k_ref.5) | copy-start | bytes 98308
  21.4 9.4 %collective-permute-start.4 = (f32[64,128]{1,0:T(8,128)S(1)}, f32[64,128]{1,0:T(8,128)S(1)}, u32[]{:S(2)}, u32[]{:S(2)}) collective-permute-start(f32[64,128]{1,0:T(8,128)S(1)} %get-tuple-element.18), channel_id=1, source_target_pairs={{1,0},{2,1},{3,2},{4,3},{5,4},{6,5},{7,6},{8,7},{9,8},{10,9},{11,1... | collective-permute-start | bytes 98312 | tf_op jit(solution)/shard_map/ppermute | solution.py:228
  22.6 8.1 %collective-permute-start.5 = (f32[64,128]{1,0:T(8,128)S(1)}, f32[64,128]{1,0:T(8,128)S(1)}, u32[]{:S(2)}, u32[]{:S(2)}) collective-permute-start(f32[64,128]{1,0:T(8,128)S(1)} %get-tuple-element.19), channel_id=1, source_target_pairs={{0,1},{1,2},{2,3},{3,4},{4,5},{5,6},{6,7},{7,8},{8,9},{9,10},{10,1... | collective-permute-start | bytes 98312 | tf_op jit(solution)/shard_map/ppermute | solution.py:228
  26.7 4.1 %copy-start.4 = (f32[32,128]{1,0:T(8,128)S(1)}, f32[32,128]{1,0:T(8,128)}, u32[]{:S(2)}) copy-start(f32[32,128]{1,0:T(8,128)} %fx_ref.1) | copy-start | bytes 49156
  26.7 4.1 %copy-start.5 = (f32[32,16]{0,1:T(8,128)S(1)}, f32[32,16]{0,1:T(8,128)}, u32[]{:S(2)}) copy-start(f32[32,16]{0,1:T(8,128)} %param.11) | copy-start | bytes 6148
  33.5 29.1 %all-to-all-start = ((f32[32,48,128]{2,1,0:T(8,128)}), f32[32,48,128]{2,1,0:T(8,128)S(1)}, u32[]{:S(2)}, u32[]{:S(2)}) async-start(f32[32,48,128]{2,1,0:T(8,128)} %bitcast.4), calls=%async_computation | async-start | bytes 1572864 | tf_op jit(solution)/shard_map/all_to_all | solution.py:246
  63.3 5.1 %collective-permute-start.6 = (f32[128,128]{1,0:T(8,128)S(1)}, f32[128,128]{1,0:T(8,128)S(1)}, u32[]{:S(2)}, u32[]{:S(2)}) collective-permute-start(f32[128,128]{1,0:T(8,128)S(1)} %convolution_bitcast_fusion.1), channel_id=1, source_target_pairs={{0,16},{16,0},{32,48},{48,32},{64,80},{80,64},{96,112},{112,96},{1... | collective-permute-start | bytes 196616 | tf_op jit(solution)/shard_map/ppermute | solution.py:253
  69.1 0.7 copy-start.6

commit v11 on v9

--- a/solution.py
+++ b/solution.py
@@ -54,14 +54,23 @@
     )(c2d, c2d, k)
 
 
+def turned(v, shift):
+    return pltpu.roll(v, shift % 128, 1) if shift % 128 else v
+
+
 def corner_kernel(xl_ref, xh_ref, lo_ref, hi_ref):
-    for at, ref in ((0, xh_ref), (NS, xl_ref)):
-        lo_ref[at : at + NS, :] = ref[0:NS, :128]
-        hi_ref[at : at + NS, :] = ref[0:NS, 128:]
+    group = lanes(NS // 2) // NZ
+    for out_ref, side, at in ((lo_ref, 0, 0), (hi_ref, 128, 128 - NZ)):
+        packed = None
+        for g in range(4):
+            ref, row = (xh_ref, xl_ref)[g // 2], (g % 2) * (NS // 2)
+            part = turned(ref[row : row + NS // 2, side : side + 128], g * NZ - at)
+            packed = part if packed is None else jnp.where(group == g, part, packed)
+        out_ref[...] = packed
 
 
 def corners(xl, xh):
-    shapes = [(2 * NS, 128)] * 2
+    shapes = [(NS // 2, 128)] * 2
     return pl.pallas_call(
         corner_kernel,
         grid=(1,),
@@ -160,14 +169,16 @@
     left[...], right[...] = a0_ref[...], a1_ref[...]
     rate = jnp.broadcast_to(rate_ref[...], (NS, 128))
     first_y, last_y = lanes(NS) < NZ, lanes(NS) >= 128 - NZ
-    for x, at, kx_ref in ((0, 0, kxh_ref), (NX - 1, NS, kxl_ref)):
+    for x, at, kx_ref in ((0, 0, kxh_ref), (NX - 1, 2, kxl_ref)):
         cut = pl.ds(x, NS, stride=NX)
         for ref, own, corner_ref, ky_ref, turn, mask in (
             (left, slice(0, 128), ch_ref, kyh_ref, 32, first_y),
             (right, slice(128, 256), cl_ref, kyl_ref, 96, last_y),
         ):
             paths = kx_ref[0:1, own] + pltpu.roll(jnp.broadcast_to(ky_ref[x : x + 1, :], (8, 128)), turn, 1)[0:1, :]
-            term = (rate * k_ref[x : x + 1, own]) * (rate * paths) * pltpu.roll(corner_ref[at : at + NS, :], turn, 1)
+            to = 0 if turn == NZ else 128 - NZ
+            corner = jnp.concatenate([turned(corner_ref[...], to - (at + g) * NZ) for g in range(2)], axis=0)
+            term = (rate * k_ref[x : x + 1, own]) * (rate * paths) * corner
             ref[cut, :] = ref[cut, :] + jnp.where(mask, term, 0.0)
     adv_ref[:, :128] = left[...]
     adv_ref[:, 128:] = right[...]
@@ -194,9 +205,9 @@
             for p, r in (a, b):
                 swapped.append(jnp.where(even_q, p, pltpu.roll(r, 32, 1)))
                 swapped.append(jnp.where(even_q, pltpu.roll(p, 96, 1), r))
-        turned = jnp.concatenate(swapped, axis=0).T
+        flipped = jnp.concatenate(swapped, axis=0).T
         for g in range(4):
-            planes_ref[pl.ds(group * 4 + g, NZ, stride=2 * NX), :] = turned[g * NZ : (g + 1) * NZ, :]
+            planes_ref[pl.ds(group * 4 + g, NZ, stride=2 * NX), :] = flipped[g * NZ : (g + 1) * NZ, :]
         return carry
 
     lax.fori_loop(0, NX // 4, four_rows, 0, unroll=True)

time: 126 us -> 127 us (level)
  no operation moved by 1% of the time
where the time goes in v11:
time: 127 us; the launch traced here: 126 us
  blocking collectives  90 us (71%)
  starting transfers between devices  21.8 us (17%)
  Pallas kernels  6.48 us (5%)
  local copies, waits for them, and re-layouts  4.04 us (3%)
  matrix products  1.49 us (1%)
  waiting for transfers between devices  1.3 us (1%)
    all_to_all x1, blocking collectives, body(): planes = lax.all_to_all(planes, 'tx', 0, 0, tiled=True)  34.1 us
    all_to_all x1, blocking collectives, body(): core = lax.all_to_all(plane, ('tx', 'ty'), 0, 0, tiled=True)  29.4 us
    all_to_all x1, blocking collectives, body(): came = lax.all_to_all(sent, 'ty', 0, 0, tiled=True)  26.5 us
    ppermute x6, starting transfers between devices, shift_to(): lax.ppermute(v, axis, [(i, i + step) for i in range(count) if 0 <= i + st...  21.8 us
    pallas_call x1, Pallas kernels, advance(): pl.pallas_call(advance_kernel, grid=(1,), out_shape=[jax.ShapeDtypeStruct...  4.05 us
    unnamed x17, local copies, waits for them, and re-layouts  2.81 us
  transfers between devices with their start and end apart: 6, of which 1 were waited for; matrix products, arithmetic and copies ran while one was open for 0% of the time, Pallas kernels for 3%

profile of v11, /device:TPU:1, one launch (start us, length us, event | category | flops | bytes accessed | tf_op | source)
XLA Modules:
  0.0 126.1 jit_solution(11157336153729704985)
XLA Ops:
  0.6 1.2 copy-done
  1.9 0.8 copy-done.2
  2.6 0.7 pack_faces.1
  3.4 1.3 %collective-permute-start.2 = (f32[544,128]{1,0:T(8,128)S(1)}, f32[544,128]{1,0:T(8,128)S(1)}, u32[]{:S(2)}, u32[]{:S(2)}) collective-permute-start(f32[544,128]{1,0:T(8,128)S(1)} %get-tuple-element.14), channel_id=1, source_target_pairs={{1,0},{2,1},{3,2},{4,3},{5,4},{6,5},{7,6},{8,7},{9,8},{10,9},{11,1... | collective-permute-start | bytes 835592 | tf_op jit(solution)/shard_map/ppermute | solution.py:237
  4.7 4.6 %collective-permute-start.3 = (f32[544,128]{1,0:T(8,128)S(1)}, f32[544,128]{1,0:T(8,128)S(1)}, u32[]{:S(2)}, u32[]{:S(2)}) collective-permute-start(f32[544,128]{1,0:T(8,128)S(1)} %get-tuple-element.15), channel_id=1, source_target_pairs={{0,1},{1,2},{2,3},{3,4},{4,5},{5,6},{6,7},{7,8},{8,9},{9,10},{10,1... | collective-permute-start | bytes 835592 | tf_op jit(solution)/shard_map/ppermute | solution.py:237
  9.3 8.8 %collective-permute-start = (f32[72,256]{1,0:T(8,128)S(1)}, f32[72,256]{1,0:T(8,128)S(1)}, u32[]{:S(2)}, u32[]{:S(2)}) collective-permute-start(f32[72,256]{1,0:T(8,128)S(1)} %get-tuple-element.12), channel_id=1, source_target_pairs={{16,0},{32,16},{48,32},{64,48},{80,64},{96,80},{112,96},{128,112},... | collective-permute-start | bytes 221192 | tf_op jit(solution)/shard_map/ppermute | solution.py:237
  18.0 1.9 %collective-permute-start.1 = (f32[72,256]{1,0:T(8,128)S(1)}, f32[72,256]{1,0:T(8,128)S(1)}, u32[]{:S(2)}, u32[]{:S(2)}) collective-permute-start(f32[72,256]{1,0:T(8,128)S(1)} %get-tuple-element.13), channel_id=1, source_target_pairs={{0,16},{16,32},{32,48},{48,64},{64,80},{80,96},{96,112},{112,128},... | collective-permute-start | bytes 221192 | tf_op jit(solution)/shard_map/ppermute | solution.py:237
  20.1 1.3 %collective-permute-done.1.xh_ref.kxh_ref = f32[72,256]{1,0:T(8,128)S(1)} collective-permute-done((f32[72,256]{1,0:T(8,128)S(1)}, f32[72,256]{1,0:T(8,128)S(1)}, u32[]{:S(2)}, u32[]{:S(2)}) %collective-permute-start.1) | collective-permute-done | bytes 73760 | tf_op jit(solution)/shard_map/ppermute | solution.py:237
  21.4 1.3 %collective-permute-start.4 = (f32[16,128]{1,0:T(8,128)S(1)}, f32[16,128]{1,0:T(8,128)S(1)}, u32[]{:S(2)}, u32[]{:S(2)}) collective-permute-start(f32[16,128]{1,0:T(8,128)S(1)} %get-tuple-element.18), channel_id=1, source_target_pairs={{1,0},{2,1},{3,2},{4,3},{5,4},{6,5},{7,6},{8,7},{9,8},{10,9},{11,1... | collective-permute-start | bytes 24584 | tf_op jit(solution)/shard_map/ppermute | solution.py:237
  22.7 4.0 %collective-permute-start.5 = (f32[16,128]{1,0:T(8,128)S(1)}, f32[16,128]{1,0:T(8,128)S(1)}, u32[]{:S(2)}, u32[]{:S(2)}) collective-permute-start(f32[16,128]{1,0:T(8,128)S(1)} %get-tuple-element.19), channel_id=1, source_target_pairs={{0,1},{1,2},{2,3},{3,4},{4,5},{5,6},{6,7},{7,8},{8,9},{9,10},{10,1... | collective-permute-start | bytes 24584 | tf_op jit(solution)/shard_map/ppermute | solution.py:237
  26.8 4.0 %advance_twice.1 = (f32[1024,128]{1,0:T(8,128)S(1)}, f32[1024,128]{1,0:T(8,128)S(1)}) custom-call(f32[1024,256]{1,0:T(8,128)S(1)} %bitcast.39, f32[1024,256]{1,0:T(8,128)S(1)} %bitcast.40, f32[32,256]{1,0:T(8,128)S(1)} %copy-done.3, f32[32,1]{1,0:T(8,128)S(1)} %copy.19.rate_ref, f32[72,256]{1,0:T(8,128)S(1)} %collective-permute-done.xl_ref.kxl_ref, ...), custom_call_target="tpu_custom_call" | custom-call | flops 10000000000 | bytes 4194304 | tf_op jit(solution)/shard_map/advance_twice/pallas_call | solution.py:150
  30.9 1.6 %reduce_species.1 = (f32[1024,256]{1,0:T(8,128)}, f32[2048,128]{1,0:T(8,128)S(1)}) custom-call(f32[1024,128]{1,0:T(8,128)S(1)} %get-tuple-element.16.a0_ref, f32[1024,128]{1,0:T(8,128)S(1)} %get-tuple-element.17.a1_ref, f32[32,256]{1,0:T(8,128)S(1)} %copy-done.3, f32[32,1]{1,0:T(8,128)S(1)} %copy.19.rate_ref, ...), custom_call_target="tpu_custom_call" | custom-call | tf_op jit(solution)/shard_map/reduce_species/pallas_call | solution.py:220
  32.5 34.1 %all_to_all.15 = f32[32,64,128]{2,1,0:T(8,128)S(1)} all-to-all(f32[32,64,128]{2,1,0:T(8,128)S(1)} %bitcast.41), channel_id=1, replica_groups=mesh['tx'=32,'ty'=16] {'tx'}, dimensions={0} | all-to-all | bytes 2097152 | tf_op jit(solution)/shard_map/all_to_all | solution.py:255
  66.6 1.0 fusion
  67.7 26.5 %all_to_all.16 = f32[16,16,128]{2,1,0:T(8,128)S(1)} all-to-all(f32[16,16,128]{2,1,0:T(8,128)S(1)} %pad_maximum_fusion), channel_id=1, replica_groups=mesh['tx'=32,'ty'=16] {'ty'}, dimensions={0} | all-to-all | bytes 262144 | tf_op jit(solution)/shard_map/all_to_all | solution.py:261
  94.3 0.1 copy.23
  94.4 0.5 convolution_bitcast_fusion
  94.9 0.2 copy.26
  95.1 0.3 reshape.41
  95.4 0.1 copy.27
  95.5 29.4 %all_to_all.17 = f32[512,1,32]{2,1,0:T(1,128)S(1)} all-to-all(f32[512,1,32]{2,1,0:T(1,128)S(1)} %copy.27), channel_id=1, replica_groups=mesh['tx'=32,'ty'=16] {'tx','ty'}, dimensions={0} | all-to-all | bytes 131072 | tf_op jit(solution)/shard_map/all_to_all | solution.py:268
  124.9 0.1 copy.28
  125.0 0.2 reshape.42
  125.3 0.8 copy.29
  (26 shorter events, 0.3 us)
Async XLA Ops:
  0.6 1.2 copy-start
  1.9 0.8 copy-start.2
  2.6 24.1 %copy-start.1 = (f32[32,32,256]{2,1,0:T(8,128)S(1)}, f32[32,32,256]{2,1,0:T(8,128)}, u32[]{:S(2)}) copy-start(f32[32,32,256]{2,1,0:T(8,128)} %param.6) | copy-start | bytes 3145732
  3.4 23.4 %collective-permute-start.2 = (f32[544,128]{1,0:T(8,128)S(1)}, f32[544,128]{1,0:T(8,128)S(1)}, u32[]{:S(2)}, u32[]{:S(2)}) collective-permute-start(f32[544,128]{1,0:T(8,128)S(1)} %get-tuple-element.14), channel_id=1, source_target_pairs={{1,0},{2,1},{3,2},{4,3},{5,4},{6,5},{7,6},{8,7},{9,8},{10,9},{11,1... | collective-permute-start | bytes 835592 | tf_op jit(solution)/shard_map/ppermute | solution.py:237
  4.7 22.1 %collective-permute-start.3 = (f32[544,128]{1,0:T(8,128)S(1)}, f32[544,128]{1,0:T(8,128)S(1)}, u32[]{:S(2)}, u32[]{:S(2)}) collective-permute-start(f32[544,128]{1,0:T(8,128)S(1)} %get-tuple-element.15), channel_id=1, source_target_pairs={{0,1},{1,2},{2,3},{3,4},{4,5},{5,6},{6,7},{7,8},{8,9},{9,10},{10,1... | collective-permute-start | bytes 835592 | tf_op jit(solution)/shard_map/ppermute | solution.py:237
  9.3 10.8 %collective-permute-start = (f32[72,256]{1,0:T(8,128)S(1)}, f32[72,256]{1,0:T(8,128)S(1)}, u32[]{:S(2)}, u32[]{:S(2)}) collective-permute-start(f32[72,256]{1,0:T(8,128)S(1)} %get-tuple-element.12), channel_id=1, source_target_pairs={{16,0},{32,16},{48,32},{64,48},{80,64},{96,80},{112,96},{128,112},... | collective-permute-start | bytes 221192 | tf_op jit(solution)/shard_map/ppermute | solution.py:237
  18.0 1.9 %copy-start.7 = (f32[32]{0:T(128)S(1)}, f32[32]{0:T(128)}, u32[]{:S(2)}) copy-start(f32[32]{0:T(128)} %param.8) | copy-start | bytes 388
  18.0 3.3 %collective-permute-start.1 = (f32[72,256]{1,0:T(8,128)S(1)}, f32[72,256]{1,0:T(8,128)S(1)}, u32[]{:S(2)}, u32[]{:S(2)}) collective-permute-start(f32[72,256]{1,0:T(8,128)S(1)} %get-tuple-element.13), channel_id=1, source_target_pairs={{0,16},{16,32},{32,48},{48,64},{64,80},{80,96},{96,112},{112,128},... | collective-permute-start | bytes 221192 | tf_op jit(solution)/shard_map/ppermute | solution.py:237
  20.1 6.7 %copy-start.3 = (f32[32,256]{1,0:T(8,128)S(1)}, f32[32,256]{1,0:T(8,128)}, u32[]{:S(2)}) copy-start(f32[32,256]{1,0:T(8,128)} %k_ref.5) | copy-start | bytes 98308
  21.4 9.4 %collective-permute-start.4 = (f32[16,128]{1,0:T(8,128)S(1)}, f32[16,128]{1,0:T(8,128)S(1)}, u32[]{:S(2)}, u32[]{:S(2)}) collective-permute-start(f32[16,128]{1,0:T(8,128)S(1)} %get-tuple-element.18), channel_id=1, source_target_pairs={{1,0},{2,1},{3,2},{4,3},{5,4},{6,5},{7,6},{8,7},{9,8},{10,9},{11,1... | collective-permute-start | bytes 24584 | tf_op jit(solution)/shard_map/ppermute | solution.py:237
  22.7 8.1 %collective-permute-start.5 = (f32[16,128]{1,0:T(8,128)S(1)}, f32[16,128]{1,0:T(8,128)S(1)}, u32[]{:S(2)}, u32[]{:S(2)}) collective-permute-start(f32[16,128]{1,0:T(8,128)S(1)} %get-tuple-element.19), channel_id=1, source_target_pairs={{0,1},{1,2},{2,3},{3,4},{4,5},{5,6},{6,7},{7,8},{8,9},{9,10},{10,1... | collective-permute-start | bytes 24584 | tf_op jit(solution)/shard_map/ppermute | solution.py:237
  26.8 4.1 %copy-start.4 = (f32[32,128]{1,0:T(8,128)S(1)}, f32[32,128]{1,0:T(8,128)}, u32[]{:S(2)}) copy-start(f32[32,128]{1,0:T(8,128)} %fx_ref.1) | copy-start | bytes 49156
  26.8 4.1 %copy-start.5 = (f32[32,16]{0,1:T(8,128)S(1)}, f32[32,16]{0,1:T(8,128)}, u32[]{:S(2)}) copy-start(f32[32,16]{0,1:T(8,128)} %param.11) | copy-start | bytes 6148
  66.6 1.1 copy-start.6

commit v12 on v8

--- a/solution.py
+++ b/solution.py
@@ -151,7 +151,7 @@
             pltpu.VMEM((NX + 16, NV + NH), f32),
         ],
         compiler_params=pltpu.CompilerParams(vmem_limit_bytes=16 * 2**20),
-        cost_estimate=pl.CostEstimate(flops=10000000000, bytes_accessed=4 * 2**20, transcendentals=0),
+        cost_estimate=pl.CostEstimate(flops=4000000000, bytes_accessed=4 * 2**20, transcendentals=0),
         name="advance_twice",
     )(c2d, c2d, *small)
 
@@ -235,15 +235,19 @@
     c2d = species.reshape(nspec * cells_x, merged)
     faces = pack(c2d, cell_factor)
     xl, xh, yl, yh = (shift_to(v, dx, dy) for v, (dx, dy) in zip(faces, [(-1, 0), (1, 0), (0, -1), (0, 1)]))
-    lo, hi, copies = corners(xl, xh, factor_x, n_tx)
+    lo, hi, copies = corners(xl, xh, factor_x, n_tx // 2)
     corner = shift_to(lo, 0, -1), shift_to(hi, 0, 1)
-    whole_x = lax.all_to_all(copies, "tx", 0, 0, tiled=True).reshape(-1, factor_x.shape[1])
+    copies = copies.reshape(n_tx, cells_x // 2, factor_x.shape[1])
+    mine = lax.all_to_all(copies, "tx", 0, 0, tiled=True)
+    other = lax.ppermute(mine, "tx", [(i, i ^ 1) for i in range(n_tx)])
     faces, rate = (xl, xh, yl, yh), species_rate[:, None]
     sides = advance(c2d, cell_factor, rate, faces)
-    advanced, planes = reduce_species(sides, cell_factor, rate, faces, corner, factor_species.T, whole_x)
+    advanced, planes = reduce_species(sides, cell_factor, rate, faces, corner, factor_species.T, mine)
     planes = planes.reshape(depth, cells_x, cells_y * ranks_q)
-    planes = lax.all_to_all(planes, "tx", 0, 0, tiled=True).reshape(-1, cells_y * ranks_q)
-    first = lax.dot_general(planes, whole_x, (((0,), (0,)), ((), ())), precision=exact_mode)
+    planes = lax.all_to_all(planes, "tx", 0, 0, tiled=True)
+    even = lax.axis_index("tx") % 2 == 0
+    whole_x = jnp.concatenate([jnp.where(even, mine, other), jnp.where(even, other, mine)], axis=1)
+    first = lax.dot_general(planes, whole_x, (((0, 1), (0, 1)), ((), ())), precision=exact_mode)
     first = first.reshape(cells_y, ranks_q, -1).transpose(1, 0, 2)
     sent = jnp.concatenate([first, jnp.broadcast_to(factor_y[None], (n_ty,) + factor_y.shape)], axis=1)
     came = lax.all_to_all(sent, "ty", 0, 0, tiled=True)

time: 127 us -> 129 us (1.016)
  blocking collectives: 75 us -> 56.2 us
  waiting for transfers between devices: 7.8 us -> 17.5 us
  starting transfers between devices: 29.4 us -> 38.5 us
    all_to_all x1 -> x0, blocking collectives: 21.5 us -> none  [body(): lax.all_to_all(planes, 'tx', 0, 0, tiled=True)]
    all_to_all x1 -> x2, waiting for transfers between devices: 6.41 us -> 14.9 us  [the longest x1 13.1 us: body(): planes = lax.all_to_all(planes, 'tx', 0, 0, tiled=True)]
    all_to_all x1 -> x2, starting transfers between devices: 7.4 us -> 14.5 us  [the longest x1 7.4 us: body(): mine = lax.all_to_all(copies, 'tx', 0, 0, tiled=True)]
    all_to_all x1, blocking collectives: 23.9 us -> 26.6 us  [body(): came = lax.all_to_all(sent, 'ty', 0, 0, tiled=True)]
    ppermute x0 -> x1, starting transfers between devices: none -> 2.14 us  [body(): other = lax.ppermute(mine, 'tx', [(i, i ^ 1) for i in range(n_tx)])]
  transfers between devices with their start and end apart: 7 -> 9, of which waited for: 2 -> 4; matrix products, arithmetic and copies ran while one was open for 0% -> 0% of each run, Pallas kernels for 4% -> 4%
where the time goes in v12:
time: 129 us; the launch traced here: 128 us
  blocking collectives  56.2 us (44%)
  starting transfers between devices  38.5 us (30%)
  waiting for transfers between devices  17.5 us (14%)
  Pallas kernels  8.02 us (6%)
  local copies, waits for them, and re-layouts  5.33 us (4%)
  matrix products  1.46 us (1%)
    all_to_all x1, blocking collectives, body(): core = lax.all_to_all(plane, ('tx', 'ty'), 0, 0, tiled=True)  29.6 us
    all_to_all x1, blocking collectives, body(): came = lax.all_to_all(sent, 'ty', 0, 0, tiled=True)  26.6 us
    ppermute x6, starting transfers between devices, shift_to(): lax.ppermute(v, axis, [(i, i + step) for i in range(count) if 0 <= i + st...  21.8 us
    all_to_all x1, waiting for transfers between devices, body(): planes = lax.all_to_all(planes, 'tx', 0, 0, tiled=True)  13.1 us
    all_to_all x1, starting transfers between devices, body(): mine = lax.all_to_all(copies, 'tx', 0, 0, tiled=True)  7.4 us
    all_to_all x1, starting transfers between devices, body(): planes = lax.all_to_all(planes, 'tx', 0, 0, tiled=True)  7.12 us
    unnamed x17, local copies, waits for them, and re-layouts  4.1 us
    pallas_call x1, Pallas kernels, advance(): pl.pallas_call(advance_kernel, grid=(1,), out_shape=[jax.ShapeDtypeStruct...  4.04 us
  transfers between devices with their start and end apart: 9, of which 4 were waited for; matrix products, arithmetic and copies ran while one was open for 0% of the time, Pallas kernels for 4%

profile of v12, /device:TPU:1, one launch (start us, length us, event | category | flops | bytes accessed | tf_op | source)
XLA Modules:
  0.0 127.9 jit_solution(2877155489282711215)
XLA Ops:
  0.6 1.2 copy-done
  1.9 0.8 copy-done.2
  2.6 0.7 pack_faces.1
  3.4 1.3 %collective-permute-start.2 = (f32[544,128]{1,0:T(8,128)S(1)}, f32[544,128]{1,0:T(8,128)S(1)}, u32[]{:S(2)}, u32[]{:S(2)}) collective-permute-start(f32[544,128]{1,0:T(8,128)S(1)} %get-tuple-element.15), channel_id=1, source_target_pairs={{1,0},{2,1},{3,2},{4,3},{5,4},{6,5},{7,6},{8,7},{9,8},{10,9},{11,1... | collective-permute-start | bytes 835592 | tf_op jit(solution)/shard_map/ppermute | solution.py:226
  4.7 4.6 %collective-permute-start.3 = (f32[544,128]{1,0:T(8,128)S(1)}, f32[544,128]{1,0:T(8,128)S(1)}, u32[]{:S(2)}, u32[]{:S(2)}) collective-permute-start(f32[544,128]{1,0:T(8,128)S(1)} %get-tuple-element.16), channel_id=1, source_target_pairs={{0,1},{1,2},{2,3},{3,4},{4,5},{5,6},{6,7},{7,8},{8,9},{9,10},{10,1... | collective-permute-start | bytes 835592 | tf_op jit(solution)/shard_map/ppermute | solution.py:226
  9.3 8.8 %collective-permute-start = (f32[72,256]{1,0:T(8,128)S(1)}, f32[72,256]{1,0:T(8,128)S(1)}, u32[]{:S(2)}, u32[]{:S(2)}) collective-permute-start(f32[72,256]{1,0:T(8,128)S(1)} %get-tuple-element.13), channel_id=1, source_target_pairs={{16,0},{32,16},{48,32},{64,48},{80,64},{96,80},{112,96},{128,112},... | collective-permute-start | bytes 221192 | tf_op jit(solution)/shard_map/ppermute | solution.py:226
  18.0 1.9 %collective-permute-start.1 = (f32[72,256]{1,0:T(8,128)S(1)}, f32[72,256]{1,0:T(8,128)S(1)}, u32[]{:S(2)}, u32[]{:S(2)}) collective-permute-start(f32[72,256]{1,0:T(8,128)S(1)} %get-tuple-element.14), channel_id=1, source_target_pairs={{0,16},{16,32},{32,48},{48,64},{64,80},{80,96},{96,112},{112,128},... | collective-permute-start | bytes 221192 | tf_op jit(solution)/shard_map/ppermute | solution.py:226
  20.0 1.4 %collective-permute-done.1.xh_ref.kxh_ref = f32[72,256]{1,0:T(8,128)S(1)} collective-permute-done((f32[72,256]{1,0:T(8,128)S(1)}, f32[72,256]{1,0:T(8,128)S(1)}, u32[]{:S(2)}, u32[]{:S(2)}) %collective-permute-start.1) | collective-permute-done | bytes 73760 | tf_op jit(solution)/shard_map/ppermute | solution.py:226
  21.3 0.7 corner_columns.1
  22.1 7.4 %all-to-all-start = ((f32[32,16,128]{2,1,0:T(8,128)}), f32[32,16,128]{2,1,0:T(8,128)S(1)}, u32[]{:S(2)}, u32[]{:S(2)}) async-start(f32[32,16,128]{2,1,0:T(8,128)} %bitcast.3), calls=%async_computation | async-start | bytes 524288 | tf_op jit(solution)/shard_map/all_to_all | solution.py:241
  29.5 0.6 copy-done.7
  30.2 1.3 %collective-permute-start.4 = (f32[64,128]{1,0:T(8,128)S(1)}, f32[64,128]{1,0:T(8,128)S(1)}, u32[]{:S(2)}, u32[]{:S(2)}) collective-permute-start(f32[64,128]{1,0:T(8,128)S(1)} %get-tuple-element.19), channel_id=1, source_target_pairs={{1,0},{2,1},{3,2},{4,3},{5,4},{6,5},{7,6},{8,7},{9,8},{10,9},{11,1... | collective-permute-start | bytes 98312 | tf_op jit(solution)/shard_map/ppermute | solution.py:226
  31.5 4.0 %collective-permute-start.5 = (f32[64,128]{1,0:T(8,128)S(1)}, f32[64,128]{1,0:T(8,128)S(1)}, u32[]{:S(2)}, u32[]{:S(2)}) collective-permute-start(f32[64,128]{1,0:T(8,128)S(1)} %get-tuple-element.20), channel_id=1, source_target_pairs={{0,1},{1,2},{2,3},{3,4},{4,5},{5,6},{6,7},{7,8},{8,9},{9,10},{10,1... | collective-permute-start | bytes 98312 | tf_op jit(solution)/shard_map/ppermute | solution.py:226
  35.6 4.0 %advance_twice.1 = (f32[1024,128]{1,0:T(8,128)S(1)}, f32[1024,128]{1,0:T(8,128)S(1)}) custom-call(f32[1024,256]{1,0:T(8,128)S(1)} %bitcast.41, f32[1024,256]{1,0:T(8,128)S(1)} %bitcast.42, f32[32,256]{1,0:T(8,128)S(1)} %copy-done.3, f32[32,1]{1,0:T(8,128)S(1)} %copy.19.rate_ref, f32[72,256]{1,0:T(8,128)S(1)} %collective-permute-done.xl_ref.kxl_ref, ...), custom_call_target="tpu_custom_call" | custom-call | flops 4000000000 | bytes 4194304 | tf_op jit(solution)/shard_map/advance_twice/pallas_call | solution.py:142
  39.6 1.8 %all-to-all-done.whole_ref = f32[32,16,128]{2,1,0:T(8,128)S(1)} async-done(((f32[32,16,128]{2,1,0:T(8,128)}), f32[32,16,128]{2,1,0:T(8,128)S(1)}, u32[]{:S(2)}, u32[]{:S(2)}) %all-to-all-start) | async-done | bytes 262176 | tf_op jit(solution)/shard_map/all_to_all | solution.py:241
  41.4 2.5 %reduce_species.1 = (f32[1024,256]{1,0:T(8,128)}, f32[1024,128]{1,0:T(8,128)}) custom-call(f32[1024,128]{1,0:T(8,128)S(1)} %get-tuple-element.17.a0_ref, f32[1024,128]{1,0:T(8,128)S(1)} %get-tuple-element.18.a1_ref, f32[32,256]{1,0:T(8,128)S(1)} %copy-done.3, f32[32,1]{1,0:T(8,128)S(1)} %copy.19.rate_ref, f32[72,256]{1,0:T(8,128)S(1)} %collective-permute-done.xl_ref.kxl_ref, ...), custom_call_target="tpu_custom_call" | custom-call | tf_op jit(solution)/shard_map/reduce_species/pallas_call | solution.py:208
  43.9 7.1 %all-to-all-start.1 = ((f32[32,32,128]{2,1,0:T(8,128)}), f32[32,32,128]{2,1,0:T(8,128)S(1)}, u32[]{:S(2)}, u32[]{:S(2)}) async-start(f32[32,32,128]{2,1,0:T(8,128)} %bitcast.5), calls=%async_computation.1 | async-start | bytes 1048576 | tf_op jit(solution)/shard_map/all_to_all | solution.py:247
  51.0 2.1 %collective-permute-start.6 = (f32[32,16,128]{2,1,0:T(8,128)S(1)}, f32[32,16,128]{2,1,0:T(8,128)S(1)}, u32[]{:S(2)}, u32[]{:S(2)}) collective-permute-start(f32[32,16,128]{2,1,0:T(8,128)S(1)} %all-to-all-done.whole_ref), channel_id=1, source_target_pairs={{0,16},{16,0},{32,48},{48,32},{64,80},{80,64},{96,112},{112,96},{1... | collective-permute-start | bytes 786440 | tf_op jit(solution)/shard_map/ppermute | solution.py:242
  53.2 1.3 collective-permute-done.6
  54.5 13.1 %all-to-all-done.1 = f32[32,32,128]{2,1,0:T(8,128)S(1)} async-done(((f32[32,32,128]{2,1,0:T(8,128)}), f32[32,32,128]{2,1,0:T(8,128)S(1)}, u32[]{:S(2)}, u32[]{:S(2)}) %all-to-all-start.1) | async-done | bytes 524320 | tf_op jit(solution)/shard_map/all_to_all | solution.py:247
  67.6 1.0 fusion
  69.3 26.6 %all_to_all.20 = f32[16,16,128]{2,1,0:T(8,128)S(1)} all-to-all(f32[16,16,128]{2,1,0:T(8,128)S(1)} %pad_maximum_fusion), channel_id=1, replica_groups=mesh['tx'=32,'ty'=16] {'ty'}, dimensions={0} | all-to-all | bytes 262144 | tf_op jit(solution)/shard_map/all_to_all | solution.py:253
  97.2 29.6 %all_to_all.21 = f32[512,1,32]{2,1,0:T(1,128)S(1)} all-to-all(f32[512,1,32]{2,1,0:T(1,128)S(1)} %copy.27), channel_id=1, replica_groups=mesh['tx'=32,'ty'=16] {'tx','ty'}, dimensions={0} | all-to-all | bytes 131072 | tf_op jit(solution)/shard_map/all_to_all | solution.py:260
  127.1 0.8 copy.29
  (32 shorter events, 2.4 us)
Async XLA Ops:
  0.6 1.2 copy-start
  1.9 0.8 copy-start.2
  2.6 18.7 %copy-start.4 = (f32[32,128]{1,0:T(8,128)S(1)}, f32[32,128]{1,0:T(8,128)}, u32[]{:S(2)}) copy-start(f32[32,128]{1,0:T(8,128)} %fx_ref.1) | copy-start | bytes 49156
  2.6 32.9 %copy-start.1 = (f32[32,32,256]{2,1,0:T(8,128)S(1)}, f32[32,32,256]{2,1,0:T(8,128)}, u32[]{:S(2)}) copy-start(f32[32,32,256]{2,1,0:T(8,128)} %param.6) | copy-start | bytes 3145732
  3.4 32.2 %collective-permute-start.2 = (f32[544,128]{1,0:T(8,128)S(1)}, f32[544,128]{1,0:T(8,128)S(1)}, u32[]{:S(2)}, u32[]{:S(2)}) collective-permute-start(f32[544,128]{1,0:T(8,128)S(1)} %get-tuple-element.15), channel_id=1, source_target_pairs={{1,0},{2,1},{3,2},{4,3},{5,4},{6,5},{7,6},{8,7},{9,8},{10,9},{11,1... | collective-permute-start | bytes 835592 | tf_op jit(solution)/shard_map/ppermute | solution.py:226
  4.7 30.9 %collective-permute-start.3 = (f32[544,128]{1,0:T(8,128)S(1)}, f32[544,128]{1,0:T(8,128)S(1)}, u32[]{:S(2)}, u32[]{:S(2)}) collective-permute-start(f32[544,128]{1,0:T(8,128)S(1)} %get-tuple-element.16), channel_id=1, source_target_pairs={{0,1},{1,2},{2,3},{3,4},{4,5},{5,6},{6,7},{7,8},{8,9},{9,10},{10,1... | collective-permute-start | bytes 835592 | tf_op jit(solution)/shard_map/ppermute | solution.py:226
  9.3 10.7 %collective-permute-start = (f32[72,256]{1,0:T(8,128)S(1)}, f32[72,256]{1,0:T(8,128)S(1)}, u32[]{:S(2)}, u32[]{:S(2)}) collective-permute-start(f32[72,256]{1,0:T(8,128)S(1)} %get-tuple-element.13), channel_id=1, source_target_pairs={{16,0},{32,16},{48,32},{64,48},{80,64},{96,80},{112,96},{128,112},... | collective-permute-start | bytes 221192 | tf_op jit(solution)/shard_map/ppermute | solution.py:226
  18.0 3.3 %collective-permute-start.1 = (f32[72,256]{1,0:T(8,128)S(1)}, f32[72,256]{1,0:T(8,128)S(1)}, u32[]{:S(2)}, u32[]{:S(2)}) collective-permute-start(f32[72,256]{1,0:T(8,128)S(1)} %get-tuple-element.14), channel_id=1, source_target_pairs={{0,16},{16,32},{32,48},{48,64},{64,80},{80,96},{96,112},{112,128},... | collective-permute-start | bytes 221192 | tf_op jit(solution)/shard_map/ppermute | solution.py:226
  22.1 13.5 %copy-start.3 = (f32[32,256]{1,0:T(8,128)S(1)}, f32[32,256]{1,0:T(8,128)}, u32[]{:S(2)}) copy-start(f32[32,256]{1,0:T(8,128)} %k_ref.5) | copy-start | bytes 98308
  22.1 19.3 %all-to-all-start = ((f32[32,16,128]{2,1,0:T(8,128)}), f32[32,16,128]{2,1,0:T(8,128)S(1)}, u32[]{:S(2)}, u32[]{:S(2)}) async-start(f32[32,16,128]{2,1,0:T(8,128)} %bitcast.3), calls=%async_computation | async-start | bytes 524288 | tf_op jit(solution)/shard_map/all_to_all | solution.py:241
  29.5 0.7 copy-start.7
  30.2 9.4 %collective-permute-start.4 = (f32[64,128]{1,0:T(8,128)S(1)}, f32[64,128]{1,0:T(8,128)S(1)}, u32[]{:S(2)}, u32[]{:S(2)}) collective-permute-start(f32[64,128]{1,0:T(8,128)S(1)} %get-tuple-element.19), channel_id=1, source_target_pairs={{1,0},{2,1},{3,2},{4,3},{5,4},{6,5},{7,6},{8,7},{9,8},{10,9},{11,1... | collective-permute-start | bytes 98312 | tf_op jit(solution)/shard_map/ppermute | solution.py:226
  31.5 8.1 %collective-permute-start.5 = (f32[64,128]{1,0:T(8,128)S(1)}, f32[64,128]{1,0:T(8,128)S(1)}, u32[]{:S(2)}, u32[]{:S(2)}) collective-permute-start(f32[64,128]{1,0:T(8,128)S(1)} %get-tuple-element.20), channel_id=1, source_target_pairs={{0,1},{1,2},{2,3},{3,4},{4,5},{5,6},{6,7},{7,8},{8,9},{9,10},{10,1... | collective-permute-start | bytes 98312 | tf_op jit(solution)/shard_map/ppermute | solution.py:226
  35.6 5.9 %copy-start.5 = (f32[32,16]{0,1:T(8,128)S(1)}, f32[32,16]{0,1:T(8,128)}, u32[]{:S(2)}) copy-start(f32[32,16]{0,1:T(8,128)} %param.11) | copy-start | bytes 6148
  43.9 23.7 %all-to-all-start.1 = ((f32[32,32,128]{2,1,0:T(8,128)}), f32[32,32,128]{2,1,0:T(8,128)S(1)}, u32[]{:S(2)}, u32[]{:S(2)}) async-start(f32[32,32,128]{2,1,0:T(8,128)} %bitcast.5), calls=%async_computation.1 | async-start | bytes 1048576 | tf_op jit(solution)/shard_map/all_to_all | solution.py:247
  51.0 3.4 %collective-permute-start.6 = (f32[32,16,128]{2,1,0:T(8,128)S(1)}, f32[32,16,128]{2,1,0:T(8,128)S(1)}, u32[]{:S(2)}, u32[]{:S(2)}) collective-permute-start(f32[32,16,128]{2,1,0:T(8,128)S(1)} %all-to-all-done.whole_ref), channel_id=1, source_target_pairs={{0,16},{16,0},{32,48},{48,32},{64,80},{80,64},{96,112},{112,96},{1... | collective-permute-start | bytes 786440 | tf_op jit(solution)/shard_map/ppermute | solution.py:242
  68.6 0.7 copy-start.6

commit v13 on v10

--- a/solution.py
+++ b/solution.py
@@ -156,9 +156,10 @@
     )(c2d, c2d, *small)
 
 
-def reduce_kernel(a0_ref, a1_ref, k_ref, rate_ref, kxl_ref, kxh_ref, kyl_ref, kyh_ref, cl_ref, ch_ref, fs_ref, fx_ref,
-                  adv_ref, planes_ref, left, right):
+def reduce_kernel(a0_ref, a1_ref, k_ref, rate_ref, kxl_ref, kxh_ref, kyl_ref, kyh_ref, cl_ref, ch_ref, fs_ref, fx_ref, fy_ref,
+                  adv_ref, planes_ref, fy_out_ref, left, right, flip):
     left[...], right[...] = a0_ref[...], a1_ref[...]
+    fy_out_ref[...] = fy_ref[...]
     rate = jnp.broadcast_to(rate_ref[...], (NS, 128))
     first_y, last_y = lanes(NS) < NZ, lanes(NS) >= 128 - NZ
     for x, at, kx_ref in ((0, 0, kxh_ref), (NX - 1, NS, kxl_ref)):
@@ -196,30 +197,30 @@
             for p, r in (a, b):
                 swapped.append(jnp.where(even_q, p, pltpu.roll(r, 32, 1)))
                 swapped.append(jnp.where(even_q, pltpu.roll(p, 96, 1), r))
-        turned = jnp.concatenate(swapped, axis=0).T
+        flip[group * 128 : (group + 1) * 128, :] = jnp.concatenate(swapped, axis=0).T
         for g in range(4):
             side, x = divmod(group * 4 + g, NX // 2)
             for e in range(2):
                 to = pl.ds(side * SENT + e * (NX // 2) + x, NZ // 2, stride=2 * SENT)
-                planes_ref[to, :] = turned[g * NZ + e * (NZ // 2) : g * NZ + (e + 1) * (NZ // 2), :]
-
-
-def reduce_species(sides, k, rate, faces, corner, fs, factor_x):
+                planes_ref[to, :] = flip[pl.ds(group * 128 + g * NZ + e, NZ // 2, stride=2), :]
+
+
+def reduce_species(sides, k, rate, faces, corner, fs, factor_x, factor_y):
     xl, xh, yl, yh = faces
     tail_x, tail_y = pl.BlockSpec((8, NV), lambda i: (2 * NS // 8, 0)), pl.BlockSpec((NX, 128), lambda i: (NS // 2, 0))
-    shapes = [(NS * NX, NV), (NZ * SENT, 128)]
+    shapes = [(NS * NX, NV), (NZ * SENT, 128), factor_y.shape]
     return pl.pallas_call(
         reduce_kernel,
         grid=(1,),
         out_shape=[jax.ShapeDtypeStruct(s, f32) for s in shapes],
         in_specs=[whole_block(v.shape) for v in (*sides, k, rate)]
         + [tail_x, tail_x, tail_y, tail_y]
-        + [whole_block(v.shape) for v in (*corner, fs, factor_x)],
+        + [whole_block(v.shape) for v in (*corner, fs, factor_x, factor_y)],
         out_specs=[whole_block(s) for s in shapes],
-        scratch_shapes=[pltpu.VMEM((NS * NX, 128), f32)] * 2,
+        scratch_shapes=[pltpu.VMEM((NS * NX, 128), f32)] * 3,
         compiler_params=pltpu.CompilerParams(vmem_limit_bytes=12 * 2**20),
         name="reduce_species",
-    )(*sides, k, rate, xl, xh, yl, yh, *corner, fs, factor_x)
+    )(*sides, k, rate, xl, xh, yl, yh, *corner, fs, factor_x, factor_y)
 
 
 def shift_to(v, dx, dy):
@@ -241,7 +242,7 @@
     corner = shift_to(lo, 0, -1), shift_to(hi, 0, 1)
     faces, rate = (xl, xh, yl, yh), species_rate[:, None]
     sides = advance(c2d, cell_factor, rate, faces)
-    advanced, planes = reduce_species(sides, cell_factor, rate, faces, corner, factor_species.T, factor_x)
+    advanced, planes, factor_y = reduce_species(sides, cell_factor, rate, faces, corner, factor_species.T, factor_x, factor_y)
     planes = planes.reshape(n_tx, SENT, cells_y * ranks_q)
     planes = lax.all_to_all(planes, "tx", 0, 0, tiled=True)
     side, half = lax.axis_index("tx") % 2, cells_x // 2
@@ -262,7 +263,7 @@
     plane = plane.reshape(n_tx, rank_a // n_tx, n_ty, rank_b // n_ty).transpose(0, 2, 1, 3)
     plane = plane.reshape(n_tx * n_ty, 1, -1)
     core = lax.all_to_all(plane, ("tx", "ty"), 0, 0, tiled=True)
-    core = core.reshape(depth // 2, 2, ranks_q, rank_a // n_tx, rank_b // n_ty).transpose(3, 2, 4, 1, 0)
+    core = core.reshape(depth, ranks_q, rank_a // n_tx, rank_b // n_ty).transpose(2, 1, 3, 0)
     return advanced.reshape(species.shape), core.reshape(rank_a // n_tx, ranks_q, -1)
 
 

time: 129 us -> 127 us (0.984)
  local copies, waits for them, and re-layouts: 6.35 us -> 4.75 us
    reshape x2 -> x1, local copies, waits for them, and re-layouts: 2.06 us -> 0.21 us  [body(): core.reshape(depth, ranks_q, rank_a // n_tx, rank_b // n_ty)]
    unnamed x16 -> x17, local copies, waits for them, and re-layouts: 2.65 us -> 3.45 us
where the time goes in v13:
time: 127 us
  blocking collectives  54.5 us (43%)
  starting transfers between devices  33.9 us (27%)
  waiting for transfers between devices  23.4 us (18%)
  Pallas kernels  7.54 us (6%)
  local copies, waits for them, and re-layouts  4.75 us (4%)
  matrix products  1.78 us (1%)
    all_to_all x1, blocking collectives, body(): core = lax.all_to_all(plane, ('tx', 'ty'), 0, 0, tiled=True)  28 us
    all_to_all x1, blocking collectives, body(): came = lax.all_to_all(sent, 'ty', 0, 0, tiled=True)  26.5 us
    ppermute x6, starting transfers between devices, shift_to(): lax.ppermute(v, axis, [(i, i + step) for i in range(count) if 0 <= i + st...  21.8 us
    all_to_all x1, waiting for transfers between devices, body(): planes = lax.all_to_all(planes, 'tx', 0, 0, tiled=True)  21.2 us
    all_to_all x1, starting transfers between devices, body(): planes = lax.all_to_all(planes, 'tx', 0, 0, tiled=True)  7.83 us
    ppermute x1, starting transfers between devices, body(): lax.ppermute(over_x(1 - side), 'tx', [(i, i ^ 1) for i in range(n_tx)])  4.22 us
    pallas_call x1, Pallas kernels, advance(): pl.pallas_call(advance_kernel, grid=(1,), out_shape=[jax.ShapeDtypeStruct...  4.05 us
    unnamed x17, local copies, waits for them, and re-layouts  3.45 us
  transfers between devices with their start and end apart: 8, of which 3 were waited for; matrix products, arithmetic and copies ran while one was open for 0% of the time, Pallas kernels for 3%

profile of v13, /device:TPU:1, one launch (start us, length us, event | category | flops | bytes accessed | tf_op | source)
XLA Modules:
  0.0 126.7 jit_solution(15785053770092776934)
XLA Ops:
  0.6 1.2 copy-done
  1.9 0.8 copy-done.2
  2.6 0.7 pack_faces.1
  3.4 1.3 %collective-permute-start.2 = (f32[544,128]{1,0:T(8,128)S(1)}, f32[544,128]{1,0:T(8,128)S(1)}, u32[]{:S(2)}, u32[]{:S(2)}) collective-permute-start(f32[544,128]{1,0:T(8,128)S(1)} %get-tuple-element.15), channel_id=1, source_target_pairs={{1,0},{2,1},{3,2},{4,3},{5,4},{6,5},{7,6},{8,7},{9,8},{10,9},{11,1... | collective-permute-start | bytes 835592 | tf_op jit(solution)/shard_map/ppermute | solution.py:229
  4.7 4.6 %collective-permute-start.3 = (f32[544,128]{1,0:T(8,128)S(1)}, f32[544,128]{1,0:T(8,128)S(1)}, u32[]{:S(2)}, u32[]{:S(2)}) collective-permute-start(f32[544,128]{1,0:T(8,128)S(1)} %get-tuple-element.16), channel_id=1, source_target_pairs={{0,1},{1,2},{2,3},{3,4},{4,5},{5,6},{6,7},{7,8},{8,9},{9,10},{10,1... | collective-permute-start | bytes 835592 | tf_op jit(solution)/shard_map/ppermute | solution.py:229
  9.3 8.8 %collective-permute-start = (f32[72,256]{1,0:T(8,128)S(1)}, f32[72,256]{1,0:T(8,128)S(1)}, u32[]{:S(2)}, u32[]{:S(2)}) collective-permute-start(f32[72,256]{1,0:T(8,128)S(1)} %get-tuple-element.13), channel_id=1, source_target_pairs={{16,0},{32,16},{48,32},{64,48},{80,64},{96,80},{112,96},{128,112},... | collective-permute-start | bytes 221192 | tf_op jit(solution)/shard_map/ppermute | solution.py:229
  18.0 1.9 %collective-permute-start.1 = (f32[72,256]{1,0:T(8,128)S(1)}, f32[72,256]{1,0:T(8,128)S(1)}, u32[]{:S(2)}, u32[]{:S(2)}) collective-permute-start(f32[72,256]{1,0:T(8,128)S(1)} %get-tuple-element.14), channel_id=1, source_target_pairs={{0,16},{16,32},{32,48},{48,64},{64,80},{80,96},{96,112},{112,128},... | collective-permute-start | bytes 221192 | tf_op jit(solution)/shard_map/ppermute | solution.py:229
  20.1 1.3 %collective-permute-done.1.xh_ref.kxh_ref = f32[72,256]{1,0:T(8,128)S(1)} collective-permute-done((f32[72,256]{1,0:T(8,128)S(1)}, f32[72,256]{1,0:T(8,128)S(1)}, u32[]{:S(2)}, u32[]{:S(2)}) %collective-permute-start.1) | collective-permute-done | bytes 73760 | tf_op jit(solution)/shard_map/ppermute | solution.py:229
  21.4 1.3 %collective-permute-start.4 = (f32[64,128]{1,0:T(8,128)S(1)}, f32[64,128]{1,0:T(8,128)S(1)}, u32[]{:S(2)}, u32[]{:S(2)}) collective-permute-start(f32[64,128]{1,0:T(8,128)S(1)} %get-tuple-element.19), channel_id=1, source_target_pairs={{1,0},{2,1},{3,2},{4,3},{5,4},{6,5},{7,6},{8,7},{9,8},{10,9},{11,1... | collective-permute-start | bytes 98312 | tf_op jit(solution)/shard_map/ppermute | solution.py:229
  22.6 4.0 %collective-permute-start.5 = (f32[64,128]{1,0:T(8,128)S(1)}, f32[64,128]{1,0:T(8,128)S(1)}, u32[]{:S(2)}, u32[]{:S(2)}) collective-permute-start(f32[64,128]{1,0:T(8,128)S(1)} %get-tuple-element.20), channel_id=1, source_target_pairs={{0,1},{1,2},{2,3},{3,4},{4,5},{5,6},{6,7},{7,8},{8,9},{9,10},{10,1... | collective-permute-start | bytes 98312 | tf_op jit(solution)/shard_map/ppermute | solution.py:229
  26.7 4.0 %advance_twice.1 = (f32[1024,128]{1,0:T(8,128)S(1)}, f32[1024,128]{1,0:T(8,128)S(1)}) custom-call(f32[1024,256]{1,0:T(8,128)S(1)} %bitcast.43, f32[1024,256]{1,0:T(8,128)S(1)} %bitcast.44, f32[32,256]{1,0:T(8,128)S(1)} %copy-done.3, f32[32,1]{1,0:T(8,128)S(1)} %copy.21.rate_ref, f32[72,256]{1,0:T(8,128)S(1)} %collective-permute-done.xl_ref.kxl_ref, ...), custom_call_target="tpu_custom_call" | custom-call | flops 10000000000 | bytes 4194304 | tf_op jit(solution)/shard_map/advance_twice/pallas_call | solution.py:142
  30.8 0.6 copy-done.6
  31.5 2.8 %reduce_species.1 = (f32[1024,256]{1,0:T(8,128)}, f32[1536,128]{1,0:T(8,128)}, f32[8,128]{1,0:T(8,128)S(1)}) custom-call(f32[1024,128]{1,0:T(8,128)S(1)} %get-tuple-element.17.a0_ref, f32[1024,128]{1,0:T(8,128)S(1)} %get-tuple-element.18.a1_ref, f32[32,256]{1,0:T(8,128)S(1)} %copy-done.3, f32[32,1]{1,0:T(8,128)S(1)} %copy.21.rate_ref, ...), custom_call_target="tpu_custom_call" | custom-call | tf_op jit(solution)/shard_map/reduce_species/pallas_call | solution.py:212
  34.2 7.8 %all-to-all-start = ((f32[32,48,128]{2,1,0:T(8,128)}), f32[32,48,128]{2,1,0:T(8,128)S(1)}, u32[]{:S(2)}, u32[]{:S(2)}) async-start(f32[32,48,128]{2,1,0:T(8,128)} %bitcast.4), calls=%async_computation | async-start | bytes 1572864 | tf_op jit(solution)/shard_map/all_to_all | solution.py:247
  42.1 21.2 %all-to-all-done = f32[32,48,128]{2,1,0:T(8,128)S(1)} async-done(((f32[32,48,128]{2,1,0:T(8,128)}), f32[32,48,128]{2,1,0:T(8,128)S(1)}, u32[]{:S(2)}, u32[]{:S(2)}) %all-to-all-start) | async-done | bytes 786464 | tf_op jit(solution)/shard_map/all_to_all | solution.py:247
  63.3 0.7 convolution_bitcast_fusion.1
  64.0 4.2 %collective-permute-start.6 = (f32[128,128]{1,0:T(8,128)S(1)}, f32[128,128]{1,0:T(8,128)S(1)}, u32[]{:S(2)}, u32[]{:S(2)}) collective-permute-start(f32[128,128]{1,0:T(8,128)S(1)} %convolution_bitcast_fusion.1), channel_id=1, source_target_pairs={{0,16},{16,0},{32,48},{48,32},{64,80},{80,64},{96,112},{112,96},{1... | collective-permute-start | bytes 196616 | tf_op jit(solution)/shard_map/ppermute | solution.py:254
  68.2 0.9 collective-permute-done.6
  69.1 0.7 fusion
  69.8 26.5 %all_to_all.15 = f32[16,16,128]{2,1,0:T(8,128)S(1)} all-to-all(f32[16,16,128]{2,1,0:T(8,128)S(1)} %pad_maximum_fusion), channel_id=1, replica_groups=mesh['tx'=32,'ty'=16] {'ty'}, dimensions={0} | all-to-all | bytes 262144 | tf_op jit(solution)/shard_map/all_to_all | solution.py:258
  96.5 0.5 convolution_bitcast_fusion
  97.2 0.3 reshape.41
  97.6 28.0 %all_to_all.16 = f32[512,1,32]{2,1,0:T(1,128)S(1)} all-to-all(f32[512,1,32]{2,1,0:T(1,128)S(1)} %copy.32), channel_id=1, replica_groups=mesh['tx'=32,'ty'=16] {'tx','ty'}, dimensions={0} | all-to-all | bytes 131072 | tf_op jit(solution)/shard_map/all_to_all | solution.py:265
  125.9 0.8 copy.34
  (31 shorter events, 1.1 us)
Async XLA Ops:
  0.6 1.2 copy-start
  1.9 0.8 copy-start.2
  2.6 24.0 %copy-start.1 = (f32[32,32,256]{2,1,0:T(8,128)S(1)}, f32[32,32,256]{2,1,0:T(8,128)}, u32[]{:S(2)}) copy-start(f32[32,32,256]{2,1,0:T(8,128)} %param.6) | copy-start | bytes 3145732
  3.4 23.3 %collective-permute-start.2 = (f32[544,128]{1,0:T(8,128)S(1)}, f32[544,128]{1,0:T(8,128)S(1)}, u32[]{:S(2)}, u32[]{:S(2)}) collective-permute-start(f32[544,128]{1,0:T(8,128)S(1)} %get-tuple-element.15), channel_id=1, source_target_pairs={{1,0},{2,1},{3,2},{4,3},{5,4},{6,5},{7,6},{8,7},{9,8},{10,9},{11,1... | collective-permute-start | bytes 835592 | tf_op jit(solution)/shard_map/ppermute | solution.py:229
  4.7 22.0 %collective-permute-start.3 = (f32[544,128]{1,0:T(8,128)S(1)}, f32[544,128]{1,0:T(8,128)S(1)}, u32[]{:S(2)}, u32[]{:S(2)}) collective-permute-start(f32[544,128]{1,0:T(8,128)S(1)} %get-tuple-element.16), channel_id=1, source_target_pairs={{0,1},{1,2},{2,3},{3,4},{4,5},{5,6},{6,7},{7,8},{8,9},{9,10},{10,1... | collective-permute-start | bytes 835592 | tf_op jit(solution)/shard_map/ppermute | solution.py:229
  9.3 10.8 %collective-permute-start = (f32[72,256]{1,0:T(8,128)S(1)}, f32[72,256]{1,0:T(8,128)S(1)}, u32[]{:S(2)}, u32[]{:S(2)}) collective-permute-start(f32[72,256]{1,0:T(8,128)S(1)} %get-tuple-element.13), channel_id=1, source_target_pairs={{16,0},{32,16},{48,32},{64,48},{80,64},{96,80},{112,96},{128,112},... | collective-permute-start | bytes 221192 | tf_op jit(solution)/shard_map/ppermute | solution.py:229
  18.0 1.9 %copy-start.7 = (f32[32]{0:T(128)S(1)}, f32[32]{0:T(128)}, u32[]{:S(2)}) copy-start(f32[32]{0:T(128)} %param.8) | copy-start | bytes 388
  18.0 3.3 %collective-permute-start.1 = (f32[72,256]{1,0:T(8,128)S(1)}, f32[72,256]{1,0:T(8,128)S(1)}, u32[]{:S(2)}, u32[]{:S(2)}) collective-permute-start(f32[72,256]{1,0:T(8,128)S(1)} %get-tuple-element.14), channel_id=1, source_target_pairs={{0,16},{16,32},{32,48},{48,64},{64,80},{80,96},{96,112},{112,128},... | collective-permute-start | bytes 221192 | tf_op jit(solution)/shard_map/ppermute | solution.py:229
  20.1 6.6 %copy-start.3 = (f32[32,256]{1,0:T(8,128)S(1)}, f32[32,256]{1,0:T(8,128)}, u32[]{:S(2)}) copy-start(f32[32,256]{1,0:T(8,128)} %k_ref.5) | copy-start | bytes 98308
  21.4 9.4 %collective-permute-start.4 = (f32[64,128]{1,0:T(8,128)S(1)}, f32[64,128]{1,0:T(8,128)S(1)}, u32[]{:S(2)}, u32[]{:S(2)}) collective-permute-start(f32[64,128]{1,0:T(8,128)S(1)} %get-tuple-element.19), channel_id=1, source_target_pairs={{1,0},{2,1},{3,2},{4,3},{5,4},{6,5},{7,6},{8,7},{9,8},{10,9},{11,1... | collective-permute-start | bytes 98312 | tf_op jit(solution)/shard_map/ppermute | solution.py:229
  22.6 8.1 %collective-permute-start.5 = (f32[64,128]{1,0:T(8,128)S(1)}, f32[64,128]{1,0:T(8,128)S(1)}, u32[]{:S(2)}, u32[]{:S(2)}) collective-permute-start(f32[64,128]{1,0:T(8,128)S(1)} %get-tuple-element.20), channel_id=1, source_target_pairs={{0,1},{1,2},{2,3},{3,4},{4,5},{5,6},{6,7},{7,8},{8,9},{9,10},{10,1... | collective-permute-start | bytes 98312 | tf_op jit(solution)/shard_map/ppermute | solution.py:229
  26.7 4.1 %copy-start.4 = (f32[32,128]{1,0:T(8,128)S(1)}, f32[32,128]{1,0:T(8,128)}, u32[]{:S(2)}) copy-start(f32[32,128]{1,0:T(8,128)} %fx_ref.1) | copy-start | bytes 49156
  26.7 4.1 %copy-start.5 = (f32[32,16]{0,1:T(8,128)S(1)}, f32[32,16]{0,1:T(8,128)}, u32[]{:S(2)}) copy-start(f32[32,16]{0,1:T(8,128)} %param.11) | copy-start | bytes 6148
  30.8 0.7 copy-start.6
  34.2 29.1 %all-to-all-start = ((f32[32,48,128]{2,1,0:T(8,128)}), f32[32,48,128]{2,1,0:T(8,128)S(1)}, u32[]{:S(2)}, u32[]{:S(2)}) async-start(f32[32,48,128]{2,1,0:T(8,128)} %bitcast.4), calls=%async_computation | async-start | bytes 1572864 | tf_op jit(solution)/shard_map/all_to_all | solution.py:247
  64.0 5.1 %collective-permute-start.6 = (f32[128,128]{1,0:T(8,128)S(1)}, f32[128,128]{1,0:T(8,128)S(1)}, u32[]{:S(2)}, u32[]{:S(2)}) collective-permute-start(f32[128,128]{1,0:T(8,128)S(1)} %convolution_bitcast_fusion.1), channel_id=1, source_target_pairs={{0,16},{16,0},{32,48},{48,32},{64,80},{80,64},{96,112},{112,96},{1... | collective-permute-start | bytes 196616 | tf_op jit(solution)/shard_map/ppermute | solution.py:254

commit v14 on v9

--- a/solution.py
+++ b/solution.py
@@ -5,7 +5,7 @@
 from jax.experimental.pallas import tpu as pltpu
 from jax.sharding import PartitionSpec as P
 
-exact_mode = lax.Precision.HIGHEST
+exact_mode = lax.Precision.HIGH
 f32, bf16 = jnp.float32, jnp.bfloat16
 NS, NX, NV, NH, NZ, NQ = 32, 32, 256, 128, 32, 16
 
@@ -14,7 +14,7 @@
     return lax.broadcasted_iota(jnp.int32, (rows, 128), 1)
 
 
-def pack_kernel(c0_ref, c1_ref, k_ref, xl_ref, xh_ref, yl_ref, yh_ref):
+def pack_kernel(k_ref, c0_ref, c1_ref, xl_ref, xh_ref, yl_ref, yh_ref):
     low = lanes(NS // 2) < 64
 
     def row(x):
@@ -47,11 +47,11 @@
         pack_kernel,
         grid=(1,),
         out_shape=[jax.ShapeDtypeStruct(s, f32) for s in shapes],
-        in_specs=halves(c2d) + [whole_block(k.shape)],
+        in_specs=[whole_block(k.shape)] + halves(c2d),
         out_specs=[whole_block(s) for s in shapes],
         compiler_params=pltpu.CompilerParams(vmem_limit_bytes=8 * 2**20),
         name="pack_faces",
-    )(c2d, c2d, k)
+    )(k, c2d, c2d)
 
 
 def corner_kernel(xl_ref, xh_ref, lo_ref, hi_ref):

time: 126 us -> 126 us (level)
  no operation moved by 1% of the time
where the time goes in v14:
time: 126 us; the launch traced here: 125 us
  blocking collectives  90 us (71%)
  starting transfers between devices  21.8 us (17%)
  Pallas kernels  6.43 us (5%)
  local copies, waits for them, and re-layouts  4.09 us (3%)
  waiting for transfers between devices  1.3 us (1%)
    all_to_all x1, blocking collectives, body(): planes = lax.all_to_all(planes, 'tx', 0, 0, tiled=True)  34.1 us
    all_to_all x1, blocking collectives, body(): core = lax.all_to_all(plane, ('tx', 'ty'), 0, 0, tiled=True)  29.4 us
    all_to_all x1, blocking collectives, body(): came = lax.all_to_all(sent, 'ty', 0, 0, tiled=True)  26.5 us
    ppermute x6, starting transfers between devices, shift_to(): lax.ppermute(v, axis, [(i, i + step) for i in range(count) if 0 <= i + st...  21.8 us
    pallas_call x1, Pallas kernels, advance(): pl.pallas_call(advance_kernel, grid=(1,), out_shape=[jax.ShapeDtypeStruct...  4.05 us
    unnamed x17, local copies, waits for them, and re-layouts  2.85 us
  transfers between devices with their start and end apart: 6, of which 1 were waited for; matrix products, arithmetic and copies ran while one was open for 0% of the time, Pallas kernels for 3%

profile of v14, /device:TPU:1, one launch (start us, length us, event | category | flops | bytes accessed | tf_op | source)
XLA Modules:
  0.0 125.5 jit_solution(6151475903168097794)
XLA Ops:
  0.6 1.2 copy-done
  1.9 0.8 copy-done.2
  2.6 0.7 pack_faces.1
  3.4 1.3 %collective-permute-start.2 = (f32[544,128]{1,0:T(8,128)S(1)}, f32[544,128]{1,0:T(8,128)S(1)}, u32[]{:S(2)}, u32[]{:S(2)}) collective-permute-start(f32[544,128]{1,0:T(8,128)S(1)} %get-tuple-element.14), channel_id=1, source_target_pairs={{1,0},{2,1},{3,2},{4,3},{5,4},{6,5},{7,6},{8,7},{9,8},{10,9},{11,1... | collective-permute-start | bytes 835592 | tf_op jit(solution)/shard_map/ppermute | solution.py:226
  4.7 4.6 %collective-permute-start.3 = (f32[544,128]{1,0:T(8,128)S(1)}, f32[544,128]{1,0:T(8,128)S(1)}, u32[]{:S(2)}, u32[]{:S(2)}) collective-permute-start(f32[544,128]{1,0:T(8,128)S(1)} %get-tuple-element.15), channel_id=1, source_target_pairs={{0,1},{1,2},{2,3},{3,4},{4,5},{5,6},{6,7},{7,8},{8,9},{9,10},{10,1... | collective-permute-start | bytes 835592 | tf_op jit(solution)/shard_map/ppermute | solution.py:226
  9.3 8.8 %collective-permute-start = (f32[72,256]{1,0:T(8,128)S(1)}, f32[72,256]{1,0:T(8,128)S(1)}, u32[]{:S(2)}, u32[]{:S(2)}) collective-permute-start(f32[72,256]{1,0:T(8,128)S(1)} %get-tuple-element.12), channel_id=1, source_target_pairs={{16,0},{32,16},{48,32},{64,48},{80,64},{96,80},{112,96},{128,112},... | collective-permute-start | bytes 221192 | tf_op jit(solution)/shard_map/ppermute | solution.py:226
  18.0 1.9 %collective-permute-start.1 = (f32[72,256]{1,0:T(8,128)S(1)}, f32[72,256]{1,0:T(8,128)S(1)}, u32[]{:S(2)}, u32[]{:S(2)}) collective-permute-start(f32[72,256]{1,0:T(8,128)S(1)} %get-tuple-element.13), channel_id=1, source_target_pairs={{0,16},{16,32},{32,48},{48,64},{64,80},{80,96},{96,112},{112,128},... | collective-permute-start | bytes 221192 | tf_op jit(solution)/shard_map/ppermute | solution.py:226
  20.1 1.3 %collective-permute-done.1.xh_ref.kxh_ref = f32[72,256]{1,0:T(8,128)S(1)} collective-permute-done((f32[72,256]{1,0:T(8,128)S(1)}, f32[72,256]{1,0:T(8,128)S(1)}, u32[]{:S(2)}, u32[]{:S(2)}) %collective-permute-start.1) | collective-permute-done | bytes 73760 | tf_op jit(solution)/shard_map/ppermute | solution.py:226
  21.4 1.3 %collective-permute-start.4 = (f32[64,128]{1,0:T(8,128)S(1)}, f32[64,128]{1,0:T(8,128)S(1)}, u32[]{:S(2)}, u32[]{:S(2)}) collective-permute-start(f32[64,128]{1,0:T(8,128)S(1)} %get-tuple-element.18), channel_id=1, source_target_pairs={{1,0},{2,1},{3,2},{4,3},{5,4},{6,5},{7,6},{8,7},{9,8},{10,9},{11,1... | collective-permute-start | bytes 98312 | tf_op jit(solution)/shard_map/ppermute | solution.py:226
  22.6 4.0 %collective-permute-start.5 = (f32[64,128]{1,0:T(8,128)S(1)}, f32[64,128]{1,0:T(8,128)S(1)}, u32[]{:S(2)}, u32[]{:S(2)}) collective-permute-start(f32[64,128]{1,0:T(8,128)S(1)} %get-tuple-element.19), channel_id=1, source_target_pairs={{0,1},{1,2},{2,3},{3,4},{4,5},{5,6},{6,7},{7,8},{8,9},{9,10},{10,1... | collective-permute-start | bytes 98312 | tf_op jit(solution)/shard_map/ppermute | solution.py:226
  26.7 4.0 %advance_twice.1 = (f32[1024,128]{1,0:T(8,128)S(1)}, f32[1024,128]{1,0:T(8,128)S(1)}) custom-call(f32[1024,256]{1,0:T(8,128)S(1)} %bitcast.39, f32[1024,256]{1,0:T(8,128)S(1)} %bitcast.40, f32[32,256]{1,0:T(8,128)S(1)} %copy-done.3, f32[32,1]{1,0:T(8,128)S(1)} %copy.19.rate_ref, f32[72,256]{1,0:T(8,128)S(1)} %collective-permute-done.xl_ref.kxl_ref, ...), custom_call_target="tpu_custom_call" | custom-call | flops 10000000000 | bytes 4194304 | tf_op jit(solution)/shard_map/advance_twice/pallas_call | solution.py:141
  30.8 1.6 %reduce_species.1 = (f32[1024,256]{1,0:T(8,128)}, f32[2048,128]{1,0:T(8,128)S(1)}) custom-call(f32[1024,128]{1,0:T(8,128)S(1)} %get-tuple-element.16.a0_ref, f32[1024,128]{1,0:T(8,128)S(1)} %get-tuple-element.17.a1_ref, f32[32,256]{1,0:T(8,128)S(1)} %copy-done.3, f32[32,1]{1,0:T(8,128)S(1)} %copy.19.rate_ref, ...), custom_call_target="tpu_custom_call" | custom-call | tf_op jit(solution)/shard_map/reduce_species/pallas_call | solution.py:209
  32.5 34.1 %all_to_all.15 = f32[32,64,128]{2,1,0:T(8,128)S(1)} all-to-all(f32[32,64,128]{2,1,0:T(8,128)S(1)} %bitcast.41), channel_id=1, replica_groups=mesh['tx'=32,'ty'=16] {'tx'}, dimensions={0} | all-to-all | bytes 2097152 | tf_op jit(solution)/shard_map/all_to_all | solution.py:244
  66.5 0.6 fusion
  67.2 26.5 %all_to_all.16 = f32[16,16,128]{2,1,0:T(8,128)S(1)} all-to-all(f32[16,16,128]{2,1,0:T(8,128)S(1)} %pad_maximum_fusion), channel_id=1, replica_groups=mesh['tx'=32,'ty'=16] {'ty'}, dimensions={0} | all-to-all | bytes 262144 | tf_op jit(solution)/shard_map/all_to_all | solution.py:250
  93.9 0.1 copy.23
  94.0 0.3 convolution_bitcast_fusion
  94.3 0.2 copy.26
  94.5 0.3 reshape.41
  94.8 0.1 copy.27
  94.9 29.4 %all_to_all.17 = f32[512,1,32]{2,1,0:T(1,128)S(1)} all-to-all(f32[512,1,32]{2,1,0:T(1,128)S(1)} %copy.27), channel_id=1, replica_groups=mesh['tx'=32,'ty'=16] {'tx','ty'}, dimensions={0} | all-to-all | bytes 131072 | tf_op jit(solution)/shard_map/all_to_all | solution.py:257
  124.3 0.1 copy.28
  124.4 0.2 reshape.42
  124.7 0.8 copy.29
  (26 shorter events, 0.3 us)
Async XLA Ops:
  0.6 1.2 copy-start
  1.9 0.8 copy-start.2
  2.6 24.0 %copy-start.1 = (f32[32,32,256]{2,1,0:T(8,128)S(1)}, f32[32,32,256]{2,1,0:T(8,128)}, u32[]{:S(2)}) copy-start(f32[32,32,256]{2,1,0:T(8,128)} %param.6) | copy-start | bytes 3145732
  3.4 23.3 %collective-permute-start.2 = (f32[544,128]{1,0:T(8,128)S(1)}, f32[544,128]{1,0:T(8,128)S(1)}, u32[]{:S(2)}, u32[]{:S(2)}) collective-permute-start(f32[544,128]{1,0:T(8,128)S(1)} %get-tuple-element.14), channel_id=1, source_target_pairs={{1,0},{2,1},{3,2},{4,3},{5,4},{6,5},{7,6},{8,7},{9,8},{10,9},{11,1... | collective-permute-start | bytes 835592 | tf_op jit(solution)/shard_map/ppermute | solution.py:226
  4.7 22.0 %collective-permute-start.3 = (f32[544,128]{1,0:T(8,128)S(1)}, f32[544,128]{1,0:T(8,128)S(1)}, u32[]{:S(2)}, u32[]{:S(2)}) collective-permute-start(f32[544,128]{1,0:T(8,128)S(1)} %get-tuple-element.15), channel_id=1, source_target_pairs={{0,1},{1,2},{2,3},{3,4},{4,5},{5,6},{6,7},{7,8},{8,9},{9,10},{10,1... | collective-permute-start | bytes 835592 | tf_op jit(solution)/shard_map/ppermute | solution.py:226
  9.3 10.8 %collective-permute-start = (f32[72,256]{1,0:T(8,128)S(1)}, f32[72,256]{1,0:T(8,128)S(1)}, u32[]{:S(2)}, u32[]{:S(2)}) collective-permute-start(f32[72,256]{1,0:T(8,128)S(1)} %get-tuple-element.12), channel_id=1, source_target_pairs={{16,0},{32,16},{48,32},{64,48},{80,64},{96,80},{112,96},{128,112},... | collective-permute-start | bytes 221192 | tf_op jit(solution)/shard_map/ppermute | solution.py:226
  18.0 1.9 %copy-start.7 = (f32[32]{0:T(128)S(1)}, f32[32]{0:T(128)}, u32[]{:S(2)}) copy-start(f32[32]{0:T(128)} %param.8) | copy-start | bytes 388
  18.0 3.3 %collective-permute-start.1 = (f32[72,256]{1,0:T(8,128)S(1)}, f32[72,256]{1,0:T(8,128)S(1)}, u32[]{:S(2)}, u32[]{:S(2)}) collective-permute-start(f32[72,256]{1,0:T(8,128)S(1)} %get-tuple-element.13), channel_id=1, source_target_pairs={{0,16},{16,32},{32,48},{48,64},{64,80},{80,96},{96,112},{112,128},... | collective-permute-start | bytes 221192 | tf_op jit(solution)/shard_map/ppermute | solution.py:226
  20.1 6.6 %copy-start.3 = (f32[32,256]{1,0:T(8,128)S(1)}, f32[32,256]{1,0:T(8,128)}, u32[]{:S(2)}) copy-start(f32[32,256]{1,0:T(8,128)} %k_ref.5) | copy-start | bytes 98308
  21.4 9.4 %collective-permute-start.4 = (f32[64,128]{1,0:T(8,128)S(1)}, f32[64,128]{1,0:T(8,128)S(1)}, u32[]{:S(2)}, u32[]{:S(2)}) collective-permute-start(f32[64,128]{1,0:T(8,128)S(1)} %get-tuple-element.18), channel_id=1, source_target_pairs={{1,0},{2,1},{3,2},{4,3},{5,4},{6,5},{7,6},{8,7},{9,8},{10,9},{11,1... | collective-permute-start | bytes 98312 | tf_op jit(solution)/shard_map/ppermute | solution.py:226
  22.6 8.1 %collective-permute-start.5 = (f32[64,128]{1,0:T(8,128)S(1)}, f32[64,128]{1,0:T(8,128)S(1)}, u32[]{:S(2)}, u32[]{:S(2)}) collective-permute-start(f32[64,128]{1,0:T(8,128)S(1)} %get-tuple-element.19), channel_id=1, source_target_pairs={{0,1},{1,2},{2,3},{3,4},{4,5},{5,6},{6,7},{7,8},{8,9},{9,10},{10,1... | collective-permute-start | bytes 98312 | tf_op jit(solution)/shard_map/ppermute | solution.py:226
  26.7 4.1 %copy-start.4 = (f32[32,128]{1,0:T(8,128)S(1)}, f32[32,128]{1,0:T(8,128)}, u32[]{:S(2)}) copy-start(f32[32,128]{1,0:T(8,128)} %fx_ref.1) | copy-start | bytes 49156
  26.7 4.1 %copy-start.5 = (f32[32,16]{0,1:T(8,128)S(1)}, f32[32,16]{0,1:T(8,128)}, u32[]{:S(2)}) copy-start(f32[32,16]{0,1:T(8,128)} %param.11) | copy-start | bytes 6148
  66.5 0.7 copy-start.6

commit v15 on v9

--- a/solution.py
+++ b/solution.py
@@ -177,14 +177,14 @@
     lane_q = lanes(NQ)
     low_q, even_q = lane_q < 64, (lane_q & 32) == 0
     fs_hi, fs_lo = split_2(fs_ref[...])
-    weights = jnp.concatenate([fs_hi, fs_hi, fs_lo, fs_lo], axis=1)
+    weights = jnp.concatenate([fs_hi, fs_hi, fs_lo], axis=1)
 
     def four_rows(group, carry):
         rows = []
         for g in range(4):
             cut = pl.ds(group * 4 + g, NS, stride=NX)
             hi, lo = split_2(jnp.concatenate([left[cut, :], right[cut, :]], axis=1))
-            stacked = jnp.concatenate([hi, lo, hi, lo], axis=0)
+            stacked = jnp.concatenate([hi, lo, hi], axis=0)
             rows.append(jnp.dot(weights, stacked, preferred_element_type=f32))
         swapped = []
         for t in range(2):

time: 126 us -> 127 us (level)
  no operation moved by 1% of the time
where the time goes in v15:
time: 127 us
  blocking collectives  90 us (71%)
  starting transfers between devices  21.8 us (17%)
  Pallas kernels  6.95 us (5%)
  local copies, waits for them, and re-layouts  4.04 us (3%)
  matrix products  1.49 us (1%)
  waiting for transfers between devices  1.3 us (1%)
    all_to_all x1, blocking collectives, body(): planes = lax.all_to_all(planes, 'tx', 0, 0, tiled=True)  34.1 us
    all_to_all x1, blocking collectives, body(): core = lax.all_to_all(plane, ('tx', 'ty'), 0, 0, tiled=True)  29.4 us
    all_to_all x1, blocking collectives, body(): came = lax.all_to_all(sent, 'ty', 0, 0, tiled=True)  26.5 us
    ppermute x6, starting transfers between devices, shift_to(): lax.ppermute(v, axis, [(i, i + step) for i in range(count) if 0 <= i + st...  21.8 us
    pallas_call x1, Pallas kernels, advance(): pl.pallas_call(advance_kernel, grid=(1,), out_shape=[jax.ShapeDtypeStruct...  4.05 us
    unnamed x17, local copies, waits for them, and re-layouts  2.81 us
  transfers between devices with their start and end apart: 6, of which 1 were waited for; matrix products, arithmetic and copies ran while one was open for 0% of the time, Pallas kernels for 3%

profile of v15, /device:TPU:1, one launch (start us, length us, event | category | flops | bytes accessed | tf_op | source)
XLA Modules:
  0.0 126.5 jit_solution(1438267708121116661)
XLA Ops:
  0.6 1.2 copy-done
  1.9 0.8 copy-done.2
  2.6 0.7 pack_faces.1
  3.4 1.3 %collective-permute-start.2 = (f32[544,128]{1,0:T(8,128)S(1)}, f32[544,128]{1,0:T(8,128)S(1)}, u32[]{:S(2)}, u32[]{:S(2)}) collective-permute-start(f32[544,128]{1,0:T(8,128)S(1)} %get-tuple-element.14), channel_id=1, source_target_pairs={{1,0},{2,1},{3,2},{4,3},{5,4},{6,5},{7,6},{8,7},{9,8},{10,9},{11,1... | collective-permute-start | bytes 835592 | tf_op jit(solution)/shard_map/ppermute | solution.py:226
  4.7 4.6 %collective-permute-start.3 = (f32[544,128]{1,0:T(8,128)S(1)}, f32[544,128]{1,0:T(8,128)S(1)}, u32[]{:S(2)}, u32[]{:S(2)}) collective-permute-start(f32[544,128]{1,0:T(8,128)S(1)} %get-tuple-element.15), channel_id=1, source_target_pairs={{0,1},{1,2},{2,3},{3,4},{4,5},{5,6},{6,7},{7,8},{8,9},{9,10},{10,1... | collective-permute-start | bytes 835592 | tf_op jit(solution)/shard_map/ppermute | solution.py:226
  9.3 8.8 %collective-permute-start = (f32[72,256]{1,0:T(8,128)S(1)}, f32[72,256]{1,0:T(8,128)S(1)}, u32[]{:S(2)}, u32[]{:S(2)}) collective-permute-start(f32[72,256]{1,0:T(8,128)S(1)} %get-tuple-element.12), channel_id=1, source_target_pairs={{16,0},{32,16},{48,32},{64,48},{80,64},{96,80},{112,96},{128,112},... | collective-permute-start | bytes 221192 | tf_op jit(solution)/shard_map/ppermute | solution.py:226
  18.0 1.9 %collective-permute-start.1 = (f32[72,256]{1,0:T(8,128)S(1)}, f32[72,256]{1,0:T(8,128)S(1)}, u32[]{:S(2)}, u32[]{:S(2)}) collective-permute-start(f32[72,256]{1,0:T(8,128)S(1)} %get-tuple-element.13), channel_id=1, source_target_pairs={{0,16},{16,32},{32,48},{48,64},{64,80},{80,96},{96,112},{112,128},... | collective-permute-start | bytes 221192 | tf_op jit(solution)/shard_map/ppermute | solution.py:226
  20.1 1.3 %collective-permute-done.1.xh_ref.kxh_ref = f32[72,256]{1,0:T(8,128)S(1)} collective-permute-done((f32[72,256]{1,0:T(8,128)S(1)}, f32[72,256]{1,0:T(8,128)S(1)}, u32[]{:S(2)}, u32[]{:S(2)}) %collective-permute-start.1) | collective-permute-done | bytes 73760 | tf_op jit(solution)/shard_map/ppermute | solution.py:226
  21.4 1.3 %collective-permute-start.4 = (f32[64,128]{1,0:T(8,128)S(1)}, f32[64,128]{1,0:T(8,128)S(1)}, u32[]{:S(2)}, u32[]{:S(2)}) collective-permute-start(f32[64,128]{1,0:T(8,128)S(1)} %get-tuple-element.18), channel_id=1, source_target_pairs={{1,0},{2,1},{3,2},{4,3},{5,4},{6,5},{7,6},{8,7},{9,8},{10,9},{11,1... | collective-permute-start | bytes 98312 | tf_op jit(solution)/shard_map/ppermute | solution.py:226
  22.6 4.0 %collective-permute-start.5 = (f32[64,128]{1,0:T(8,128)S(1)}, f32[64,128]{1,0:T(8,128)S(1)}, u32[]{:S(2)}, u32[]{:S(2)}) collective-permute-start(f32[64,128]{1,0:T(8,128)S(1)} %get-tuple-element.19), channel_id=1, source_target_pairs={{0,1},{1,2},{2,3},{3,4},{4,5},{5,6},{6,7},{7,8},{8,9},{9,10},{10,1... | collective-permute-start | bytes 98312 | tf_op jit(solution)/shard_map/ppermute | solution.py:226
  26.7 4.0 %advance_twice.1 = (f32[1024,128]{1,0:T(8,128)S(1)}, f32[1024,128]{1,0:T(8,128)S(1)}) custom-call(f32[1024,256]{1,0:T(8,128)S(1)} %bitcast.39, f32[1024,256]{1,0:T(8,128)S(1)} %bitcast.40, f32[32,256]{1,0:T(8,128)S(1)} %copy-done.3, f32[32,1]{1,0:T(8,128)S(1)} %copy.19.rate_ref, f32[72,256]{1,0:T(8,128)S(1)} %collective-permute-done.xl_ref.kxl_ref, ...), custom_call_target="tpu_custom_call" | custom-call | flops 10000000000 | bytes 4194304 | tf_op jit(solution)/shard_map/advance_twice/pallas_call | solution.py:141
  30.8 2.2 %reduce_species.1 = (f32[1024,256]{1,0:T(8,128)}, f32[2048,128]{1,0:T(8,128)S(1)}) custom-call(f32[1024,128]{1,0:T(8,128)S(1)} %get-tuple-element.16.a0_ref, f32[1024,128]{1,0:T(8,128)S(1)} %get-tuple-element.17.a1_ref, f32[32,256]{1,0:T(8,128)S(1)} %copy-done.3, f32[32,1]{1,0:T(8,128)S(1)} %copy.19.rate_ref, ...), custom_call_target="tpu_custom_call" | custom-call | tf_op jit(solution)/shard_map/reduce_species/pallas_call | solution.py:209
  33.0 34.1 %all_to_all.15 = f32[32,64,128]{2,1,0:T(8,128)S(1)} all-to-all(f32[32,64,128]{2,1,0:T(8,128)S(1)} %bitcast.41), channel_id=1, replica_groups=mesh['tx'=32,'ty'=16] {'tx'}, dimensions={0} | all-to-all | bytes 2097152 | tf_op jit(solution)/shard_map/all_to_all | solution.py:244
  67.0 1.0 fusion
  68.1 26.5 %all_to_all.16 = f32[16,16,128]{2,1,0:T(8,128)S(1)} all-to-all(f32[16,16,128]{2,1,0:T(8,128)S(1)} %pad_maximum_fusion), channel_id=1, replica_groups=mesh['tx'=32,'ty'=16] {'ty'}, dimensions={0} | all-to-all | bytes 262144 | tf_op jit(solution)/shard_map/all_to_all | solution.py:250
  94.8 0.1 copy.23
  94.9 0.5 convolution_bitcast_fusion
  95.3 0.2 copy.26
  95.5 0.3 reshape.41
  95.8 0.1 copy.27
  96.0 29.4 %all_to_all.17 = f32[512,1,32]{2,1,0:T(1,128)S(1)} all-to-all(f32[512,1,32]{2,1,0:T(1,128)S(1)} %copy.27), channel_id=1, replica_groups=mesh['tx'=32,'ty'=16] {'tx','ty'}, dimensions={0} | all-to-all | bytes 131072 | tf_op jit(solution)/shard_map/all_to_all | solution.py:257
  125.4 0.1 copy.28
  125.5 0.2 reshape.42
  125.7 0.8 copy.29
  (26 shorter events, 0.3 us)
Async XLA Ops:
  0.6 1.2 copy-start
  1.9 0.8 copy-start.2
  2.6 24.0 %copy-start.1 = (f32[32,32,256]{2,1,0:T(8,128)S(1)}, f32[32,32,256]{2,1,0:T(8,128)}, u32[]{:S(2)}) copy-start(f32[32,32,256]{2,1,0:T(8,128)} %param.6) | copy-start | bytes 3145732
  3.4 23.3 %collective-permute-start.2 = (f32[544,128]{1,0:T(8,128)S(1)}, f32[544,128]{1,0:T(8,128)S(1)}, u32[]{:S(2)}, u32[]{:S(2)}) collective-permute-start(f32[544,128]{1,0:T(8,128)S(1)} %get-tuple-element.14), channel_id=1, source_target_pairs={{1,0},{2,1},{3,2},{4,3},{5,4},{6,5},{7,6},{8,7},{9,8},{10,9},{11,1... | collective-permute-start | bytes 835592 | tf_op jit(solution)/shard_map/ppermute | solution.py:226
  4.7 22.0 %collective-permute-start.3 = (f32[544,128]{1,0:T(8,128)S(1)}, f32[544,128]{1,0:T(8,128)S(1)}, u32[]{:S(2)}, u32[]{:S(2)}) collective-permute-start(f32[544,128]{1,0:T(8,128)S(1)} %get-tuple-element.15), channel_id=1, source_target_pairs={{0,1},{1,2},{2,3},{3,4},{4,5},{5,6},{6,7},{7,8},{8,9},{9,10},{10,1... | collective-permute-start | bytes 835592 | tf_op jit(solution)/shard_map/ppermute | solution.py:226
  9.3 10.8 %collective-permute-start = (f32[72,256]{1,0:T(8,128)S(1)}, f32[72,256]{1,0:T(8,128)S(1)}, u32[]{:S(2)}, u32[]{:S(2)}) collective-permute-start(f32[72,256]{1,0:T(8,128)S(1)} %get-tuple-element.12), channel_id=1, source_target_pairs={{16,0},{32,16},{48,32},{64,48},{80,64},{96,80},{112,96},{128,112},... | collective-permute-start | bytes 221192 | tf_op jit(solution)/shard_map/ppermute | solution.py:226
  18.0 1.9 %copy-start.7 = (f32[32]{0:T(128)S(1)}, f32[32]{0:T(128)}, u32[]{:S(2)}) copy-start(f32[32]{0:T(128)} %param.8) | copy-start | bytes 388
  18.0 3.3 %collective-permute-start.1 = (f32[72,256]{1,0:T(8,128)S(1)}, f32[72,256]{1,0:T(8,128)S(1)}, u32[]{:S(2)}, u32[]{:S(2)}) collective-permute-start(f32[72,256]{1,0:T(8,128)S(1)} %get-tuple-element.13), channel_id=1, source_target_pairs={{0,16},{16,32},{32,48},{48,64},{64,80},{80,96},{96,112},{112,128},... | collective-permute-start | bytes 221192 | tf_op jit(solution)/shard_map/ppermute | solution.py:226
  20.1 6.6 %copy-start.3 = (f32[32,256]{1,0:T(8,128)S(1)}, f32[32,256]{1,0:T(8,128)}, u32[]{:S(2)}) copy-start(f32[32,256]{1,0:T(8,128)} %k_ref.5) | copy-start | bytes 98308
  21.4 9.4 %collective-permute-start.4 = (f32[64,128]{1,0:T(8,128)S(1)}, f32[64,128]{1,0:T(8,128)S(1)}, u32[]{:S(2)}, u32[]{:S(2)}) collective-permute-start(f32[64,128]{1,0:T(8,128)S(1)} %get-tuple-element.18), channel_id=1, source_target_pairs={{1,0},{2,1},{3,2},{4,3},{5,4},{6,5},{7,6},{8,7},{9,8},{10,9},{11,1... | collective-permute-start | bytes 98312 | tf_op jit(solution)/shard_map/ppermute | solution.py:226
  22.6 8.1 %collective-permute-start.5 = (f32[64,128]{1,0:T(8,128)S(1)}, f32[64,128]{1,0:T(8,128)S(1)}, u32[]{:S(2)}, u32[]{:S(2)}) collective-permute-start(f32[64,128]{1,0:T(8,128)S(1)} %get-tuple-element.19), channel_id=1, source_target_pairs={{0,1},{1,2},{2,3},{3,4},{4,5},{5,6},{6,7},{7,8},{8,9},{9,10},{10,1... | collective-permute-start | bytes 98312 | tf_op jit(solution)/shard_map/ppermute | solution.py:226
  26.7 4.1 %copy-start.4 = (f32[32,128]{1,0:T(8,128)S(1)}, f32[32,128]{1,0:T(8,128)}, u32[]{:S(2)}) copy-start(f32[32,128]{1,0:T(8,128)} %fx_ref.1) | copy-start | bytes 49156
  26.7 4.1 %copy-start.5 = (f32[32,16]{0,1:T(8,128)S(1)}, f32[32,16]{0,1:T(8,128)}, u32[]{:S(2)}) copy-start(f32[32,16]{0,1:T(8,128)} %param.11) | copy-start | bytes 6148
  67.0 1.1 copy-start.6
